TPU v7x, 32 devices: a whole 2x2x4 slice. The times are simulated.
32 devices in a mesh: blk: 8 (over y, x, core), expert: 4 (over z).
Axes of the slice: x: 2, y: 2, z: 4, core: 2. Of those that a mesh axis runs over, the one named last changes fastest.
Arguments:
- queries: bfloat16 [16, 72, 1024], P('expert', None, 'blk'), may hold values from -6 to 6
- keys: bfloat16 [16, 72, 1024], P('expert', None, 'blk'), may hold values from -6 to 6
- values: bfloat16 [16, 72, 1024], P('expert', None, 'blk'), may hold values from -24 to 24
- image_ids: int32 [256], P('blk'), may hold values from 0 to 2, as said below
- placement: int32 [256, 1], P('blk'), may hold values from 0 to 7; in each aligned block of 32 rows (0 to 31, 32 to 63, ...) at most 16 rows name the same one
- merge_gain: float32 [16, 288], P('expert'), may hold values from 0.1 to 1.9
- merge_weight: bfloat16 [16, 288, 2048], P('expert'), may hold values from -0.09375 to 0.09375
- text: bfloat16 [1024, 2048], P('blk'), may hold values from -6 to 6
- norm_gain: float32 [2048], replicated, may hold values from 0.1 to 1.9
- w_gate: bfloat16 [8, 3072, 2048], P('blk', 'expert'), may hold values from -0.125 to 0.125
- w_up: bfloat16 [8, 3072, 2048], P('blk', 'expert'), may hold values from -0.125 to 0.125
- w_down: bfloat16 [8, 3072, 2048], P('blk', 'expert'), may hold values from -0.15625 to 0.15625
- routes: int32 [1024, 8], P('blk'), may hold values from 0 to 127, all different within a row; in each aligned block of 128 rows (0 to 127, 128 to 255, ...) at most 10 rows name the same one
- route_gates: float32 [1024, 8], P('blk'), may hold values from 0.2 to 1
- cotangent: bfloat16 [1024, 2048], P('blk'), may hold values from -6 to 6
Outputs:
- llm_out: bfloat16 [1024, 2048], P('blk')
- attn_grad: float32 [16, 72, 1024], P('expert', None, 'blk')
Inputs may be any that keep to these rules, and one draw needn't show every extreme that they name: `image_ids`: three images in order: ids never fall along the sequence; image 0 holds from 16 to 31 merged rows and image 2 from 17 to 32. `placement`: among the 32 rows of one encoder index no shard is named more than 16 times. `routes`: each token names 8 different experts; among the 128 tokens of one shard no expert is named more than 10 times.
All inputs are finite; a program needn't handle non-finite values.
Results may differ from a plain program's by a relative error of at most 0.03.
Values may be sent and summed in bfloat16 or wider, within the bound.
No kernel may reach another device: no remote copies, remote signals or barrier semaphores. Data moves between devices by JAX's collectives and lax.ppermute only.
A program may use at most 64 MiB of HBM per device.

v0:
```python
import functools

import jax
import jax.numpy as jnp
from jax import lax
from jax.experimental import pallas as pl
from jax.experimental.pallas import tpu as pltpu
from jax.sharding import PartitionSpec as P

CAPX = 10
SLOTS = 16
SEND = 24
EPS = 1e-06
VMEM_BYTES = 16 * 1024 * 1024
PACK_BYTES = 60 * 1024 * 1024
F32 = jnp.float32
BF16 = jnp.bfloat16


def iota(shape, dim):
    return lax.broadcasted_iota(jnp.int32, shape, dim)


def dot(a, b):
    return jnp.dot(a.astype(BF16), b.astype(BF16), preferred_element_type=F32)


def dot_nt(a, b):
    return lax.dot_general(a, b, (((1,), (1,)), ((), ())), preferred_element_type=F32)


def dot_tn(a, b):
    return lax.dot_general(a, b, (((0,), (0,)), ((), ())), preferred_element_type=F32)


def three(value):
    first = value.astype(BF16).astype(F32)
    second = (value - first).astype(BF16).astype(F32)
    return first, second, value - first - second


def put_scalars(columns, rows):
    lane = iota((rows, 128), 1)
    out = jnp.zeros((rows, 128), F32)
    place = 0
    for column in columns:
        for piece in three(column):
            out = jnp.where(lane == place, piece, out)
            place += 1
    return out


def get_scalar(block, which):
    lane = iota(block.shape, 1)
    return jnp.sum(jnp.where(lane // 3 == which, block, 0.0), axis=1, keepdims=True)


def bring(far_refs, near_refs, sems):
    copies = [
        pltpu.make_async_copy(far, near, sems.at[i])
        for i, (far, near) in enumerate(zip(far_refs, near_refs))
    ]
    for copy in copies:
        copy.start()
    return copies


def pack_kernel(*refs):
    far_refs, out_ref, near_refs, sems = refs[:5], refs[5], refs[6:11], refs[11]
    for copy in bring(far_refs, near_refs, sems):
        copy.wait()
    out_ref[...] = packed(*near_refs).astype(BF16)


def packed(keys_ref, values_ref, images_ref, placement_ref, routes_ref):
    rows = images_ref.shape[1]
    patches = keys_ref.shape[1]
    repeat = (iota((rows, patches), 0) == iota((rows, patches), 1) // 4).astype(F32)
    keep = (iota((rows, patches), 0) == iota((rows, patches), 1)).astype(F32)
    patch_ids = dot(images_ref[...].astype(F32), repeat)
    dest = dot(placement_ref[...].astype(F32), keep)
    line = iota((8, patches), 0)
    rest = jnp.where(line == 0, patch_ids, jnp.where(line == 1, dest, 0.0))
    parts = [keys_ref[...], values_ref[...], routes_ref[...], rest]
    return jnp.concatenate([part.astype(F32) for part in parts], axis=0)


def route_kernel(routes_ref, gates_ref, comb_ref, pick_ref, factor_ref, *, groups, share):
    blocks = comb_ref.shape[1] // SLOTS
    tokens = routes_ref.shape[1]
    me, expert_index = lax.axis_index("blk"), lax.axis_index("expert")
    member = expert_index // groups
    before = (iota((tokens, tokens), 0) < iota((tokens, tokens), 1)).astype(BF16)
    pair_of = 2 * (iota((blocks, tokens), 0) ^ me) + member
    out_hit = jnp.zeros((blocks, tokens), F32)
    out_gate = jnp.zeros((blocks, tokens), F32)
    for k in range(routes_ref.shape[0]):
        same = pair_of == routes_ref[k : k + 1, :]
        out_hit = out_hit + same.astype(F32)
        out_gate = out_gate + jnp.where(same, gates_ref[k : k + 1, :], 0.0)
    out_rank = dot(out_hit, before)

    def expand(stride):
        count = blocks * stride
        pick = (iota((count, blocks), 0) // stride == iota((count, blocks), 1)).astype(BF16)
        gate = sum(dot(pick, piece) for piece in three(out_gate))
        return dot(pick, out_hit), dot(pick, out_rank).astype(jnp.int32), gate

    hits, ranks, gates = expand(SLOTS)
    live = jnp.where(ranks == iota(hits.shape, 0) % SLOTS, hits, 0.0)
    weight = live * gates
    high = weight.astype(BF16).astype(F32)
    part = tokens // share
    col = iota((tokens, tokens), 1)
    turned = (col // part * 0).astype(jnp.int32)
    for place, k in enumerate(halving_order(share)):
        turned = jnp.where(col // part == place, k, turned)
    turned = (iota((tokens, tokens), 0) == (turned ^ expert_index) * part + col % part)
    turned = turned.astype(F32)
    comb_ref[0] = dot(high, turned).astype(BF16)
    comb_ref[1] = dot(weight - high, turned).astype(BF16)

    hits, ranks, gates = expand(SEND)
    place = iota(hits.shape, 0) % SEND
    input_pick = jnp.where((place < CAPX) & (ranks == place), hits, 0.0)
    back_pick = jnp.where((place >= CAPX) & (place < 2 * CAPX) & (ranks == place - CAPX), hits, 0.0)
    pick_ref[0] = input_pick.astype(BF16)
    pick_ref[1] = back_pick.astype(BF16)
    factor = jnp.sum(back_pick * gates, axis=1, keepdims=True)
    factor_ref[...] = jnp.broadcast_to(factor, factor_ref.shape)


def dispatch_kernel(pick_ref, factor_ref, text_ref, gain_ref, cot_ref, *send_refs):
    text = text_ref[...].astype(F32)
    scale = lax.rsqrt(jnp.mean(text * text, axis=1, keepdims=True) + EPS)
    h_rows = (text * scale * gain_ref[...]).astype(BF16)
    factor = factor_ref[:, :1]
    send = dot(pick_ref[0], h_rows) + factor * dot(pick_ref[1], cot_ref[...])
    send = send.astype(BF16)
    count = 2 * SEND
    for k, ref in enumerate(send_refs):
        ref[...] = send[k * count : (k + 1) * count]


def plan_kernel(
    meta_ref, cot_ref, slots_ref, placed_ref, back_ref, *, blocks, groups, merged_rows, row_share
):
    tokens = cot_ref.shape[0]
    rows = blocks * merged_rows
    me, expert_index = lax.axis_index("blk"), lax.axis_index("expert")
    member = expert_index // groups
    meta = [meta_ref[k * 16 : (k + 1) * 16].astype(F32) for k in range(blocks)]
    mine = (2 * me + member).astype(F32)
    hits = [jnp.sum((part[:8] == mine).astype(F32), axis=0, keepdims=True) for part in meta]
    hit = jnp.concatenate(hits, axis=0)
    dest = jnp.concatenate([part[9:10] for part in meta], axis=0)
    before = (iota((tokens, tokens), 0) < iota((tokens, tokens), 1)).astype(BF16)
    rank = dot(hit, before)

    def row_of(col):
        inner = col % merged_rows
        return ((inner // row_share) ^ expert_index) * row_share + inner % row_share

    def place_of(col):
        return ((col // merged_rows) ^ me) * merged_rows + row_of(col)

    spread = (iota((128, rows), 0) == row_of(iota((128, rows), 1))).astype(F32)
    own_block = iota((blocks, rows), 1) // merged_rows == iota((blocks, rows), 0)
    dest_row = jnp.sum(jnp.where(own_block, dot(dest, spread), 0.0), axis=0, keepdims=True)
    dest_row = dest_row.astype(jnp.int32) ^ me
    dest_hit = (iota((blocks, rows), 0) == dest_row).astype(F32)
    rows_before = place_of(iota((rows, rows), 0)) < place_of(iota((rows, rows), 1))
    earlier = dot(dest_hit, rows_before.astype(F32))
    slot = jnp.sum(dest_hit * earlier, axis=0, keepdims=True).astype(jnp.int32)
    at_token = (iota((tokens, rows), 0) == slot).astype(F32)
    row_hit = jnp.sum(dest_hit * dot(hit, at_token), axis=0, keepdims=True)
    row_rank = jnp.sum(dest_hit * dot(rank, at_token), axis=0, keepdims=True).astype(jnp.int32)
    slot_id = dest_row * SLOTS + row_rank
    slot_count = slots_ref.shape[0]
    chosen = (iota((slot_count, rows), 0) == slot_id) & (row_hit > 0.5)
    slots_ref[...] = chosen.astype(F32).astype(BF16)
    placed = jnp.where(dest_row == 0, at_token, 0.0).astype(BF16)
    placed_ref[...] = placed
    back_rows = blocks * row_share
    source = iota((back_rows, rows), 0)
    wanted = source // row_share * merged_rows + source % row_share
    row_pick = (iota((back_rows, rows), 1) == wanted).astype(F32).astype(BF16)
    back_ref[...] = dot(dot_nt(row_pick, placed), cot_ref[...]).astype(BF16)


def flat_gain(gain_ref):
    return jnp.concatenate([gain_ref[h : h + 1] for h in range(gain_ref.shape[0])], axis=1)


def attend_kernel(*refs, blocks, row_share):
    query_ref, gain_ref = refs[:2]
    near_refs = refs[7 : 6 + blocks]
    merged_ref, meta_ref, left_ref, scalar_ref = refs[6 + blocks :]
    heads, size, patches = query_ref.shape
    rows, features = merged_ref.shape
    depth = heads * size
    near = [packed(*refs[2:7])] + [ref[...].astype(F32) for ref in near_refs]
    meta_ref[...] = jnp.concatenate([part[2 * depth :] for part in near], axis=0).astype(BF16)
    key_ids = jnp.concatenate([part[2 * depth + 8 : 2 * depth + 9] for part in near], axis=1)
    eye = iota((patches, patches), 0) == iota((patches, patches), 1)
    own_ids = jnp.sum(jnp.where(eye, key_ids[:, :patches], 0.0), axis=1, keepdims=True)
    same = own_ids == key_ids
    spread = jnp.zeros((patches, features), F32)
    place_row, place_col = iota((size, features), 0), iota((size, features), 1)
    for head in range(heads):
        first = head * size
        keys = jnp.concatenate([part[first : first + size] for part in near], axis=1)
        first = depth + head * size
        values = jnp.concatenate([part[first : first + size] for part in near], axis=1)
        query = query_ref[head].astype(F32).T.astype(BF16)
        scores = dot(query, keys) * (size**-0.5)
        scores = jnp.where(same, scores, -1e30)
        weights = jnp.exp(scores - jnp.max(scores, axis=1, keepdims=True))
        total = jnp.sum(weights, axis=1, keepdims=True)
        attn = dot_nt(weights.astype(BF16), values.astype(BF16)) / total
        place = (place_col % size == place_row) & (place_col // (4 * size) == head)
        spread = spread + dot(attn, place.astype(F32))
    spot = iota((patches, features), 1) // size % 4 == iota((patches, features), 0) % 4
    line = iota((rows, patches), 0)
    line = ((line // row_share) ^ lax.axis_index("expert")) * row_share + line % row_share
    fold = (iota((rows, patches), 1) // 4 == line).astype(F32)
    merged = dot(fold, jnp.where(spot, spread, 0.0))
    merged_ref[...] = merged.astype(BF16)
    local_mean = jnp.sum(merged, axis=1, keepdims=True) / features
    centered = merged - local_mean
    squares = jnp.sum(centered * centered, axis=1, keepdims=True)
    gain = flat_gain(gain_ref)
    gain_high = gain.astype(BF16).astype(F32)
    extra = iota((16, features), 0)
    gain_rows = jnp.where(extra == 0, gain_high, jnp.where(extra == 1, gain - gain_high, 0.0))
    left_ref[...] = jnp.concatenate([centered * gain, gain_rows], axis=0).astype(BF16)
    scalar_ref[...] = put_scalars([local_mean, squares], rows)


def project_kernel(left_ref, scalar_ref, weight_ref, _, *message_refs):
    rows = scalar_ref.shape[0]
    width = weight_ref.shape[1]
    row_share = rows // len(message_refs)
    product = dot(left_ref[...], weight_ref[...])
    gain_sum = product[rows : rows + 1] + product[rows + 1 : rows + 2]
    piece = width // row_share
    pieces = [gain_sum[:, j * piece : (j + 1) * piece] for j in range(row_share)]
    pieces = jnp.concatenate(pieces, axis=0).astype(BF16)
    scalars = scalar_ref[...].astype(BF16)
    for k, message_ref in enumerate(message_refs):
        mine = slice(k * row_share, (k + 1) * row_share)
        message_ref[:, :width] = product[mine].astype(BF16)
        message_ref[:, width : width + piece] = pieces
        message_ref[:, width + piece :] = scalars[mine]


def merge_kernel(_, *refs, width, features):
    *message_refs, out_ref, vision_ref, gain_ref = refs
    share, row_share = len(message_refs), out_ref.shape[0]
    piece = width // row_share
    parts = [ref[...].astype(F32) for ref in message_refs]
    scalars = [part[:, width + piece :] for part in parts]
    means = [get_scalar(block, 0) for block in scalars]
    squares = [get_scalar(block, 1) for block in scalars]
    mean = sum(means) / share
    spread = sum(q + features * (m - mean) * (m - mean) for q, m in zip(squares, means))
    inv_std = lax.rsqrt(spread / (share * features) + EPS)
    total = jnp.zeros((row_share, width), F32)
    gain_total = jnp.zeros((1, width), F32)
    for part, local in zip(parts, means):
        tail = part[:, width : width + piece]
        gain_sum = jnp.concatenate([tail[j : j + 1] for j in range(row_share)], axis=1)
        total = total + part[:, :width] + (local - mean) * gain_sum
        gain_total = gain_total + gain_sum
    vision_ref[...] = total * inv_std
    gain_ref[...] = gain_total
    out_ref[:, :width] = (total * inv_std).astype(BF16)
    out_ref[:, width:] = put_scalars([mean, inv_std], row_share).astype(BF16)


def stack_kernel(*refs):
    *part_refs, out_ref = refs
    out_ref[...] = stacked(part_refs)


def stacked(part_refs):
    return jnp.concatenate([ref[...].astype(F32) for ref in part_refs], axis=0).astype(BF16)


def by_chip(own_refs, sibling_ref):
    parts = []
    sibling = sibling_ref[...].astype(F32)
    for k, own_ref in enumerate(own_refs):
        half = own_ref.shape[0] // 2
        parts.append(own_ref[...].astype(F32)[:half])
        parts.append(sibling[k * half : (k + 1) * half])
    return jnp.concatenate(parts, axis=0).astype(BF16)


def other_half_kernel(*refs, count):
    out_ref = refs[-1]
    parts = [ref[...].astype(F32)[ref.shape[0] // 2 :] for ref in refs[:count]]
    out_ref[...] = jnp.concatenate(parts, axis=0).astype(BF16)


def slot_pick(slot_count, send_rows, shift):
    row, col = iota((slot_count, send_rows), 0), iota((slot_count, send_rows), 1)
    place = row % SLOTS
    pick = (col == row // SLOTS * SEND + place + shift) & (place < CAPX)
    return pick.astype(F32)


def early_kernel(down_ref, *refs):
    *early_refs, sibling_ref, text_out, grad_out = refs
    slot_count = text_out.shape[0]
    early = by_chip(early_refs, sibling_ref)
    text_out[...] = dot(slot_pick(slot_count, early.shape[0], 0), early).astype(BF16)
    back_rows = dot(slot_pick(slot_count, early.shape[0], CAPX), early).astype(BF16)
    grad_out[...] = dot_nt(back_rows, down_ref[0])


def forward_kernel(*refs, blocks):
    slots_ref, gain_ref, gate_ref, up_ref, down_ref, text_ref = refs[:6]
    vision_refs = refs[6 : 6 + blocks]
    gate_out, up_out, *down_refs = refs[6 + blocks : -2]
    h_ref, sum_ref = refs[-2:]
    _, hidden, width = gate_ref.shape
    chosen = slots_ref[...]
    is_vision = jnp.sum(chosen.astype(F32), axis=1, keepdims=True) > 0.5
    vision = jnp.concatenate([ref[:, :width] for ref in vision_refs], axis=0)
    inputs = dot(chosen, vision)
    scale = lax.rsqrt(jnp.mean(inputs * inputs, axis=1, keepdims=True) + EPS)
    normed = inputs * scale * gain_ref[...]
    h_ref[...] = jnp.where(is_vision, normed, text_ref[...].astype(F32)).astype(BF16)
    tile = tile_of(hidden)
    for i in range(hidden // tile):
        mine = slice(i * tile, (i + 1) * tile)
        gate_pre = dot_nt(h_ref[...], gate_ref[0, mine])
        up_proj = dot_nt(h_ref[...], up_ref[0, mine])
        gate_out[:, mine] = gate_pre
        up_out[:, mine] = up_proj
        activated = gate_pre * jax.nn.sigmoid(gate_pre) * up_proj
        product = dot(activated, down_ref[0, mine])
        sum_ref[...] = product if i == 0 else sum_ref[...] + product
    count = 2 * SLOTS
    for k, ref in enumerate(down_refs):
        ref[...] = sum_ref[k * count : (k + 1) * count].astype(BF16)


def backward_kernel(
    slots_ref, grad_ref, gate_in, up_in, cot_ref, gate_ref, up_ref, even_ref, odd_ref, sum_ref,
    *, blocks,
):
    hidden = gate_ref.shape[1]
    tile = tile_of(hidden)
    for i in range(hidden // tile):
        mine = slice(i * tile, (i + 1) * tile)
        act_grad = grad_ref[:, mine]
        gate_pre, up_proj = gate_in[:, mine], up_in[:, mine]
        sigmoid = jax.nn.sigmoid(gate_pre)
        gate_grad = act_grad * up_proj * sigmoid * (1.0 + gate_pre * (1.0 - sigmoid))
        up_grad = act_grad * gate_pre * sigmoid
        product = dot(gate_grad, gate_ref[0, mine]) + dot(up_grad, up_ref[0, mine])
        sum_ref[...] = product if i == 0 else sum_ref[...] + product
    grads = dot_tn(slots_ref[...], sum_ref[...].astype(BF16))
    cots = cot_ref[...].astype(F32)
    rows, row_share = grads.shape[0] // blocks, cots.shape[0] // blocks
    parts = ([], [])
    for k in range(blocks):
        parts[k % 2].append(grads[k * rows : (k + 1) * rows])
        parts[k % 2].append(cots[k * row_share : (k + 1) * row_share])
    even_ref[...] = jnp.concatenate(parts[0], axis=0).astype(BF16)
    odd_ref[...] = jnp.concatenate(parts[1], axis=0).astype(BF16)


def tile_of(hidden):
    return 256 if hidden % 256 == 0 else hidden


def halving_order(share):
    order = [0]
    step = share // 2
    while step:
        order = order + [k + step for k in order]
        step //= 2
    return [sum(1 << j for j in range(share.bit_length() - 1) if k >> j & 1) for k in order]


def pair_sum_kernel(own_ref, sibling_ref, *out_refs):
    rows = out_refs[0].shape[0]
    total = own_ref[...].astype(F32) + sibling_ref[...].astype(F32)
    for k, out_ref in enumerate(out_refs):
        out_ref[...] = total[k * rows : (k + 1) * rows].astype(BF16)


def total_of(part_refs):
    total = part_refs[0][...].astype(F32)
    for ref in part_refs[1:]:
        total = total + ref[...].astype(F32)
    return total


def chip_sum_kernel(*refs, count):
    cot_ref, *out_refs = refs[count + 1 :]
    total = total_of(refs[:count])
    rows = cot_ref.shape[0]
    for k, out_ref in enumerate(out_refs):
        out_ref[...] = total[k * rows : (k + 1) * rows].astype(BF16)
    cot_ref[...] = total[len(out_refs) * rows :].astype(BF16)


def quarters(total, out_refs):
    count = out_refs[0].shape[0]
    for k, ref in enumerate(out_refs):
        ref[...] = total[k * count : (k + 1) * count].astype(ref.dtype)


def combine_kernel(comb_ref, *refs):
    *part_refs, sibling_ref = refs[:-4]
    rows = by_chip(part_refs, sibling_ref)
    quarters(dot_tn(comb_ref[0], rows) + dot_tn(comb_ref[1], rows), refs[-4:])


def halve_kernel(*refs):
    low, high, arrived_low, arrived_high = [ref[...].astype(F32) for ref in refs[:4]]
    quarters(jnp.concatenate([low + arrived_low, high + arrived_high], axis=0), refs[4:])


def last_halve_kernel(high_ref, arrived_ref, *refs):
    refs[-1][...] = (high_ref[...] + arrived_ref[...].astype(F32)).astype(BF16)


def finish_kernel(placed_ref, text_ref, own_ref, arrived_ref, second_ref, *refs, blocks):
    vision_refs, out_ref = refs[:blocks], refs[-1]
    count, width = out_ref.shape
    tokens = placed_ref.shape[0]
    first = lax.axis_index("expert") * count
    pick = iota((count, tokens), 1) == iota((count, tokens), 0) + first
    pick = pick.astype(F32)
    placed = dot(pick, placed_ref[...])
    is_vision = jnp.sum(placed, axis=1, keepdims=True) > 0.5
    vision = jnp.concatenate([ref[:, :width] for ref in vision_refs], axis=0)
    inputs = jnp.where(is_vision, dot(placed, vision), dot(pick, text_ref[...]))
    arrived = arrived_ref[...].astype(F32) + second_ref[...].astype(F32)
    out_ref[...] = (inputs + own_ref[...] + arrived).astype(BF16)


def lay_kernel(*refs):
    *part_refs, out_ref = refs
    count = part_refs[0].shape[0]
    for k, ref in enumerate(part_refs):
        first = pl.multiple_of((lax.axis_index("expert") ^ k) * count, count)
        out_ref[pl.ds(first, count), :] = ref[...]


def norm_grad_kernel(
    own_ref, gain_ref, cot_ref, vision_ref, total_ref, *refs, features
):
    *part_refs, out_ref = refs
    width = gain_ref.shape[1]
    hidden = total_of(part_refs)
    cotangent = cot_ref[...].astype(F32)
    inputs = own_ref[:, :width].astype(F32)
    scale = lax.rsqrt(jnp.mean(inputs * inputs, axis=1, keepdims=True) + EPS)
    pulled = hidden * gain_ref[...]
    cross = jnp.mean(pulled * inputs, axis=1, keepdims=True)
    grad = cotangent + scale * pulled - inputs * (scale * scale * scale) * cross
    grad = grad.astype(BF16)
    out_ref[:, :width] = grad
    grad = grad.astype(F32)
    grad_mean = jnp.sum(grad * total_ref[...], axis=1, keepdims=True) / features
    cross_mean = jnp.sum(grad * vision_ref[...], axis=1, keepdims=True) / features
    out_ref[:, width:] = put_scalars([grad_mean, cross_mean], grad.shape[0]).astype(BF16)


def merge_grad_kernel(*refs, size):
    gain_ref, merged_ref, scalar_ref, weight_ref, *part_refs, out_ref = refs
    rows, features = merged_ref.shape
    width = weight_ref.shape[1]
    depth, patches = out_ref.shape
    row_share = part_refs[0].shape[0]
    parts = stacked(part_refs)
    normed_grad = dot_nt(parts[:, :width], weight_ref[...]) * flat_gain(gain_ref)
    means = parts[:, width:].astype(F32)
    scalars = scalar_ref[:, width:].astype(F32)
    inv_std = get_scalar(scalars, 1)
    normed = (merged_ref[...].astype(F32) - get_scalar(scalars, 0)) * inv_std
    grad = inv_std * (normed_grad - get_scalar(means, 0) - normed * get_scalar(means, 1))
    high = grad.astype(BF16)
    low = (grad - high.astype(F32)).astype(BF16)
    line = iota((patches, rows), 1)
    line = ((line // row_share) ^ lax.axis_index("expert")) * row_share + line % row_share
    unfold = (iota((patches, rows), 0) // 4 == line).astype(F32)
    spot = iota((patches, features), 1) // size % 4 == iota((patches, features), 0) % 4
    row, col = iota((depth, features), 0), iota((depth, features), 1)
    place = (col // (4 * size) == row // size) & (col % size == row % size)
    place = place.astype(F32).astype(BF16)
    out = jnp.zeros((depth, patches), F32)
    for piece in (high, low):
        wide = jnp.where(spot, dot(unfold, piece), 0.0).astype(BF16)
        out = out + dot_nt(place, wide)
    out_ref[...] = out


def whole(memory_space=pltpu.VMEM):
    return pl.BlockSpec(memory_space=memory_space)


def run(kernel, outs, *args, far=(), scratch=(), cost=1.0, vmem=VMEM_BYTES, name=None):
    specs = [whole()] * len(args)
    for place in far:
        specs[place] = whole(pl.ANY)
    return pl.pallas_call(
        kernel,
        out_shape=outs,
        in_specs=specs,
        out_specs=jax.tree.map(lambda _: whole(), outs),
        scratch_shapes=scratch,
        compiler_params=pltpu.CompilerParams(vmem_limit_bytes=vmem),
        cost_estimate=microseconds(cost),
        name=name,
    )(*args)


def to_sibling(parts, deps, name):
    rows, width = parts[0].shape
    half = run(
        functools.partial(other_half_kernel, count=len(parts)),
        shape((len(parts) * rows // 2, width)), *parts, *deps,
        far=range(len(parts), len(parts) + len(deps)), cost=0.01, name=name,
    )
    return swap(half, "blk", 1)


def microseconds(time):
    return pl.CostEstimate(flops=0, transcendentals=0, bytes_accessed=int(time * 3e6))


def after(values, deps):
    count = len(values)
    return pl.pallas_call(
        lambda *refs: None,
        out_shape=[shape(value.shape, value.dtype) for value in values],
        in_specs=[whole(pl.ANY)] * (count + len(deps)),
        out_specs=[whole(pl.ANY)] * count,
        input_output_aliases={i: i for i in range(count)},
        compiler_params=pltpu.CompilerParams(vmem_limit_bytes=VMEM_BYTES),
        cost_estimate=microseconds(0.1),
        name="after",
    )(*values, *deps)


def shape(dims, dtype=BF16):
    return jax.ShapeDtypeStruct(dims, dtype)


def swap(value, axis, step):
    count = lax.axis_size(axis)
    return lax.ppermute(value, axis, [(i, i ^ step) for i in range(count)])


def trade(parts, axis):
    return [parts[0]] + [swap(parts[k], axis, k) for k in range(1, len(parts))]


def spread_out(value, axis):
    return trade([value] * lax.axis_size(axis), axis)


def gather_blocks(value, deps=None):
    own = [value] + [swap(value, "blk", k) for k in range(2, lax.axis_size("blk"), 2)]
    if deps is not None:
        own = own[:1] + list(after(own[1:], deps))
    sibling = [swap(part, "blk", 1) for part in own]
    return [part for pair in zip(own, sibling) for part in pair]


def to_chips(parts):
    return [parts[0]] + [swap(parts[k], "blk", 2 * k) for k in range(1, len(parts))]


def body(
    queries, keys, values, image_ids, placement, merge_gain, merge_weight, text, norm_gain,
    w_gate, w_up, w_down, routes, route_gates, cotangent,
):
    blocks = lax.axis_size("blk")
    share = lax.axis_size("expert")
    heads, size, patches = queries.shape
    depth = heads * size
    rows = image_ids.shape[0]
    row_share = rows // share
    tokens, width = text.shape
    part = tokens // share
    all_rows = blocks * rows
    features = heads * 4 * size
    hidden = w_gate.shape[1]
    slot_count = blocks * SLOTS
    groups = share // 2
    routes_t, gates_t, gain_row = routes.T, route_gates.T, norm_gain[None]

    small = [
        keys.reshape(depth, patches), values.reshape(depth, patches),
        image_ids[None], placement.reshape(1, rows), routes_t,
    ]
    local = run(
        pack_kernel, shape((2 * depth + 16, patches)), *small, far=range(5),
        scratch=[pltpu.VMEM(array.shape, array.dtype) for array in small]
        + [pltpu.SemaphoreType.DMA((5,))],
        vmem=PACK_BYTES, name="pack",
    )
    comb, pick, factor = run(
        functools.partial(route_kernel, groups=groups, share=share),
        [
            shape((2, slot_count, tokens)), shape((2, blocks * SEND, tokens)),
            shape((blocks * SEND, 128), F32),
        ],
        routes_t, gates_t, cost=3.0, name="route",
    )
    send = run(
        dispatch_kernel, [shape((2 * SEND, width))] * (blocks // 2),
        pick, factor, text, gain_row, cotangent, cost=2.0, name="dispatch",
    )
    near = gather_blocks(local, send)
    early = to_chips(after(send, near[2::2]))

    weight_flat = merge_weight.reshape(features, width)
    message_width = width + width // row_share + 128
    merged, meta, left, local_scalars = run(
        functools.partial(attend_kernel, blocks=blocks, row_share=row_share),
        [
            shape((rows, features)), shape((blocks * 16, patches)), shape((rows + 16, features)),
            shape((rows, 128), F32),
        ],
        queries, merge_gain, *small, *near[1:], cost=3.0, name="attend",
    )
    message = run(
        project_kernel, [shape((row_share, message_width))] * share,
        left, local_scalars, weight_flat, early[1], far=(3,), cost=2.0, name="project",
    )
    slots, placed, back_cots = run(
        functools.partial(
            plan_kernel, blocks=blocks, groups=groups, merged_rows=rows, row_share=row_share
        ),
        [
            shape((slot_count, all_rows)), shape((tokens, all_rows)),
            shape((blocks * row_share, width)),
        ],
        meta, cotangent, cost=1.5, name="plan",
    )
    message = trade(message, "expert")
    early = early[:1] + list(after(early[1:], message[1:]))
    own, vision_exact, gain_total = run(
        functools.partial(merge_kernel, width=width, features=features),
        [
            shape((row_share, width + 128)), shape((row_share, width), F32),
            shape((1, width), F32),
        ],
        early[1], *message, far=(0,), cost=0.2, name="merge",
    )
    owns = spread_out(own, "expert")
    block_rows = run(
        stack_kernel, shape((rows, width + 128)), *owns, cost=0.2, name="stack",
    )
    text_rows, act_grad = run(
        early_kernel, [shape((slot_count, width)), shape((slot_count, hidden), F32)],
        w_down, *early, to_sibling(early, owns[1:], "early_half"), cost=3.0, name="early",
    )

    vision = gather_blocks(block_rows, [text_rows, slots])
    gate_pre, up_proj, *down = run(
        functools.partial(forward_kernel, blocks=blocks),
        [
            shape((slot_count, hidden), F32), shape((slot_count, hidden), F32),
        ] + [shape((2 * SLOTS, width))] * (blocks // 2),
        slots, gain_row, w_gate, w_up, w_down, text_rows, *vision,
        scratch=[pltpu.VMEM((slot_count, width), BF16), pltpu.VMEM((slot_count, width), F32)],
        cost=4.0, name="forward",
    )
    returned = to_chips(down)
    block = rows + row_share
    even, odd = run(
        functools.partial(backward_kernel, blocks=blocks),
        [shape((blocks // 2 * block, width))] * 2,
        slots, act_grad, gate_pre, up_proj, back_cots, w_gate, w_up,
        scratch=[pltpu.VMEM((slot_count, width), F32)],
        cost=4.0, name="backward",
    )
    grads = run(
        pair_sum_kernel, [shape((block, width))] * (blocks // 2), even, swap(odd, "blk", 1),
        cost=0.2, name="pair_sum",
    )
    grads = to_chips(grads)
    count = tokens // 4
    pieces = [shape((count, width), F32)] * 2 + [shape((count, width))] * 2
    low, high, sent_low, sent_high = run(
        combine_kernel, pieces, comb, *returned,
        to_sibling(returned, grads[:1], "returned_half"), cost=0.01, name="combine",
    )
    first_sent, step = sent_low, 1
    arrived_high = swap(sent_high, "expert", step)
    arrived_low = swap(sent_low, "expert", step)
    while count > part:
        count //= 2
        step *= 2
        pieces = [shape((count, width), F32)] * 2 + [shape((count, width))] * 2
        low, high, sent_low, sent_high = run(
            halve_kernel, pieces, low, high, arrived_low, arrived_high, cost=0.3, name="halve"
        )
        arrived_high = swap(sent_high, "expert", step)
        arrived_low = swap(sent_low, "expert", step)
    step *= 2
    chips = len(grads) - 1
    sent = run(
        last_halve_kernel, shape((part, width)), high, arrived_high, *grads[1:],
        far=range(2, 2 + chips), cost=0.3, name="last_halve",
    )
    cot_rows, *grads = run(
        functools.partial(chip_sum_kernel, count=blocks // 2),
        [shape((row_share, width))] * (share + 1), *grads, first_sent, far=(blocks // 2,), cost=0.2,
        name="chip_sum",
    )
    grads = trade(grads, "expert")
    vision_grad = run(
        functools.partial(norm_grad_kernel, features=share * features),
        shape((row_share, width + 128)),
        own, gain_row, cot_rows, vision_exact, gain_total, *grads, cost=0.3, name="norm_grad",
    )
    vision_grads = spread_out(vision_grad, "expert")
    attn_grad = run(
        functools.partial(merge_grad_kernel, size=size), shape((depth, patches), F32),
        merge_gain, merged, block_rows, weight_flat, *vision_grads, cost=4.0, name="merge_grad",
    )

    finished = run(
        functools.partial(finish_kernel, blocks=blocks), shape((part, width)),
        placed, text, low, arrived_low, swap(sent, "expert", step), *vision, *grads[1:],
        far=range(5 + blocks, 4 + blocks + share),
        cost=1.0, name="finish",
    )
    laid = {0: finished}
    while step:
        far_ones = [k for k in laid if k]
        if far_ones:
            laid.update(zip(far_ones, after([laid[k] for k in far_ones], vision_grads[1:])))
        laid.update({k + step: swap(laid[k], "expert", step) for k in list(laid)})
        step //= 2
    llm_out = run(
        lay_kernel, shape((tokens, width)), *[laid[k] for k in sorted(laid)], cost=1.0, name="lay"
    )
    return llm_out, attn_grad.reshape(heads, size, patches)


def solution(mesh):
    return jax.shard_map(
        body,
        mesh=mesh,
        in_specs=(
            P("expert", None, "blk"),
            P("expert", None, "blk"),
            P("expert", None, "blk"),
            P("blk"),
            P("blk", None),
            P("expert", None),
            P("expert", None, None),
            P("blk", None),
            P(),
            P("blk", "expert", None),
            P("blk", "expert", None),
            P("blk", "expert", None),
            P("blk", None),
            P("blk", None),
            P("blk", None),
        ),
        out_specs=(P("blk", None), P("expert", None, "blk")),
        check_vma=False,
    )
```

profile of v0, /device:TPU:0, one launch (start us, length us, event | category | flops | bytes accessed | tf_op | source)
XLA Modules:
  0.0 105.6 jit_solution(13528056359048073827)
XLA Ops:
  0.7 1.8 %pack.1 = bf16[592,128]{1,0:T(8,128)(2,1)} custom-call(bf16[288,128]{1,0:T(8,128)(2,1)} %bitcast.11, bf16[288,128]{1,0:T(8,128)(2,1)} %bitcast.13, s32[1,32]{1,0:T(1,128)} %bitcast.22, s32[1,32]{1,0:T(1,128)} %bitcast.24, s32[8,128]{1,0:T(8,128)} %bitcast.18), custom_call_target="tpu_custom_call" | custom-call | bytes 3000000 | tf_op jit(solution)/shard_map/pack/pallas_call | solution.py:513
  2.6 4.0 %collective-permute-start.3 = (bf16[592,128]{1,0:T(8,128)(2,1)}, bf16[592,128]{1,0:T(8,128)(2,1)S(1)}, u32[]{:S(2)}, u32[]{:S(2)}) collective-permute-start(bf16[592,128]{1,0:T(8,128)(2,1)} %pack.1), channel_id=1, source_target_pairs={{0,24},{4,28},{8,16},{12,20},{16,8},{20,12},{24,0},{28,4},{1,25},{... | collective-permute-start | bytes 454664 | tf_op jit(solution)/shard_map/ppermute | solution.py:559
  12.5 1.4 %collective-permute-done.2.refs_1_ = bf16[592,128]{1,0:T(8,128)(2,1)S(1)} collective-permute-done((bf16[592,128]{1,0:T(8,128)(2,1)}, bf16[592,128]{1,0:T(8,128)(2,1)S(1)}, u32[]{:S(2)}, u32[]{:S(2)}) %collective-permute-start.2) | collective-permute-done | bytes 151584 | tf_op jit(solution)/shard_map/ppermute | solution.py:559
  14.2 1.5 %collective-permute-start.7 = (bf16[48,2048]{1,0:T(8,128)(2,1)S(1)}, bf16[48,2048]{1,0:T(8,128)(2,1)S(1)}, u32[]{:S(2)}, u32[]{:S(2)}) collective-permute-start(bf16[48,2048]{1,0:T(8,128)(2,1)S(1)} %get-tuple-element.73), channel_id=1, source_target_pairs={{0,8},{4,12},{8,0},{12,4},{16,24},{20,28},{24,16},{28,20},{1,9},{5... | collective-permute-start | bytes 589832 | tf_op jit(solution)/shard_map/ppermute | solution.py:559
  19.4 2.6 %attend.1 = (bf16[32,1152]{1,0:T(8,128)(2,1)S(1)}, bf16[128,128]{1,0:T(8,128)(2,1)S(1)}, bf16[48,1152]{1,0:T(8,128)(2,1)S(1)}, f32[32,128]{1,0:T(8,128)S(1)}) custom-call(bf16[4,72,128]{2,1,0:T(8,128)(2,1)S(1)} %copy-done.12, f32[4,288]{1,0:T(4,128)S(1)} %copy-done.15, bf16[288,128]{1,0:T(8,128)(2,1)S(1)} %bitcast.12, bf16[288,128]{1,0:T(8,128)(2,1)S(1)} %bitcast.14, ...), custom_call_target="tpu_custom_call" | custom-call | bytes 9000000 | tf_op jit(solution)/shard_map/attend/pallas_call | solution.py:513
  23.0 1.7 %collective-permute-start.10 = (bf16[8,2432]{1,0:T(8,128)(2,1)S(1)}, bf16[8,2432]{1,0:T(8,128)(2,1)S(1)}, u32[]{:S(2)}, u32[]{:S(2)}) collective-permute-start(bf16[8,2432]{1,0:T(8,128)(2,1)S(1)} %get-tuple-element.78), channel_id=1, source_target_pairs={{0,1},{1,0},{2,3},{3,2},{4,5},{5,4},{6,7},{7,6},{8,9},{9,8},{10,11... | collective-permute-start | bytes 116744 | tf_op jit(solution)/shard_map/ppermute | solution.py:559
  24.6 2.6 %collective-permute-start.11 = (bf16[8,2432]{1,0:T(8,128)(2,1)S(1)}, bf16[8,2432]{1,0:T(8,128)(2,1)S(1)}, u32[]{:S(2)}, u32[]{:S(2)}) collective-permute-start(bf16[8,2432]{1,0:T(8,128)(2,1)S(1)} %get-tuple-element.79), channel_id=1, source_target_pairs={{0,2},{1,3},{2,0},{3,1},{4,6},{5,7},{6,4},{7,5},{8,10},{9,11},{10,... | collective-permute-start | bytes 116744 | tf_op jit(solution)/shard_map/ppermute | solution.py:559
  27.4 2.8 %collective-permute-done.11.refs_4_.refs_2_ = bf16[8,2432]{1,0:T(8,128)(2,1)S(1)} collective-permute-done((bf16[8,2432]{1,0:T(8,128)(2,1)S(1)}, bf16[8,2432]{1,0:T(8,128)(2,1)S(1)}, u32[]{:S(2)}, u32[]{:S(2)}) %collective-permute-start.11) | collective-permute-done | bytes 38944 | tf_op jit(solution)/shard_map/ppermute | solution.py:559
  30.2 2.8 %collective-permute-done.12.refs_5_.refs_3_ = bf16[8,2432]{1,0:T(8,128)(2,1)S(1)} collective-permute-done((bf16[8,2432]{1,0:T(8,128)(2,1)S(1)}, bf16[8,2432]{1,0:T(8,128)(2,1)S(1)}, u32[]{:S(2)}, u32[]{:S(2)}) %collective-permute-start.12) | collective-permute-done | bytes 38944 | tf_op jit(solution)/shard_map/ppermute | solution.py:559
  33.9 3.7 %collective-permute-start.13 = (bf16[8,2176]{1,0:T(8,128)(2,1)S(1)}, bf16[8,2176]{1,0:T(8,128)(2,1)S(1)}, u32[]{:S(2)}, u32[]{:S(2)}) collective-permute-start(bf16[8,2176]{1,0:T(8,128)(2,1)S(1)} %get-tuple-element.85.refs_0_.own_ref), channel_id=1, source_target_pairs={{0,1},{1,0},{2,3},{3,2},{4,5},{5,4},{6,7},{7,6},{8,9},{9,8},{10,11... | collective-permute-start | bytes 104456 | tf_op jit(solution)/shard_map/ppermute | solution.py:559
  37.6 1.4 %collective-permute-done.15.refs_6_.refs_3_ = bf16[8,2176]{1,0:T(8,128)(2,1)S(1)} collective-permute-done((bf16[8,2176]{1,0:T(8,128)(2,1)S(1)}, bf16[8,2176]{1,0:T(8,128)(2,1)S(1)}, u32[]{:S(2)}, u32[]{:S(2)}) %collective-permute-start.15) | collective-permute-done | bytes 34848 | tf_op jit(solution)/shard_map/ppermute | solution.py:559
  39.7 1.9 %collective-permute-start.20 = (bf16[32,2176]{1,0:T(8,128)(2,1)S(1)}, bf16[32,2176]{1,0:T(8,128)(2,1)S(1)}, u32[]{:S(2)}, u32[]{:S(2)}) collective-permute-start(bf16[32,2176]{1,0:T(8,128)(2,1)S(1)} %stack.1.refs_6_.refs_0_.refs_2_), channel_id=1, source_target_pairs={{0,24},{4,28},{8,16},{12,20},{16,8},{20,12},{24,0},{28,4},{1,25},{... | collective-permute-start | bytes 417800 | tf_op jit(solution)/shard_map/ppermute | solution.py:559
  45.4 1.8 %collective-permute-done.20.refs_2_ = bf16[32,2176]{1,0:T(8,128)(2,1)S(1)} collective-permute-done((bf16[32,2176]{1,0:T(8,128)(2,1)S(1)}, bf16[32,2176]{1,0:T(8,128)(2,1)S(1)}, u32[]{:S(2)}, u32[]{:S(2)}) %collective-permute-start.20) | collective-permute-done | bytes 139296 | tf_op jit(solution)/shard_map/ppermute | solution.py:559
  47.2 2.5 %collective-permute-done.19.refs_1_ = bf16[32,2176]{1,0:T(8,128)(2,1)S(1)} collective-permute-done((bf16[32,2176]{1,0:T(8,128)(2,1)S(1)}, bf16[32,2176]{1,0:T(8,128)(2,1)S(1)}, u32[]{:S(2)}, u32[]{:S(2)}) %collective-permute-start.19) | collective-permute-done | bytes 139296 | tf_op jit(solution)/shard_map/ppermute | solution.py:559
  51.7 3.3 %forward.1 = (f32[128,768]{1,0:T(8,128)S(1)}, f32[128,768]{1,0:T(8,128)S(1)}, bf16[32,2048]{1,0:T(8,128)(2,1)S(1)}, bf16[32,2048]{1,0:T(8,128)(2,1)S(1)}, bf16[3...) custom-call(bf16[128,256]{1,0:T(8,128)(2,1)S(1)} %get-tuple-element.71.refs_4_.refs_0_.slots_ref, ...), custom_call_target="tpu_custom_call" | custom-call | bytes 12000000 | tf_op jit(solution)/shard_map/forward/pallas_call | solution.py:513
  56.7 1.4 %collective-permute-start.24 = (bf16[32,2048]{1,0:T(8,128)(2,1)S(1)}, bf16[32,2048]{1,0:T(8,128)(2,1)S(1)}, u32[]{:S(2)}, u32[]{:S(2)}) collective-permute-start(bf16[32,2048]{1,0:T(8,128)(2,1)S(1)} %get-tuple-element.91), channel_id=1, source_target_pairs={{0,8},{4,12},{8,0},{12,4},{16,24},{20,28},{24,16},{28,20},{1,9},{5... | collective-permute-start | bytes 393224 | tf_op jit(solution)/shard_map/ppermute | solution.py:559
  60.3 2.5 %collective-permute-done.24.refs_1_ = bf16[32,2048]{1,0:T(8,128)(2,1)S(1)} collective-permute-done((bf16[32,2048]{1,0:T(8,128)(2,1)S(1)}, bf16[32,2048]{1,0:T(8,128)(2,1)S(1)}, u32[]{:S(2)}, u32[]{:S(2)}) %collective-permute-start.24) | collective-permute-done | bytes 131104 | tf_op jit(solution)/shard_map/ppermute | solution.py:559
  62.8 3.5 %collective-permute-done.25.refs_2_ = bf16[32,2048]{1,0:T(8,128)(2,1)S(1)} collective-permute-done((bf16[32,2048]{1,0:T(8,128)(2,1)S(1)}, bf16[32,2048]{1,0:T(8,128)(2,1)S(1)}, u32[]{:S(2)}, u32[]{:S(2)}) %collective-permute-start.25) | collective-permute-done | bytes 131104 | tf_op jit(solution)/shard_map/ppermute | solution.py:559
  67.1 1.4 %collective-permute-start.32 = (bf16[40,2048]{1,0:T(8,128)(2,1)S(1)}, bf16[40,2048]{1,0:T(8,128)(2,1)S(1)}, u32[]{:S(2)}, u32[]{:S(2)}) collective-permute-start(bf16[40,2048]{1,0:T(8,128)(2,1)S(1)} %get-tuple-element.106), channel_id=1, source_target_pairs={{0,16},{4,20},{8,24},{12,28},{16,0},{20,4},{24,8},{28,12},{1,17},{... | collective-permute-start | bytes 491528 | tf_op jit(solution)/shard_map/ppermute | solution.py:559
  68.5 1.5 %collective-permute-start.33 = (bf16[40,2048]{1,0:T(8,128)(2,1)S(1)}, bf16[40,2048]{1,0:T(8,128)(2,1)S(1)}, u32[]{:S(2)}, u32[]{:S(2)}) collective-permute-start(bf16[40,2048]{1,0:T(8,128)(2,1)S(1)} %get-tuple-element.107), channel_id=1, source_target_pairs={{0,24},{4,28},{8,16},{12,20},{16,8},{20,12},{24,0},{28,4},{1,25},{... | collective-permute-start | bytes 491528 | tf_op jit(solution)/shard_map/ppermute | solution.py:559
  70.4 2.1 %collective-permute-start.30 = (bf16[32,2048]{1,0:T(8,128)(2,1)S(1)}, bf16[32,2048]{1,0:T(8,128)(2,1)S(1)}, u32[]{:S(2)}, u32[]{:S(2)}) collective-permute-start(bf16[32,2048]{1,0:T(8,128)(2,1)S(1)} %get-tuple-element.104), channel_id=1, source_target_pairs={{0,1},{1,0},{2,3},{3,2},{4,5},{5,4},{6,7},{7,6},{8,9},{9,8},{10,11... | collective-permute-start | bytes 393224 | tf_op jit(solution)/shard_map/ppermute | solution.py:559
  73.5 2.4 %collective-permute-done.32.refs_1_.refs_2_ = bf16[40,2048]{1,0:T(8,128)(2,1)S(1)} collective-permute-done((bf16[40,2048]{1,0:T(8,128)(2,1)S(1)}, bf16[40,2048]{1,0:T(8,128)(2,1)S(1)}, u32[]{:S(2)}, u32[]{:S(2)}) %collective-permute-start.32) | collective-permute-done | bytes 163872 | tf_op jit(solution)/shard_map/ppermute | solution.py:559
  78.3 1.8 %collective-permute-start.35 = (bf16[8,2048]{1,0:T(8,128)(2,1)S(1)}, bf16[8,2048]{1,0:T(8,128)(2,1)S(1)}, u32[]{:S(2)}, u32[]{:S(2)}) collective-permute-start(bf16[8,2048]{1,0:T(8,128)(2,1)S(1)} %get-tuple-element.108), channel_id=1, source_target_pairs={{0,1},{1,0},{2,3},{3,2},{4,5},{5,4},{6,7},{7,6},{8,9},{9,8},{10,11... | collective-permute-start | bytes 98312 | tf_op jit(solution)/shard_map/ppermute | solution.py:559
  80.1 2.0 %collective-permute-start.36 = (bf16[8,2048]{1,0:T(8,128)(2,1)S(1)}, bf16[8,2048]{1,0:T(8,128)(2,1)S(1)}, u32[]{:S(2)}, u32[]{:S(2)}) collective-permute-start(bf16[8,2048]{1,0:T(8,128)(2,1)S(1)} %get-tuple-element.109), channel_id=1, source_target_pairs={{0,2},{1,3},{2,0},{3,1},{4,6},{5,7},{6,4},{7,5},{8,10},{9,11},{10,... | collective-permute-start | bytes 98312 | tf_op jit(solution)/shard_map/ppermute | solution.py:559
  82.7 5.4 %collective-permute-done.36.refs_9_.refs_2_ = bf16[8,2048]{1,0:T(8,128)(2,1)S(1)} collective-permute-done((bf16[8,2048]{1,0:T(8,128)(2,1)S(1)}, bf16[8,2048]{1,0:T(8,128)(2,1)S(1)}, u32[]{:S(2)}, u32[]{:S(2)}) %collective-permute-start.36) | collective-permute-done | bytes 32800 | tf_op jit(solution)/shard_map/ppermute | solution.py:559
  88.7 1.6 %collective-permute-start.39 = (bf16[32,2048]{1,0:T(8,128)(2,1)S(1)}, bf16[32,2048]{1,0:T(8,128)(2,1)S(1)}, u32[]{:S(2)}, u32[]{:S(2)}) collective-permute-start(bf16[32,2048]{1,0:T(8,128)(2,1)S(1)} %finish.1.refs_0_), channel_id=1, source_target_pairs={{0,2},{1,3},{2,0},{3,1},{4,6},{5,7},{6,4},{7,5},{8,10},{9,11},{10,... | collective-permute-start | bytes 393224 | tf_op jit(solution)/shard_map/ppermute | solution.py:559
  90.5 1.8 %collective-permute-start.42 = (bf16[8,2176]{1,0:T(8,128)(2,1)S(1)}, bf16[8,2176]{1,0:T(8,128)(2,1)S(1)}, u32[]{:S(2)}, u32[]{:S(2)}) collective-permute-start(bf16[8,2176]{1,0:T(8,128)(2,1)S(1)} %norm_grad.1.refs_4_), channel_id=1, source_target_pairs={{0,3},{1,2},{2,1},{3,0},{4,7},{5,6},{6,5},{7,4},{8,11},{9,10},{10,... | collective-permute-start | bytes 104456 | tf_op jit(solution)/shard_map/ppermute | solution.py:559
  92.8 2.1 %collective-permute-start.40 = (bf16[8,2176]{1,0:T(8,128)(2,1)S(1)}, bf16[8,2176]{1,0:T(8,128)(2,1)S(1)}, u32[]{:S(2)}, u32[]{:S(2)}) collective-permute-start(bf16[8,2176]{1,0:T(8,128)(2,1)S(1)} %norm_grad.1.refs_4_), channel_id=1, source_target_pairs={{0,1},{1,0},{2,3},{3,2},{4,5},{5,4},{6,7},{7,6},{8,9},{9,8},{10,11... | collective-permute-start | bytes 104456 | tf_op jit(solution)/shard_map/ppermute | solution.py:559
  94.9 1.7 %collective-permute-done.42.refs_3_.refs_7_ = bf16[8,2176]{1,0:T(8,128)(2,1)S(1)} collective-permute-done((bf16[8,2176]{1,0:T(8,128)(2,1)S(1)}, bf16[8,2176]{1,0:T(8,128)(2,1)S(1)}, u32[]{:S(2)}, u32[]{:S(2)}) %collective-permute-start.42) | collective-permute-done | bytes 34848 | tf_op jit(solution)/shard_map/ppermute | solution.py:559
  96.7 3.1 %collective-permute-done.41.refs_2_.refs_6_ = bf16[8,2176]{1,0:T(8,128)(2,1)S(1)} collective-permute-done((bf16[8,2176]{1,0:T(8,128)(2,1)S(1)}, bf16[8,2176]{1,0:T(8,128)(2,1)S(1)}, u32[]{:S(2)}, u32[]{:S(2)}) %collective-permute-start.41) | collective-permute-done | bytes 34848 | tf_op jit(solution)/shard_map/ppermute | solution.py:559
  100.0 3.0 %merge_grad.1 = f32[288,128]{1,0:T(8,128)} custom-call(f32[4,288]{1,0:T(4,128)S(1)} %copy-done.15, bf16[32,1152]{1,0:T(8,128)(2,1)S(1)} %get-tuple-element.115.refs_1_, bf16[32,2176]{1,0:T(8,128)(2,1)S(1)} %stack.1.refs_6_.refs_0_.refs_2_, bf16[1152,2048]{1,0:T(8,128)(2,1)S(1)} %bitcast.10, bf16[8,2176]{1,0:T(8,128)(2,1)S(1)} %norm_grad.1.refs_4_, ...), custom_call_target="tpu_custom_call" | custom-call | bytes 12000000 | tf_op jit(solution)/shard_map/merge_grad/pallas_call | solution.py:513
  103.0 1.8 %collective-permute-done.43.refs_3_ = bf16[32,2048]{1,0:T(8,128)(2,1)S(1)} collective-permute-done((bf16[32,2048]{1,0:T(8,128)(2,1)S(1)}, bf16[32,2048]{1,0:T(8,128)(2,1)S(1)}, u32[]{:S(2)}, u32[]{:S(2)}) %collective-permute-start.43) | collective-permute-done | bytes 131104 | tf_op jit(solution)/shard_map/ppermute | solution.py:559
  (120 shorter events, 29.8 us)
Async XLA Ops:
  2.6 10.0 %collective-permute-start.3 = (bf16[592,128]{1,0:T(8,128)(2,1)}, bf16[592,128]{1,0:T(8,128)(2,1)S(1)}, u32[]{:S(2)}, u32[]{:S(2)}) collective-permute-start(bf16[592,128]{1,0:T(8,128)(2,1)} %pack.1), channel_id=1, source_target_pairs={{0,24},{4,28},{8,16},{12,20},{16,8},{20,12},{24,0},{28,4},{1,25},{... | collective-permute-start | bytes 454664 | tf_op jit(solution)/shard_map/ppermute | solution.py:559
  6.5 7.4 %collective-permute-start.2 = (bf16[592,128]{1,0:T(8,128)(2,1)}, bf16[592,128]{1,0:T(8,128)(2,1)S(1)}, u32[]{:S(2)}, u32[]{:S(2)}) collective-permute-start(bf16[592,128]{1,0:T(8,128)(2,1)} %pack.1), channel_id=1, source_target_pairs={{0,16},{4,20},{8,24},{12,28},{16,0},{20,4},{24,8},{28,12},{1,17},{... | collective-permute-start | bytes 454664 | tf_op jit(solution)/shard_map/ppermute | solution.py:559
  7.0 7.2 %collective-permute-start.1 = (bf16[592,128]{1,0:T(8,128)(2,1)}, bf16[592,128]{1,0:T(8,128)(2,1)S(1)}, u32[]{:S(2)}, u32[]{:S(2)}) collective-permute-start(bf16[592,128]{1,0:T(8,128)(2,1)} %pack.1), channel_id=1, source_target_pairs={{0,8},{4,12},{8,0},{12,4},{16,24},{20,28},{24,16},{28,20},{1,9},{5... | collective-permute-start | bytes 454664 | tf_op jit(solution)/shard_map/ppermute | solution.py:559
  7.2 10.5 %collective-permute-start = (bf16[592,128]{1,0:T(8,128)(2,1)}, bf16[592,128]{1,0:T(8,128)(2,1)S(1)}, u32[]{:S(2)}, u32[]{:S(2)}) collective-permute-start(bf16[592,128]{1,0:T(8,128)(2,1)} %pack.1), channel_id=1, source_target_pairs={{0,4},{4,0},{8,12},{12,8},{16,20},{20,16},{24,28},{28,24},{1,5},{5... | collective-permute-start | bytes 454664 | tf_op jit(solution)/shard_map/ppermute | solution.py:559
  14.2 7.7 %collective-permute-start.7 = (bf16[48,2048]{1,0:T(8,128)(2,1)S(1)}, bf16[48,2048]{1,0:T(8,128)(2,1)S(1)}, u32[]{:S(2)}, u32[]{:S(2)}) collective-permute-start(bf16[48,2048]{1,0:T(8,128)(2,1)S(1)} %get-tuple-element.73), channel_id=1, source_target_pairs={{0,8},{4,12},{8,0},{12,4},{16,24},{20,28},{24,16},{28,20},{1,9},{5... | collective-permute-start | bytes 589832 | tf_op jit(solution)/shard_map/ppermute | solution.py:559
  15.7 11.7 %collective-permute-start.8 = (bf16[48,2048]{1,0:T(8,128)(2,1)S(1)}, bf16[48,2048]{1,0:T(8,128)(2,1)S(1)}, u32[]{:S(2)}, u32[]{:S(2)}) collective-permute-start(bf16[48,2048]{1,0:T(8,128)(2,1)S(1)} %get-tuple-element.74), channel_id=1, source_target_pairs={{0,16},{4,20},{8,24},{12,28},{16,0},{20,4},{24,8},{28,12},{1,17},{... | collective-permute-start | bytes 589832 | tf_op jit(solution)/shard_map/ppermute | solution.py:559
  16.6 10.9 %collective-permute-start.9 = (bf16[48,2048]{1,0:T(8,128)(2,1)S(1)}, bf16[48,2048]{1,0:T(8,128)(2,1)S(1)}, u32[]{:S(2)}, u32[]{:S(2)}) collective-permute-start(bf16[48,2048]{1,0:T(8,128)(2,1)S(1)} %get-tuple-element.75), channel_id=1, source_target_pairs={{0,24},{4,28},{8,16},{12,20},{16,8},{20,12},{24,0},{28,4},{1,25},{... | collective-permute-start | bytes 589832 | tf_op jit(solution)/shard_map/ppermute | solution.py:559
  24.6 5.6 %collective-permute-start.11 = (bf16[8,2432]{1,0:T(8,128)(2,1)S(1)}, bf16[8,2432]{1,0:T(8,128)(2,1)S(1)}, u32[]{:S(2)}, u32[]{:S(2)}) collective-permute-start(bf16[8,2432]{1,0:T(8,128)(2,1)S(1)} %get-tuple-element.79), channel_id=1, source_target_pairs={{0,2},{1,3},{2,0},{3,1},{4,6},{5,7},{6,4},{7,5},{8,10},{9,11},{10,... | collective-permute-start | bytes 116744 | tf_op jit(solution)/shard_map/ppermute | solution.py:559
  27.2 5.8 %collective-permute-start.12 = (bf16[8,2432]{1,0:T(8,128)(2,1)S(1)}, bf16[8,2432]{1,0:T(8,128)(2,1)S(1)}, u32[]{:S(2)}, u32[]{:S(2)}) collective-permute-start(bf16[8,2432]{1,0:T(8,128)(2,1)S(1)} %get-tuple-element.80), channel_id=1, source_target_pairs={{0,3},{1,2},{2,1},{3,0},{4,7},{5,6},{6,5},{7,4},{8,11},{9,10},{10,... | collective-permute-start | bytes 116744 | tf_op jit(solution)/shard_map/ppermute | solution.py:559
  33.1 5.9 %collective-permute-start.15 = (bf16[8,2176]{1,0:T(8,128)(2,1)S(1)}, bf16[8,2176]{1,0:T(8,128)(2,1)S(1)}, u32[]{:S(2)}, u32[]{:S(2)}) collective-permute-start(bf16[8,2176]{1,0:T(8,128)(2,1)S(1)} %get-tuple-element.85.refs_0_.own_ref), channel_id=1, source_target_pairs={{0,3},{1,2},{2,1},{3,0},{4,7},{5,6},{6,5},{7,4},{8,11},{9,10},{10,... | collective-permute-start | bytes 104456 | tf_op jit(solution)/shard_map/ppermute | solution.py:559
  33.9 5.7 %collective-permute-start.14 = (bf16[8,2176]{1,0:T(8,128)(2,1)S(1)}, bf16[8,2176]{1,0:T(8,128)(2,1)S(1)}, u32[]{:S(2)}, u32[]{:S(2)}) collective-permute-start(bf16[8,2176]{1,0:T(8,128)(2,1)S(1)} %get-tuple-element.85.refs_0_.own_ref), channel_id=1, source_target_pairs={{0,2},{1,3},{2,0},{3,1},{4,6},{5,7},{6,4},{7,5},{8,10},{9,11},{10,... | collective-permute-start | bytes 104456 | tf_op jit(solution)/shard_map/ppermute | solution.py:559
  33.9 5.7 %collective-permute-start.13 = (bf16[8,2176]{1,0:T(8,128)(2,1)S(1)}, bf16[8,2176]{1,0:T(8,128)(2,1)S(1)}, u32[]{:S(2)}, u32[]{:S(2)}) collective-permute-start(bf16[8,2176]{1,0:T(8,128)(2,1)S(1)} %get-tuple-element.85.refs_0_.own_ref), channel_id=1, source_target_pairs={{0,1},{1,0},{2,3},{3,2},{4,5},{5,4},{6,7},{7,6},{8,9},{9,8},{10,11... | collective-permute-start | bytes 104456 | tf_op jit(solution)/shard_map/ppermute | solution.py:559
  39.7 7.5 %collective-permute-start.20 = (bf16[32,2176]{1,0:T(8,128)(2,1)S(1)}, bf16[32,2176]{1,0:T(8,128)(2,1)S(1)}, u32[]{:S(2)}, u32[]{:S(2)}) collective-permute-start(bf16[32,2176]{1,0:T(8,128)(2,1)S(1)} %stack.1.refs_6_.refs_0_.refs_2_), channel_id=1, source_target_pairs={{0,24},{4,28},{8,16},{12,20},{16,8},{20,12},{24,0},{28,4},{1,25},{... | collective-permute-start | bytes 417800 | tf_op jit(solution)/shard_map/ppermute | solution.py:559
  41.6 8.1 %collective-permute-start.19 = (bf16[32,2176]{1,0:T(8,128)(2,1)S(1)}, bf16[32,2176]{1,0:T(8,128)(2,1)S(1)}, u32[]{:S(2)}, u32[]{:S(2)}) collective-permute-start(bf16[32,2176]{1,0:T(8,128)(2,1)S(1)} %stack.1.refs_6_.refs_0_.refs_2_), channel_id=1, source_target_pairs={{0,16},{4,20},{8,24},{12,28},{16,0},{20,4},{24,8},{28,12},{1,17},{... | collective-permute-start | bytes 417800 | tf_op jit(solution)/shard_map/ppermute | solution.py:559
  42.7 7.1 %collective-permute-start.18 = (bf16[32,2176]{1,0:T(8,128)(2,1)S(1)}, bf16[32,2176]{1,0:T(8,128)(2,1)S(1)}, u32[]{:S(2)}, u32[]{:S(2)}) collective-permute-start(bf16[32,2176]{1,0:T(8,128)(2,1)S(1)} %stack.1.refs_6_.refs_0_.refs_2_), channel_id=1, source_target_pairs={{0,8},{4,12},{8,0},{12,4},{16,24},{20,28},{24,16},{28,20},{1,9},{5... | collective-permute-start | bytes 417800 | tf_op jit(solution)/shard_map/ppermute | solution.py:559
  44.0 6.4 %collective-permute-start.17 = (bf16[32,2176]{1,0:T(8,128)(2,1)S(1)}, bf16[32,2176]{1,0:T(8,128)(2,1)S(1)}, u32[]{:S(2)}, u32[]{:S(2)}) collective-permute-start(bf16[32,2176]{1,0:T(8,128)(2,1)S(1)} %stack.1.refs_6_.refs_0_.refs_2_), channel_id=1, source_target_pairs={{0,4},{4,0},{8,12},{12,8},{16,20},{20,16},{24,28},{28,24},{1,5},{5... | collective-permute-start | bytes 417800 | tf_op jit(solution)/shard_map/ppermute | solution.py:559
  56.7 6.1 %collective-permute-start.24 = (bf16[32,2048]{1,0:T(8,128)(2,1)S(1)}, bf16[32,2048]{1,0:T(8,128)(2,1)S(1)}, u32[]{:S(2)}, u32[]{:S(2)}) collective-permute-start(bf16[32,2048]{1,0:T(8,128)(2,1)S(1)} %get-tuple-element.91), channel_id=1, source_target_pairs={{0,8},{4,12},{8,0},{12,4},{16,24},{20,28},{24,16},{28,20},{1,9},{5... | collective-permute-start | bytes 393224 | tf_op jit(solution)/shard_map/ppermute | solution.py:559
  58.1 8.2 %collective-permute-start.25 = (bf16[32,2048]{1,0:T(8,128)(2,1)S(1)}, bf16[32,2048]{1,0:T(8,128)(2,1)S(1)}, u32[]{:S(2)}, u32[]{:S(2)}) collective-permute-start(bf16[32,2048]{1,0:T(8,128)(2,1)S(1)} %get-tuple-element.92), channel_id=1, source_target_pairs={{0,16},{4,20},{8,24},{12,28},{16,0},{20,4},{24,8},{28,12},{1,17},{... | collective-permute-start | bytes 393224 | tf_op jit(solution)/shard_map/ppermute | solution.py:559
  58.9 7.4 %collective-permute-start.26 = (bf16[32,2048]{1,0:T(8,128)(2,1)S(1)}, bf16[32,2048]{1,0:T(8,128)(2,1)S(1)}, u32[]{:S(2)}, u32[]{:S(2)}) collective-permute-start(bf16[32,2048]{1,0:T(8,128)(2,1)S(1)} %get-tuple-element.93), channel_id=1, source_target_pairs={{0,24},{4,28},{8,16},{12,20},{16,8},{20,12},{24,0},{28,4},{1,25},{... | collective-permute-start | bytes 393224 | tf_op jit(solution)/shard_map/ppermute | solution.py:559
  66.4 7.1 %collective-permute-start.31 = (bf16[40,2048]{1,0:T(8,128)(2,1)S(1)}, bf16[40,2048]{1,0:T(8,128)(2,1)S(1)}, u32[]{:S(2)}, u32[]{:S(2)}) collective-permute-start(bf16[40,2048]{1,0:T(8,128)(2,1)S(1)} %get-tuple-element.105), channel_id=1, source_target_pairs={{0,8},{4,12},{8,0},{12,4},{16,24},{20,28},{24,16},{28,20},{1,9},{5... | collective-permute-start | bytes 491528 | tf_op jit(solution)/shard_map/ppermute | solution.py:559
  67.1 8.8 %collective-permute-start.32 = (bf16[40,2048]{1,0:T(8,128)(2,1)S(1)}, bf16[40,2048]{1,0:T(8,128)(2,1)S(1)}, u32[]{:S(2)}, u32[]{:S(2)}) collective-permute-start(bf16[40,2048]{1,0:T(8,128)(2,1)S(1)} %get-tuple-element.106), channel_id=1, source_target_pairs={{0,16},{4,20},{8,24},{12,28},{16,0},{20,4},{24,8},{28,12},{1,17},{... | collective-permute-start | bytes 491528 | tf_op jit(solution)/shard_map/ppermute | solution.py:559
  68.5 8.4 %collective-permute-start.33 = (bf16[40,2048]{1,0:T(8,128)(2,1)S(1)}, bf16[40,2048]{1,0:T(8,128)(2,1)S(1)}, u32[]{:S(2)}, u32[]{:S(2)}) collective-permute-start(bf16[40,2048]{1,0:T(8,128)(2,1)S(1)} %get-tuple-element.107), channel_id=1, source_target_pairs={{0,24},{4,28},{8,16},{12,20},{16,8},{20,12},{24,0},{28,4},{1,25},{... | collective-permute-start | bytes 491528 | tf_op jit(solution)/shard_map/ppermute | solution.py:559
  70.4 6.4 %collective-permute-start.30 = (bf16[32,2048]{1,0:T(8,128)(2,1)S(1)}, bf16[32,2048]{1,0:T(8,128)(2,1)S(1)}, u32[]{:S(2)}, u32[]{:S(2)}) collective-permute-start(bf16[32,2048]{1,0:T(8,128)(2,1)S(1)} %get-tuple-element.104), channel_id=1, source_target_pairs={{0,1},{1,0},{2,3},{3,2},{4,5},{5,4},{6,7},{7,6},{8,9},{9,8},{10,11... | collective-permute-start | bytes 393224 | tf_op jit(solution)/shard_map/ppermute | solution.py:559
  72.5 15.6 %collective-permute-start.29 = (bf16[32,2048]{1,0:T(8,128)(2,1)S(1)}, bf16[32,2048]{1,0:T(8,128)(2,1)S(1)}, u32[]{:S(2)}, u32[]{:S(2)}) collective-permute-start(bf16[32,2048]{1,0:T(8,128)(2,1)S(1)} %get-tuple-element.102.refs_4_), channel_id=1, source_target_pairs={{0,1},{1,0},{2,3},{3,2},{4,5},{5,4},{6,7},{7,6},{8,9},{9,8},{10,11... | collective-permute-start | bytes 393224 | tf_op jit(solution)/shard_map/ppermute | solution.py:559
  76.9 11.2 %collective-permute-start.34 = (bf16[32,2048]{1,0:T(8,128)(2,1)S(1)}, bf16[32,2048]{1,0:T(8,128)(2,1)S(1)}, u32[]{:S(2)}, u32[]{:S(2)}) collective-permute-start(bf16[32,2048]{1,0:T(8,128)(2,1)S(1)} %last_halve.1), channel_id=1, source_target_pairs={{0,2},{1,3},{2,0},{3,1},{4,6},{5,7},{6,4},{7,5},{8,10},{9,11},{10,... | collective-permute-start | bytes 393224 | tf_op jit(solution)/shard_map/ppermute | solution.py:559
  80.1 8.1 %collective-permute-start.36 = (bf16[8,2048]{1,0:T(8,128)(2,1)S(1)}, bf16[8,2048]{1,0:T(8,128)(2,1)S(1)}, u32[]{:S(2)}, u32[]{:S(2)}) collective-permute-start(bf16[8,2048]{1,0:T(8,128)(2,1)S(1)} %get-tuple-element.109), channel_id=1, source_target_pairs={{0,2},{1,3},{2,0},{3,1},{4,6},{5,7},{6,4},{7,5},{8,10},{9,11},{10,... | collective-permute-start | bytes 98312 | tf_op jit(solution)/shard_map/ppermute | solution.py:559
  82.1 6.1 %collective-permute-start.37 = (bf16[8,2048]{1,0:T(8,128)(2,1)S(1)}, bf16[8,2048]{1,0:T(8,128)(2,1)S(1)}, u32[]{:S(2)}, u32[]{:S(2)}) collective-permute-start(bf16[8,2048]{1,0:T(8,128)(2,1)S(1)} %get-tuple-element.110), channel_id=1, source_target_pairs={{0,3},{1,2},{2,1},{3,0},{4,7},{5,6},{6,5},{7,4},{8,11},{9,10},{10,... | collective-permute-start | bytes 98312 | tf_op jit(solution)/shard_map/ppermute | solution.py:559
  88.7 11.1 %collective-permute-start.39 = (bf16[32,2048]{1,0:T(8,128)(2,1)S(1)}, bf16[32,2048]{1,0:T(8,128)(2,1)S(1)}, u32[]{:S(2)}, u32[]{:S(2)}) collective-permute-start(bf16[32,2048]{1,0:T(8,128)(2,1)S(1)} %finish.1.refs_0_), channel_id=1, source_target_pairs={{0,2},{1,3},{2,0},{3,1},{4,6},{5,7},{6,4},{7,5},{8,10},{9,11},{10,... | collective-permute-start | bytes 393224 | tf_op jit(solution)/shard_map/ppermute | solution.py:559
  90.5 6.2 %collective-permute-start.42 = (bf16[8,2176]{1,0:T(8,128)(2,1)S(1)}, bf16[8,2176]{1,0:T(8,128)(2,1)S(1)}, u32[]{:S(2)}, u32[]{:S(2)}) collective-permute-start(bf16[8,2176]{1,0:T(8,128)(2,1)S(1)} %norm_grad.1.refs_4_), channel_id=1, source_target_pairs={{0,3},{1,2},{2,1},{3,0},{4,7},{5,6},{6,5},{7,4},{8,11},{9,10},{10,... | collective-permute-start | bytes 104456 | tf_op jit(solution)/shard_map/ppermute | solution.py:559
  92.2 7.5 %collective-permute-start.41 = (bf16[8,2176]{1,0:T(8,128)(2,1)S(1)}, bf16[8,2176]{1,0:T(8,128)(2,1)S(1)}, u32[]{:S(2)}, u32[]{:S(2)}) collective-permute-start(bf16[8,2176]{1,0:T(8,128)(2,1)S(1)} %norm_grad.1.refs_4_), channel_id=1, source_target_pairs={{0,2},{1,3},{2,0},{3,1},{4,6},{5,7},{6,4},{7,5},{8,10},{9,11},{10,... | collective-permute-start | bytes 104456 | tf_op jit(solution)/shard_map/ppermute | solution.py:559
  92.8 7.0 %collective-permute-start.40 = (bf16[8,2176]{1,0:T(8,128)(2,1)S(1)}, bf16[8,2176]{1,0:T(8,128)(2,1)S(1)}, u32[]{:S(2)}, u32[]{:S(2)}) collective-permute-start(bf16[8,2176]{1,0:T(8,128)(2,1)S(1)} %norm_grad.1.refs_4_), channel_id=1, source_target_pairs={{0,1},{1,0},{2,3},{3,2},{4,5},{5,4},{6,7},{7,6},{8,9},{9,8},{10,11... | collective-permute-start | bytes 104456 | tf_op jit(solution)/shard_map/ppermute | solution.py:559
  94.9 8.1 %collective-permute-start.38 = (bf16[32,2048]{1,0:T(8,128)(2,1)S(1)}, bf16[32,2048]{1,0:T(8,128)(2,1)S(1)}, u32[]{:S(2)}, u32[]{:S(2)}) collective-permute-start(bf16[32,2048]{1,0:T(8,128)(2,1)S(1)} %finish.1.refs_0_), channel_id=1, source_target_pairs={{0,1},{1,0},{2,3},{3,2},{4,5},{5,4},{6,7},{7,6},{8,9},{9,8},{10,11... | collective-permute-start | bytes 393224 | tf_op jit(solution)/shard_map/ppermute | solution.py:559
  (31 other events, 302.1 us)
where the time goes:
time: 106 us
  starting transfers between devices  43.2 us (41%)
  waiting for transfers between devices  38.5 us (36%)
  Pallas kernels  18.7 us (18%)
  local copies, waits for them, and re-layouts  4.22 us (4%)
    ppermute x44, starting transfers between devices, swap(): return lax.ppermute(value, axis, [(i, i ^ step) for i in range(count)])  43.2 us
    ppermute x44, waiting for transfers between devices, swap(): return lax.ppermute(value, axis, [(i, i ^ step) for i in range(count)])  38.5 us
    pallas_call x21, Pallas kernels, run(): pl.pallas_call(kernel, out_shape=outs, in_specs=specs, out_specs=jax.tree...  18.7 us
    unnamed x38, local copies, waits for them, and re-layouts  4.22 us
  transfers between devices with their start and end apart: 44, of which 23 were waited for; matrix products, arithmetic and copies ran while one was open for 0% of the time, Pallas kernels for 10%

commit v1 on v0

--- a/solution.py
+++ b/solution.py
@@ -8,7 +8,7 @@
 from jax.sharding import PartitionSpec as P
 
 CAPX = 10
-SLOTS = 16
+SLOTS = 12
 SEND = 24
 EPS = 1e-06
 VMEM_BYTES = 16 * 1024 * 1024
@@ -426,23 +426,22 @@
     quarters(jnp.concatenate([low + arrived_low, high + arrived_high], axis=0), refs[4:])
 
 
-def last_halve_kernel(high_ref, arrived_ref, *refs):
-    refs[-1][...] = (high_ref[...] + arrived_ref[...].astype(F32)).astype(BF16)
-
-
-def finish_kernel(placed_ref, text_ref, own_ref, arrived_ref, second_ref, *refs, blocks):
+def add_kernel(own_ref, arrived_ref, *refs):
+    refs[-1][...] = (own_ref[...] + arrived_ref[...].astype(F32)).astype(BF16)
+
+
+def finish_kernel(placed_ref, text_ref, own_ref, arrived_ref, *refs, blocks, turn):
     vision_refs, out_ref = refs[:blocks], refs[-1]
     count, width = out_ref.shape
     tokens = placed_ref.shape[0]
-    first = lax.axis_index("expert") * count
+    first = (lax.axis_index("expert") ^ turn) * count
     pick = iota((count, tokens), 1) == iota((count, tokens), 0) + first
     pick = pick.astype(F32)
     placed = dot(pick, placed_ref[...])
     is_vision = jnp.sum(placed, axis=1, keepdims=True) > 0.5
     vision = jnp.concatenate([ref[:, :width] for ref in vision_refs], axis=0)
     inputs = jnp.where(is_vision, dot(placed, vision), dot(pick, text_ref[...]))
-    arrived = arrived_ref[...].astype(F32) + second_ref[...].astype(F32)
-    out_ref[...] = (inputs + own_ref[...] + arrived).astype(BF16)
+    out_ref[...] = (inputs + (own_ref[...].astype(F32) + arrived_ref[...].astype(F32))).astype(BF16)
 
 
 def lay_kernel(*refs):
@@ -710,10 +709,15 @@
         arrived_low = swap(sent_low, "expert", step)
     step *= 2
     chips = len(grads) - 1
-    sent = run(
-        last_halve_kernel, shape((part, width)), high, arrived_high, *grads[1:],
-        far=range(2, 2 + chips), cost=0.3, name="last_halve",
-    )
+
+    def add(own_part, arrived, name):
+        return run(
+            add_kernel, shape((part, width)), own_part, arrived, *grads[1:],
+            far=range(2, 2 + chips), cost=0.3, name=name,
+        )
+
+    sums = [add(low, arrived_low, "add_low"), add(high, arrived_high, "add_high")]
+    others = [swap(value, "expert", step) for value in sums][::-1]
     cot_rows, *grads = run(
         functools.partial(chip_sum_kernel, count=blocks // 2),
         [shape((row_share, width))] * (share + 1), *grads, first_sent, far=(blocks // 2,), cost=0.2,
@@ -731,19 +735,16 @@
         merge_gain, merged, block_rows, weight_flat, *vision_grads, cost=4.0, name="merge_grad",
     )
 
-    finished = run(
-        functools.partial(finish_kernel, blocks=blocks), shape((part, width)),
-        placed, text, low, arrived_low, swap(sent, "expert", step), *vision, *grads[1:],
-        far=range(5 + blocks, 4 + blocks + share),
-        cost=1.0, name="finish",
-    )
-    laid = {0: finished}
-    while step:
-        far_ones = [k for k in laid if k]
-        if far_ones:
-            laid.update(zip(far_ones, after([laid[k] for k in far_ones], vision_grads[1:])))
+    laid = {}
+    for turn, value, other, gate in zip((0, step), sums, others, (grads, vision_grads)):
+        laid[turn] = run(
+            functools.partial(finish_kernel, blocks=blocks, turn=turn), shape((part, width)),
+            placed, text, value, other, *vision, *gate[1:],
+            far=range(4 + blocks, 3 + blocks + share), cost=1.0, name="finish",
+        )
+    while step > 1:
+        step //= 2
         laid.update({k + step: swap(laid[k], "expert", step) for k in list(laid)})
-        step //= 2
     llm_out = run(
         lay_kernel, shape((tokens, width)), *[laid[k] for k in sorted(laid)], cost=1.0, name="lay"
     )

time: 106 us -> 107 us (level)
    pallas_call x21 -> x23, Pallas kernels: 18.7 us -> 19.2 us  [run(): pl.pallas_call(kernel, out_shape=outs, in_specs=specs, out_specs=jax.tree...]
  transfers between devices with their start and end apart: 44 -> 44, of which waited for: 23 -> 25; matrix products, arithmetic and copies ran while one was open for 0% -> 0% of each run, Pallas kernels for 10% -> 11%
where the time goes in v1:
time: 107 us; the launch traced here: 106 us
  starting transfers between devices  44.2 us (41%)
  waiting for transfers between devices  37.5 us (35%)
  Pallas kernels  19.2 us (18%)
  local copies, waits for them, and re-layouts  4.22 us (4%)
    ppermute x44, starting transfers between devices, swap(): return lax.ppermute(value, axis, [(i, i ^ step) for i in range(count)])  44.2 us
    ppermute x44, waiting for transfers between devices, swap(): return lax.ppermute(value, axis, [(i, i ^ step) for i in range(count)])  37.5 us
    pallas_call x23, Pallas kernels, run(): pl.pallas_call(kernel, out_shape=outs, in_specs=specs, out_specs=jax.tree...  19.2 us
    unnamed x38, local copies, waits for them, and re-layouts  4.22 us
  transfers between devices with their start and end apart: 44, of which 25 were waited for; matrix products, arithmetic and copies ran while one was open for 0% of the time, Pallas kernels for 11%

profile of v1, /device:TPU:0, one launch (start us, length us, event | category | flops | bytes accessed | tf_op | source)
XLA Modules:
  0.0 106.2 jit_solution(6980461923862969783)
XLA Ops:
  0.7 1.8 %pack.1 = bf16[592,128]{1,0:T(8,128)(2,1)} custom-call(bf16[288,128]{1,0:T(8,128)(2,1)} %bitcast.11, bf16[288,128]{1,0:T(8,128)(2,1)} %bitcast.13, s32[1,32]{1,0:T(1,128)} %bitcast.22, s32[1,32]{1,0:T(1,128)} %bitcast.24, s32[8,128]{1,0:T(8,128)} %bitcast.18), custom_call_target="tpu_custom_call" | custom-call | bytes 3000000 | tf_op jit(solution)/shard_map/pack/pallas_call | solution.py:512
  2.6 4.0 %collective-permute-start.3 = (bf16[592,128]{1,0:T(8,128)(2,1)}, bf16[592,128]{1,0:T(8,128)(2,1)S(1)}, u32[]{:S(2)}, u32[]{:S(2)}) collective-permute-start(bf16[592,128]{1,0:T(8,128)(2,1)} %pack.1), channel_id=1, source_target_pairs={{0,24},{4,28},{8,16},{12,20},{16,8},{20,12},{24,0},{28,4},{1,25},{... | collective-permute-start | bytes 454664 | tf_op jit(solution)/shard_map/ppermute | solution.py:558
  12.6 1.4 %collective-permute-done.2.refs_1_ = bf16[592,128]{1,0:T(8,128)(2,1)S(1)} collective-permute-done((bf16[592,128]{1,0:T(8,128)(2,1)}, bf16[592,128]{1,0:T(8,128)(2,1)S(1)}, u32[]{:S(2)}, u32[]{:S(2)}) %collective-permute-start.2) | collective-permute-done | bytes 151584 | tf_op jit(solution)/shard_map/ppermute | solution.py:558
  14.2 1.5 %collective-permute-start.7 = (bf16[48,2048]{1,0:T(8,128)(2,1)S(1)}, bf16[48,2048]{1,0:T(8,128)(2,1)S(1)}, u32[]{:S(2)}, u32[]{:S(2)}) collective-permute-start(bf16[48,2048]{1,0:T(8,128)(2,1)S(1)} %get-tuple-element.73), channel_id=1, source_target_pairs={{0,8},{4,12},{8,0},{12,4},{16,24},{20,28},{24,16},{28,20},{1,9},{5... | collective-permute-start | bytes 589832 | tf_op jit(solution)/shard_map/ppermute | solution.py:558
  19.4 2.6 %attend.1 = (bf16[32,1152]{1,0:T(8,128)(2,1)S(1)}, bf16[128,128]{1,0:T(8,128)(2,1)S(1)}, bf16[48,1152]{1,0:T(8,128)(2,1)S(1)}, f32[32,128]{1,0:T(8,128)S(1)}) custom-call(bf16[4,72,128]{2,1,0:T(8,128)(2,1)S(1)} %copy-done.12, f32[4,288]{1,0:T(4,128)S(1)} %copy-done.15, bf16[288,128]{1,0:T(8,128)(2,1)S(1)} %bitcast.12, bf16[288,128]{1,0:T(8,128)(2,1)S(1)} %bitcast.14, ...), custom_call_target="tpu_custom_call" | custom-call | bytes 9000000 | tf_op jit(solution)/shard_map/attend/pallas_call | solution.py:512
  23.0 1.6 %collective-permute-start.10 = (bf16[8,2432]{1,0:T(8,128)(2,1)S(1)}, bf16[8,2432]{1,0:T(8,128)(2,1)S(1)}, u32[]{:S(2)}, u32[]{:S(2)}) collective-permute-start(bf16[8,2432]{1,0:T(8,128)(2,1)S(1)} %get-tuple-element.78), channel_id=1, source_target_pairs={{0,1},{1,0},{2,3},{3,2},{4,5},{5,4},{6,7},{7,6},{8,9},{9,8},{10,11... | collective-permute-start | bytes 116744 | tf_op jit(solution)/shard_map/ppermute | solution.py:558
  24.6 2.6 %collective-permute-start.11 = (bf16[8,2432]{1,0:T(8,128)(2,1)S(1)}, bf16[8,2432]{1,0:T(8,128)(2,1)S(1)}, u32[]{:S(2)}, u32[]{:S(2)}) collective-permute-start(bf16[8,2432]{1,0:T(8,128)(2,1)S(1)} %get-tuple-element.79), channel_id=1, source_target_pairs={{0,2},{1,3},{2,0},{3,1},{4,6},{5,7},{6,4},{7,5},{8,10},{9,11},{10,... | collective-permute-start | bytes 116744 | tf_op jit(solution)/shard_map/ppermute | solution.py:558
  27.4 2.8 %collective-permute-done.11.refs_4_.refs_2_ = bf16[8,2432]{1,0:T(8,128)(2,1)S(1)} collective-permute-done((bf16[8,2432]{1,0:T(8,128)(2,1)S(1)}, bf16[8,2432]{1,0:T(8,128)(2,1)S(1)}, u32[]{:S(2)}, u32[]{:S(2)}) %collective-permute-start.11) | collective-permute-done | bytes 38944 | tf_op jit(solution)/shard_map/ppermute | solution.py:558
  30.2 2.8 %collective-permute-done.12.refs_5_.refs_3_ = bf16[8,2432]{1,0:T(8,128)(2,1)S(1)} collective-permute-done((bf16[8,2432]{1,0:T(8,128)(2,1)S(1)}, bf16[8,2432]{1,0:T(8,128)(2,1)S(1)}, u32[]{:S(2)}, u32[]{:S(2)}) %collective-permute-start.12) | collective-permute-done | bytes 38944 | tf_op jit(solution)/shard_map/ppermute | solution.py:558
  33.9 3.7 %collective-permute-start.13 = (bf16[8,2176]{1,0:T(8,128)(2,1)S(1)}, bf16[8,2176]{1,0:T(8,128)(2,1)S(1)}, u32[]{:S(2)}, u32[]{:S(2)}) collective-permute-start(bf16[8,2176]{1,0:T(8,128)(2,1)S(1)} %get-tuple-element.85.refs_0_.own_ref), channel_id=1, source_target_pairs={{0,1},{1,0},{2,3},{3,2},{4,5},{5,4},{6,7},{7,6},{8,9},{9,8},{10,11... | collective-permute-start | bytes 104456 | tf_op jit(solution)/shard_map/ppermute | solution.py:558
  37.6 1.4 %collective-permute-done.15.refs_6_.refs_3_ = bf16[8,2176]{1,0:T(8,128)(2,1)S(1)} collective-permute-done((bf16[8,2176]{1,0:T(8,128)(2,1)S(1)}, bf16[8,2176]{1,0:T(8,128)(2,1)S(1)}, u32[]{:S(2)}, u32[]{:S(2)}) %collective-permute-start.15) | collective-permute-done | bytes 34848 | tf_op jit(solution)/shard_map/ppermute | solution.py:558
  39.7 1.9 %collective-permute-start.20 = (bf16[32,2176]{1,0:T(8,128)(2,1)S(1)}, bf16[32,2176]{1,0:T(8,128)(2,1)S(1)}, u32[]{:S(2)}, u32[]{:S(2)}) collective-permute-start(bf16[32,2176]{1,0:T(8,128)(2,1)S(1)} %stack.1.refs_6_.refs_0_.refs_2_), channel_id=1, source_target_pairs={{0,24},{4,28},{8,16},{12,20},{16,8},{20,12},{24,0},{28,4},{1,25},{... | collective-permute-start | bytes 417800 | tf_op jit(solution)/shard_map/ppermute | solution.py:558
  44.0 1.3 %early.1 = (bf16[96,2048]{1,0:T(8,128)(2,1)S(1)}, f32[96,768]{1,0:T(8,128)S(1)}) custom-call(bf16[1,768,2048]{2,1,0:T(8,128)(2,1)S(1)} %copy-done.3, bf16[48,2048]{1,0:T(8,128)(2,1)S(1)} %get-tuple-element.72.refs_0_, bf16[48,2048]{1,0:T(8,128)(2,1)S(1)} %get-tuple-element.81._.refs_1_, bf16[48,2048]{1,0:T(8,128)(2,1)S(1)} %get-tuple-element.82.refs_2_, ...), custom_call_target="tpu_custom_call" | custom-call | bytes 9000000 | tf_op jit(solution)/shard_map/early/pallas_call | solution.py:512
  45.3 1.9 %collective-permute-done.20.refs_2_ = bf16[32,2176]{1,0:T(8,128)(2,1)S(1)} collective-permute-done((bf16[32,2176]{1,0:T(8,128)(2,1)S(1)}, bf16[32,2176]{1,0:T(8,128)(2,1)S(1)}, u32[]{:S(2)}, u32[]{:S(2)}) %collective-permute-start.20) | collective-permute-done | bytes 139296 | tf_op jit(solution)/shard_map/ppermute | solution.py:558
  47.2 2.5 %collective-permute-done.19.refs_1_ = bf16[32,2176]{1,0:T(8,128)(2,1)S(1)} collective-permute-done((bf16[32,2176]{1,0:T(8,128)(2,1)S(1)}, bf16[32,2176]{1,0:T(8,128)(2,1)S(1)}, u32[]{:S(2)}, u32[]{:S(2)}) %collective-permute-start.19) | collective-permute-done | bytes 139296 | tf_op jit(solution)/shard_map/ppermute | solution.py:558
  51.7 3.2 %forward.1 = (f32[96,768]{1,0:T(8,128)S(1)}, f32[96,768]{1,0:T(8,128)S(1)}, bf16[24,2048]{1,0:T(8,128)(2,1)S(1)}, bf16[24,2048]{1,0:T(8,128)(2,1)S(1)}, bf16[24,...) custom-call(bf16[96,256]{1,0:T(8,128)(2,1)S(1)} %get-tuple-element.71.refs_4_.refs_0_.slots_ref, ...), custom_call_target="tpu_custom_call" | custom-call | bytes 12000000 | tf_op jit(solution)/shard_map/forward/pallas_call | solution.py:512
  54.9 1.5 %backward.1 = (bf16[160,2048]{1,0:T(8,128)(2,1)S(1)}, bf16[160,2048]{1,0:T(8,128)(2,1)S(1)}) custom-call(bf16[96,256]{1,0:T(8,128)(2,1)S(1)} %get-tuple-element.71.refs_4_.refs_0_.slots_ref, f32[96,768]{1,0:T(8,128)S(1)} %get-tuple-element.94.grad_ref, f32[96,768]{1,0:T(8,128)S(1)} %get-tuple-element.95.gate_in, f32[96,768]{1,0:T(8,128)S(1)} %get-tuple-element.96.up_in, ...), custom_call_target="tpu_custom_call" | custom-call | bytes 12000000 | tf_op jit(solution)/shard_map/backward/pallas_call | solution.py:512
  56.7 1.4 %collective-permute-start.24 = (bf16[24,2048]{1,0:T(8,128)(2,1)S(1)}, bf16[24,2048]{1,0:T(8,128)(2,1)S(1)}, u32[]{:S(2)}, u32[]{:S(2)}) collective-permute-start(bf16[24,2048]{1,0:T(8,128)(2,1)S(1)} %get-tuple-element.91), channel_id=1, source_target_pairs={{0,8},{4,12},{8,0},{12,4},{16,24},{20,28},{24,16},{28,20},{1,9},{5... | collective-permute-start | bytes 294920 | tf_op jit(solution)/shard_map/ppermute | solution.py:558
  60.3 1.4 %collective-permute-done.24.refs_1_ = bf16[24,2048]{1,0:T(8,128)(2,1)S(1)} collective-permute-done((bf16[24,2048]{1,0:T(8,128)(2,1)S(1)}, bf16[24,2048]{1,0:T(8,128)(2,1)S(1)}, u32[]{:S(2)}, u32[]{:S(2)}) %collective-permute-start.24) | collective-permute-done | bytes 98336 | tf_op jit(solution)/shard_map/ppermute | solution.py:558
  61.7 3.2 %collective-permute-done.25.refs_2_ = bf16[24,2048]{1,0:T(8,128)(2,1)S(1)} collective-permute-done((bf16[24,2048]{1,0:T(8,128)(2,1)S(1)}, bf16[24,2048]{1,0:T(8,128)(2,1)S(1)}, u32[]{:S(2)}, u32[]{:S(2)}) %collective-permute-start.25) | collective-permute-done | bytes 98336 | tf_op jit(solution)/shard_map/ppermute | solution.py:558
  65.8 1.3 %collective-permute-start.31 = (bf16[40,2048]{1,0:T(8,128)(2,1)S(1)}, bf16[40,2048]{1,0:T(8,128)(2,1)S(1)}, u32[]{:S(2)}, u32[]{:S(2)}) collective-permute-start(bf16[40,2048]{1,0:T(8,128)(2,1)S(1)} %get-tuple-element.104), channel_id=1, source_target_pairs={{0,16},{4,20},{8,24},{12,28},{16,0},{20,4},{24,8},{28,12},{1,17},{... | collective-permute-start | bytes 491528 | tf_op jit(solution)/shard_map/ppermute | solution.py:558
  67.1 1.5 %collective-permute-start.32 = (bf16[40,2048]{1,0:T(8,128)(2,1)S(1)}, bf16[40,2048]{1,0:T(8,128)(2,1)S(1)}, u32[]{:S(2)}, u32[]{:S(2)}) collective-permute-start(bf16[40,2048]{1,0:T(8,128)(2,1)S(1)} %get-tuple-element.105), channel_id=1, source_target_pairs={{0,24},{4,28},{8,16},{12,20},{16,8},{20,12},{24,0},{28,4},{1,25},{... | collective-permute-start | bytes 491528 | tf_op jit(solution)/shard_map/ppermute | solution.py:558
  69.1 2.1 %collective-permute-start.33 = (bf16[32,2048]{1,0:T(8,128)(2,1)S(1)}, bf16[32,2048]{1,0:T(8,128)(2,1)S(1)}, u32[]{:S(2)}, u32[]{:S(2)}) collective-permute-start(bf16[32,2048]{1,0:T(8,128)(2,1)S(1)} %get-tuple-element.107), channel_id=1, source_target_pairs={{0,1},{1,0},{2,3},{3,2},{4,5},{5,4},{6,7},{7,6},{8,9},{9,8},{10,11... | collective-permute-start | bytes 393224 | tf_op jit(solution)/shard_map/ppermute | solution.py:558
  72.1 3.5 %collective-permute-done.31.refs_1_.refs_2_ = bf16[40,2048]{1,0:T(8,128)(2,1)S(1)} collective-permute-done((bf16[40,2048]{1,0:T(8,128)(2,1)S(1)}, bf16[40,2048]{1,0:T(8,128)(2,1)S(1)}, u32[]{:S(2)}, u32[]{:S(2)}) %collective-permute-start.31) | collective-permute-done | bytes 163872 | tf_op jit(solution)/shard_map/ppermute | solution.py:558
  77.2 1.5 %collective-permute-start.39 = (bf16[32,2048]{1,0:T(8,128)(2,1)S(1)}, bf16[32,2048]{1,0:T(8,128)(2,1)S(1)}, u32[]{:S(2)}, u32[]{:S(2)}) collective-permute-start(bf16[32,2048]{1,0:T(8,128)(2,1)S(1)} %add_low.1.own_ref), channel_id=1, source_target_pairs={{0,2},{1,3},{2,0},{3,1},{4,6},{5,7},{6,4},{7,5},{8,10},{9,11},{10,... | collective-permute-start | bytes 393224 | tf_op jit(solution)/shard_map/ppermute | solution.py:558
  78.8 2.1 %collective-permute-start.35 = (bf16[8,2048]{1,0:T(8,128)(2,1)S(1)}, bf16[8,2048]{1,0:T(8,128)(2,1)S(1)}, u32[]{:S(2)}, u32[]{:S(2)}) collective-permute-start(bf16[8,2048]{1,0:T(8,128)(2,1)S(1)} %get-tuple-element.108), channel_id=1, source_target_pairs={{0,1},{1,0},{2,3},{3,2},{4,5},{5,4},{6,7},{7,6},{8,9},{9,8},{10,11... | collective-permute-start | bytes 98312 | tf_op jit(solution)/shard_map/ppermute | solution.py:558
  80.9 1.3 %collective-permute-start.36 = (bf16[8,2048]{1,0:T(8,128)(2,1)S(1)}, bf16[8,2048]{1,0:T(8,128)(2,1)S(1)}, u32[]{:S(2)}, u32[]{:S(2)}) collective-permute-start(bf16[8,2048]{1,0:T(8,128)(2,1)S(1)} %get-tuple-element.109), channel_id=1, source_target_pairs={{0,2},{1,3},{2,0},{3,1},{4,6},{5,7},{6,4},{7,5},{8,10},{9,11},{10,... | collective-permute-start | bytes 98312 | tf_op jit(solution)/shard_map/ppermute | solution.py:558
  83.6 8.8 %collective-permute-done.36.refs_9_.refs_2_ = bf16[8,2048]{1,0:T(8,128)(2,1)S(1)} collective-permute-done((bf16[8,2048]{1,0:T(8,128)(2,1)S(1)}, bf16[8,2048]{1,0:T(8,128)(2,1)S(1)}, u32[]{:S(2)}, u32[]{:S(2)}) %collective-permute-start.36) | collective-permute-done | bytes 32800 | tf_op jit(solution)/shard_map/ppermute | solution.py:558
  92.6 1.8 %collective-permute-start.42 = (bf16[8,2176]{1,0:T(8,128)(2,1)S(1)}, bf16[8,2176]{1,0:T(8,128)(2,1)S(1)}, u32[]{:S(2)}, u32[]{:S(2)}) collective-permute-start(bf16[8,2176]{1,0:T(8,128)(2,1)S(1)} %norm_grad.1.refs_4_), channel_id=1, source_target_pairs={{0,3},{1,2},{2,1},{3,0},{4,7},{5,6},{6,5},{7,4},{8,11},{9,10},{10,... | collective-permute-start | bytes 104456 | tf_op jit(solution)/shard_map/ppermute | solution.py:558
  95.0 2.0 %collective-permute-start.40 = (bf16[8,2176]{1,0:T(8,128)(2,1)S(1)}, bf16[8,2176]{1,0:T(8,128)(2,1)S(1)}, u32[]{:S(2)}, u32[]{:S(2)}) collective-permute-start(bf16[8,2176]{1,0:T(8,128)(2,1)S(1)} %norm_grad.1.refs_4_), channel_id=1, source_target_pairs={{0,1},{1,0},{2,3},{3,2},{4,5},{5,4},{6,7},{7,6},{8,9},{9,8},{10,11... | collective-permute-start | bytes 104456 | tf_op jit(solution)/shard_map/ppermute | solution.py:558
  100.2 1.3 %collective-permute-start.43 = (bf16[32,2048]{1,0:T(8,128)(2,1)S(1)}, bf16[32,2048]{1,0:T(8,128)(2,1)S(1)}, u32[]{:S(2)}, u32[]{:S(2)}) collective-permute-start(bf16[32,2048]{1,0:T(8,128)(2,1)S(1)} %finish.3.refs_2_), channel_id=1, source_target_pairs={{0,1},{1,0},{2,3},{3,2},{4,5},{5,4},{6,7},{7,6},{8,9},{9,8},{10,11... | collective-permute-start | bytes 393224 | tf_op jit(solution)/shard_map/ppermute | solution.py:558
  101.5 3.0 %merge_grad.1 = f32[288,128]{1,0:T(8,128)} custom-call(f32[4,288]{1,0:T(4,128)S(1)} %copy-done.15, bf16[32,1152]{1,0:T(8,128)(2,1)S(1)} %get-tuple-element.115.refs_1_, bf16[32,2176]{1,0:T(8,128)(2,1)S(1)} %stack.1.refs_6_.refs_0_.refs_2_, bf16[1152,2048]{1,0:T(8,128)(2,1)S(1)} %bitcast.10, bf16[8,2176]{1,0:T(8,128)(2,1)S(1)} %norm_grad.1.refs_4_, ...), custom_call_target="tpu_custom_call" | custom-call | bytes 12000000 | tf_op jit(solution)/shard_map/merge_grad/pallas_call | solution.py:512
  (121 shorter events, 30.7 us)
Async XLA Ops:
  2.6 10.0 %collective-permute-start.3 = (bf16[592,128]{1,0:T(8,128)(2,1)}, bf16[592,128]{1,0:T(8,128)(2,1)S(1)}, u32[]{:S(2)}, u32[]{:S(2)}) collective-permute-start(bf16[592,128]{1,0:T(8,128)(2,1)} %pack.1), channel_id=1, source_target_pairs={{0,24},{4,28},{8,16},{12,20},{16,8},{20,12},{24,0},{28,4},{1,25},{... | collective-permute-start | bytes 454664 | tf_op jit(solution)/shard_map/ppermute | solution.py:558
  6.5 7.4 %collective-permute-start.2 = (bf16[592,128]{1,0:T(8,128)(2,1)}, bf16[592,128]{1,0:T(8,128)(2,1)S(1)}, u32[]{:S(2)}, u32[]{:S(2)}) collective-permute-start(bf16[592,128]{1,0:T(8,128)(2,1)} %pack.1), channel_id=1, source_target_pairs={{0,16},{4,20},{8,24},{12,28},{16,0},{20,4},{24,8},{28,12},{1,17},{... | collective-permute-start | bytes 454664 | tf_op jit(solution)/shard_map/ppermute | solution.py:558
  7.0 7.2 %collective-permute-start.1 = (bf16[592,128]{1,0:T(8,128)(2,1)}, bf16[592,128]{1,0:T(8,128)(2,1)S(1)}, u32[]{:S(2)}, u32[]{:S(2)}) collective-permute-start(bf16[592,128]{1,0:T(8,128)(2,1)} %pack.1), channel_id=1, source_target_pairs={{0,8},{4,12},{8,0},{12,4},{16,24},{20,28},{24,16},{28,20},{1,9},{5... | collective-permute-start | bytes 454664 | tf_op jit(solution)/shard_map/ppermute | solution.py:558
  7.2 10.5 %collective-permute-start = (bf16[592,128]{1,0:T(8,128)(2,1)}, bf16[592,128]{1,0:T(8,128)(2,1)S(1)}, u32[]{:S(2)}, u32[]{:S(2)}) collective-permute-start(bf16[592,128]{1,0:T(8,128)(2,1)} %pack.1), channel_id=1, source_target_pairs={{0,4},{4,0},{8,12},{12,8},{16,20},{20,16},{24,28},{28,24},{1,5},{5... | collective-permute-start | bytes 454664 | tf_op jit(solution)/shard_map/ppermute | solution.py:558
  14.2 7.8 %collective-permute-start.7 = (bf16[48,2048]{1,0:T(8,128)(2,1)S(1)}, bf16[48,2048]{1,0:T(8,128)(2,1)S(1)}, u32[]{:S(2)}, u32[]{:S(2)}) collective-permute-start(bf16[48,2048]{1,0:T(8,128)(2,1)S(1)} %get-tuple-element.73), channel_id=1, source_target_pairs={{0,8},{4,12},{8,0},{12,4},{16,24},{20,28},{24,16},{28,20},{1,9},{5... | collective-permute-start | bytes 589832 | tf_op jit(solution)/shard_map/ppermute | solution.py:558
  15.7 11.7 %collective-permute-start.8 = (bf16[48,2048]{1,0:T(8,128)(2,1)S(1)}, bf16[48,2048]{1,0:T(8,128)(2,1)S(1)}, u32[]{:S(2)}, u32[]{:S(2)}) collective-permute-start(bf16[48,2048]{1,0:T(8,128)(2,1)S(1)} %get-tuple-element.74), channel_id=1, source_target_pairs={{0,16},{4,20},{8,24},{12,28},{16,0},{20,4},{24,8},{28,12},{1,17},{... | collective-permute-start | bytes 589832 | tf_op jit(solution)/shard_map/ppermute | solution.py:558
  16.6 10.9 %collective-permute-start.9 = (bf16[48,2048]{1,0:T(8,128)(2,1)S(1)}, bf16[48,2048]{1,0:T(8,128)(2,1)S(1)}, u32[]{:S(2)}, u32[]{:S(2)}) collective-permute-start(bf16[48,2048]{1,0:T(8,128)(2,1)S(1)} %get-tuple-element.75), channel_id=1, source_target_pairs={{0,24},{4,28},{8,16},{12,20},{16,8},{20,12},{24,0},{28,4},{1,25},{... | collective-permute-start | bytes 589832 | tf_op jit(solution)/shard_map/ppermute | solution.py:558
  24.6 5.6 %collective-permute-start.11 = (bf16[8,2432]{1,0:T(8,128)(2,1)S(1)}, bf16[8,2432]{1,0:T(8,128)(2,1)S(1)}, u32[]{:S(2)}, u32[]{:S(2)}) collective-permute-start(bf16[8,2432]{1,0:T(8,128)(2,1)S(1)} %get-tuple-element.79), channel_id=1, source_target_pairs={{0,2},{1,3},{2,0},{3,1},{4,6},{5,7},{6,4},{7,5},{8,10},{9,11},{10,... | collective-permute-start | bytes 116744 | tf_op jit(solution)/shard_map/ppermute | solution.py:558
  27.2 5.8 %collective-permute-start.12 = (bf16[8,2432]{1,0:T(8,128)(2,1)S(1)}, bf16[8,2432]{1,0:T(8,128)(2,1)S(1)}, u32[]{:S(2)}, u32[]{:S(2)}) collective-permute-start(bf16[8,2432]{1,0:T(8,128)(2,1)S(1)} %get-tuple-element.80), channel_id=1, source_target_pairs={{0,3},{1,2},{2,1},{3,0},{4,7},{5,6},{6,5},{7,4},{8,11},{9,10},{10,... | collective-permute-start | bytes 116744 | tf_op jit(solution)/shard_map/ppermute | solution.py:558
  33.1 5.9 %collective-permute-start.15 = (bf16[8,2176]{1,0:T(8,128)(2,1)S(1)}, bf16[8,2176]{1,0:T(8,128)(2,1)S(1)}, u32[]{:S(2)}, u32[]{:S(2)}) collective-permute-start(bf16[8,2176]{1,0:T(8,128)(2,1)S(1)} %get-tuple-element.85.refs_0_.own_ref), channel_id=1, source_target_pairs={{0,3},{1,2},{2,1},{3,0},{4,7},{5,6},{6,5},{7,4},{8,11},{9,10},{10,... | collective-permute-start | bytes 104456 | tf_op jit(solution)/shard_map/ppermute | solution.py:558
  33.9 5.7 %collective-permute-start.14 = (bf16[8,2176]{1,0:T(8,128)(2,1)S(1)}, bf16[8,2176]{1,0:T(8,128)(2,1)S(1)}, u32[]{:S(2)}, u32[]{:S(2)}) collective-permute-start(bf16[8,2176]{1,0:T(8,128)(2,1)S(1)} %get-tuple-element.85.refs_0_.own_ref), channel_id=1, source_target_pairs={{0,2},{1,3},{2,0},{3,1},{4,6},{5,7},{6,4},{7,5},{8,10},{9,11},{10,... | collective-permute-start | bytes 104456 | tf_op jit(solution)/shard_map/ppermute | solution.py:558
  33.9 5.7 %collective-permute-start.13 = (bf16[8,2176]{1,0:T(8,128)(2,1)S(1)}, bf16[8,2176]{1,0:T(8,128)(2,1)S(1)}, u32[]{:S(2)}, u32[]{:S(2)}) collective-permute-start(bf16[8,2176]{1,0:T(8,128)(2,1)S(1)} %get-tuple-element.85.refs_0_.own_ref), channel_id=1, source_target_pairs={{0,1},{1,0},{2,3},{3,2},{4,5},{5,4},{6,7},{7,6},{8,9},{9,8},{10,11... | collective-permute-start | bytes 104456 | tf_op jit(solution)/shard_map/ppermute | solution.py:558
  39.7 7.5 %collective-permute-start.20 = (bf16[32,2176]{1,0:T(8,128)(2,1)S(1)}, bf16[32,2176]{1,0:T(8,128)(2,1)S(1)}, u32[]{:S(2)}, u32[]{:S(2)}) collective-permute-start(bf16[32,2176]{1,0:T(8,128)(2,1)S(1)} %stack.1.refs_6_.refs_0_.refs_2_), channel_id=1, source_target_pairs={{0,24},{4,28},{8,16},{12,20},{16,8},{20,12},{24,0},{28,4},{1,25},{... | collective-permute-start | bytes 417800 | tf_op jit(solution)/shard_map/ppermute | solution.py:558
  41.6 8.1 %collective-permute-start.19 = (bf16[32,2176]{1,0:T(8,128)(2,1)S(1)}, bf16[32,2176]{1,0:T(8,128)(2,1)S(1)}, u32[]{:S(2)}, u32[]{:S(2)}) collective-permute-start(bf16[32,2176]{1,0:T(8,128)(2,1)S(1)} %stack.1.refs_6_.refs_0_.refs_2_), channel_id=1, source_target_pairs={{0,16},{4,20},{8,24},{12,28},{16,0},{20,4},{24,8},{28,12},{1,17},{... | collective-permute-start | bytes 417800 | tf_op jit(solution)/shard_map/ppermute | solution.py:558
  42.7 7.1 %collective-permute-start.18 = (bf16[32,2176]{1,0:T(8,128)(2,1)S(1)}, bf16[32,2176]{1,0:T(8,128)(2,1)S(1)}, u32[]{:S(2)}, u32[]{:S(2)}) collective-permute-start(bf16[32,2176]{1,0:T(8,128)(2,1)S(1)} %stack.1.refs_6_.refs_0_.refs_2_), channel_id=1, source_target_pairs={{0,8},{4,12},{8,0},{12,4},{16,24},{20,28},{24,16},{28,20},{1,9},{5... | collective-permute-start | bytes 417800 | tf_op jit(solution)/shard_map/ppermute | solution.py:558
  43.9 6.4 %collective-permute-start.17 = (bf16[32,2176]{1,0:T(8,128)(2,1)S(1)}, bf16[32,2176]{1,0:T(8,128)(2,1)S(1)}, u32[]{:S(2)}, u32[]{:S(2)}) collective-permute-start(bf16[32,2176]{1,0:T(8,128)(2,1)S(1)} %stack.1.refs_6_.refs_0_.refs_2_), channel_id=1, source_target_pairs={{0,4},{4,0},{8,12},{12,8},{16,20},{20,16},{24,28},{28,24},{1,5},{5... | collective-permute-start | bytes 417800 | tf_op jit(solution)/shard_map/ppermute | solution.py:558
  56.7 5.0 %collective-permute-start.24 = (bf16[24,2048]{1,0:T(8,128)(2,1)S(1)}, bf16[24,2048]{1,0:T(8,128)(2,1)S(1)}, u32[]{:S(2)}, u32[]{:S(2)}) collective-permute-start(bf16[24,2048]{1,0:T(8,128)(2,1)S(1)} %get-tuple-element.91), channel_id=1, source_target_pairs={{0,8},{4,12},{8,0},{12,4},{16,24},{20,28},{24,16},{28,20},{1,9},{5... | collective-permute-start | bytes 294920 | tf_op jit(solution)/shard_map/ppermute | solution.py:558
  58.1 6.8 %collective-permute-start.25 = (bf16[24,2048]{1,0:T(8,128)(2,1)S(1)}, bf16[24,2048]{1,0:T(8,128)(2,1)S(1)}, u32[]{:S(2)}, u32[]{:S(2)}) collective-permute-start(bf16[24,2048]{1,0:T(8,128)(2,1)S(1)} %get-tuple-element.92), channel_id=1, source_target_pairs={{0,16},{4,20},{8,24},{12,28},{16,0},{20,4},{24,8},{28,12},{1,17},{... | collective-permute-start | bytes 294920 | tf_op jit(solution)/shard_map/ppermute | solution.py:558
  58.9 6.0 %collective-permute-start.26 = (bf16[24,2048]{1,0:T(8,128)(2,1)S(1)}, bf16[24,2048]{1,0:T(8,128)(2,1)S(1)}, u32[]{:S(2)}, u32[]{:S(2)}) collective-permute-start(bf16[24,2048]{1,0:T(8,128)(2,1)S(1)} %get-tuple-element.93), channel_id=1, source_target_pairs={{0,24},{4,28},{8,16},{12,20},{16,8},{20,12},{24,0},{28,4},{1,25},{... | collective-permute-start | bytes 294920 | tf_op jit(solution)/shard_map/ppermute | solution.py:558
  65.0 7.1 %collective-permute-start.30 = (bf16[40,2048]{1,0:T(8,128)(2,1)S(1)}, bf16[40,2048]{1,0:T(8,128)(2,1)S(1)}, u32[]{:S(2)}, u32[]{:S(2)}) collective-permute-start(bf16[40,2048]{1,0:T(8,128)(2,1)S(1)} %get-tuple-element.103), channel_id=1, source_target_pairs={{0,8},{4,12},{8,0},{12,4},{16,24},{20,28},{24,16},{28,20},{1,9},{5... | collective-permute-start | bytes 491528 | tf_op jit(solution)/shard_map/ppermute | solution.py:558
  65.8 9.8 %collective-permute-start.31 = (bf16[40,2048]{1,0:T(8,128)(2,1)S(1)}, bf16[40,2048]{1,0:T(8,128)(2,1)S(1)}, u32[]{:S(2)}, u32[]{:S(2)}) collective-permute-start(bf16[40,2048]{1,0:T(8,128)(2,1)S(1)} %get-tuple-element.104), channel_id=1, source_target_pairs={{0,16},{4,20},{8,24},{12,28},{16,0},{20,4},{24,8},{28,12},{1,17},{... | collective-permute-start | bytes 491528 | tf_op jit(solution)/shard_map/ppermute | solution.py:558
  67.1 8.5 %collective-permute-start.32 = (bf16[40,2048]{1,0:T(8,128)(2,1)S(1)}, bf16[40,2048]{1,0:T(8,128)(2,1)S(1)}, u32[]{:S(2)}, u32[]{:S(2)}) collective-permute-start(bf16[40,2048]{1,0:T(8,128)(2,1)S(1)} %get-tuple-element.105), channel_id=1, source_target_pairs={{0,24},{4,28},{8,16},{12,20},{16,8},{20,12},{24,0},{28,4},{1,25},{... | collective-permute-start | bytes 491528 | tf_op jit(solution)/shard_map/ppermute | solution.py:558
  69.1 6.5 %collective-permute-start.33 = (bf16[32,2048]{1,0:T(8,128)(2,1)S(1)}, bf16[32,2048]{1,0:T(8,128)(2,1)S(1)}, u32[]{:S(2)}, u32[]{:S(2)}) collective-permute-start(bf16[32,2048]{1,0:T(8,128)(2,1)S(1)} %get-tuple-element.107), channel_id=1, source_target_pairs={{0,1},{1,0},{2,3},{3,2},{4,5},{5,4},{6,7},{7,6},{8,9},{9,8},{10,11... | collective-permute-start | bytes 393224 | tf_op jit(solution)/shard_map/ppermute | solution.py:558
  71.1 6.1 %collective-permute-start.29 = (bf16[32,2048]{1,0:T(8,128)(2,1)S(1)}, bf16[32,2048]{1,0:T(8,128)(2,1)S(1)}, u32[]{:S(2)}, u32[]{:S(2)}) collective-permute-start(bf16[32,2048]{1,0:T(8,128)(2,1)S(1)} %get-tuple-element.102.refs_4_), channel_id=1, source_target_pairs={{0,1},{1,0},{2,3},{3,2},{4,5},{5,4},{6,7},{7,6},{8,9},{9,8},{10,11... | collective-permute-start | bytes 393224 | tf_op jit(solution)/shard_map/ppermute | solution.py:558
  75.6 21.4 %collective-permute-start.34 = (bf16[32,2048]{1,0:T(8,128)(2,1)S(1)}, bf16[32,2048]{1,0:T(8,128)(2,1)S(1)}, u32[]{:S(2)}, u32[]{:S(2)}) collective-permute-start(bf16[32,2048]{1,0:T(8,128)(2,1)S(1)} %add_high.1.own_ref), channel_id=1, source_target_pairs={{0,2},{1,3},{2,0},{3,1},{4,6},{5,7},{6,4},{7,5},{8,10},{9,11},{10,... | collective-permute-start | bytes 393224 | tf_op jit(solution)/shard_map/ppermute | solution.py:558
  77.2 22.5 %collective-permute-start.39 = (bf16[32,2048]{1,0:T(8,128)(2,1)S(1)}, bf16[32,2048]{1,0:T(8,128)(2,1)S(1)}, u32[]{:S(2)}, u32[]{:S(2)}) collective-permute-start(bf16[32,2048]{1,0:T(8,128)(2,1)S(1)} %add_low.1.own_ref), channel_id=1, source_target_pairs={{0,2},{1,3},{2,0},{3,1},{4,6},{5,7},{6,4},{7,5},{8,10},{9,11},{10,... | collective-permute-start | bytes 393224 | tf_op jit(solution)/shard_map/ppermute | solution.py:558
  80.9 11.5 %collective-permute-start.36 = (bf16[8,2048]{1,0:T(8,128)(2,1)S(1)}, bf16[8,2048]{1,0:T(8,128)(2,1)S(1)}, u32[]{:S(2)}, u32[]{:S(2)}) collective-permute-start(bf16[8,2048]{1,0:T(8,128)(2,1)S(1)} %get-tuple-element.109), channel_id=1, source_target_pairs={{0,2},{1,3},{2,0},{3,1},{4,6},{5,7},{6,4},{7,5},{8,10},{9,11},{10,... | collective-permute-start | bytes 98312 | tf_op jit(solution)/shard_map/ppermute | solution.py:558
  82.1 10.3 %collective-permute-start.37 = (bf16[8,2048]{1,0:T(8,128)(2,1)S(1)}, bf16[8,2048]{1,0:T(8,128)(2,1)S(1)}, u32[]{:S(2)}, u32[]{:S(2)}) collective-permute-start(bf16[8,2048]{1,0:T(8,128)(2,1)S(1)} %get-tuple-element.110), channel_id=1, source_target_pairs={{0,3},{1,2},{2,1},{3,0},{4,7},{5,6},{6,5},{7,4},{8,11},{9,10},{10,... | collective-permute-start | bytes 98312 | tf_op jit(solution)/shard_map/ppermute | solution.py:558
  92.6 5.8 %collective-permute-start.42 = (bf16[8,2176]{1,0:T(8,128)(2,1)S(1)}, bf16[8,2176]{1,0:T(8,128)(2,1)S(1)}, u32[]{:S(2)}, u32[]{:S(2)}) collective-permute-start(bf16[8,2176]{1,0:T(8,128)(2,1)S(1)} %norm_grad.1.refs_4_), channel_id=1, source_target_pairs={{0,3},{1,2},{2,1},{3,0},{4,7},{5,6},{6,5},{7,4},{8,11},{9,10},{10,... | collective-permute-start | bytes 104456 | tf_op jit(solution)/shard_map/ppermute | solution.py:558
  94.5 5.0 %collective-permute-start.41 = (bf16[8,2176]{1,0:T(8,128)(2,1)S(1)}, bf16[8,2176]{1,0:T(8,128)(2,1)S(1)}, u32[]{:S(2)}, u32[]{:S(2)}) collective-permute-start(bf16[8,2176]{1,0:T(8,128)(2,1)S(1)} %norm_grad.1.refs_4_), channel_id=1, source_target_pairs={{0,2},{1,3},{2,0},{3,1},{4,6},{5,7},{6,4},{7,5},{8,10},{9,11},{10,... | collective-permute-start | bytes 104456 | tf_op jit(solution)/shard_map/ppermute | solution.py:558
  97.5 7.0 %collective-permute-start.38 = (bf16[32,2048]{1,0:T(8,128)(2,1)S(1)}, bf16[32,2048]{1,0:T(8,128)(2,1)S(1)}, u32[]{:S(2)}, u32[]{:S(2)}) collective-permute-start(bf16[32,2048]{1,0:T(8,128)(2,1)S(1)} %finish.2.refs_0_), channel_id=1, source_target_pairs={{0,1},{1,0},{2,3},{3,2},{4,5},{5,4},{6,7},{7,6},{8,9},{9,8},{10,11... | collective-permute-start | bytes 393224 | tf_op jit(solution)/shard_map/ppermute | solution.py:558
  100.2 5.1 %collective-permute-start.43 = (bf16[32,2048]{1,0:T(8,128)(2,1)S(1)}, bf16[32,2048]{1,0:T(8,128)(2,1)S(1)}, u32[]{:S(2)}, u32[]{:S(2)}) collective-permute-start(bf16[32,2048]{1,0:T(8,128)(2,1)S(1)} %finish.3.refs_2_), channel_id=1, source_target_pairs={{0,1},{1,0},{2,3},{3,2},{4,5},{5,4},{6,7},{7,6},{8,9},{9,8},{10,11... | collective-permute-start | bytes 393224 | tf_op jit(solution)/shard_map/ppermute | solution.py:558
  (31 other events, 311.0 us)

commit v2 on v1

--- a/solution.py
+++ b/solution.py
@@ -708,22 +708,22 @@
         arrived_high = swap(sent_high, "expert", step)
         arrived_low = swap(sent_low, "expert", step)
     step *= 2
-    chips = len(grads) - 1
-
-    def add(own_part, arrived, name):
+
+    def add(own_part, arrived, gate, name):
         return run(
-            add_kernel, shape((part, width)), own_part, arrived, *grads[1:],
-            far=range(2, 2 + chips), cost=0.3, name=name,
+            add_kernel, shape((part, width)), own_part, arrived, *gate,
+            far=range(2, 2 + len(gate)), cost=0.3, name=name,
         )
 
-    sums = [add(low, arrived_low, "add_low"), add(high, arrived_high, "add_high")]
-    others = [swap(value, "expert", step) for value in sums][::-1]
+    sum_high = add(high, arrived_high, grads[1:], "add_high")
     cot_rows, *grads = run(
         functools.partial(chip_sum_kernel, count=blocks // 2),
         [shape((row_share, width))] * (share + 1), *grads, first_sent, far=(blocks // 2,), cost=0.2,
         name="chip_sum",
     )
     grads = trade(grads, "expert")
+    sums = [add(low, arrived_low, grads[1:], "add_low"), sum_high]
+    others = [swap(value, "expert", step) for value in sums][::-1]
     vision_grad = run(
         functools.partial(norm_grad_kernel, features=share * features),
         shape((row_share, width + 128)),

time: 107 us -> 104 us (0.972)
  waiting for transfers between devices: 37.5 us -> 34 us
  starting transfers between devices: 44.2 us -> 45.6 us
    ppermute x44, waiting for transfers between devices: 37.5 us -> 34 us  [swap(): return lax.ppermute(value, axis, [(i, i ^ step) for i in range(count)])]
    ppermute x44, starting transfers between devices: 44.2 us -> 45.6 us  [swap(): return lax.ppermute(value, axis, [(i, i ^ step) for i in range(count)])]
  transfers between devices with their start and end apart: 44 -> 44, of which waited for: 25 -> 23; matrix products, arithmetic and copies ran while one was open for 0% -> 0% of each run, Pallas kernels for 11% -> 11%
where the time goes in v2:
time: 104 us
  starting transfers between devices  45.6 us (44%)
  waiting for transfers between devices  34 us (33%)
  Pallas kernels  19.2 us (18%)
  local copies, waits for them, and re-layouts  4.22 us (4%)
    ppermute x44, starting transfers between devices, swap(): return lax.ppermute(value, axis, [(i, i ^ step) for i in range(count)])  45.6 us
    ppermute x44, waiting for transfers between devices, swap(): return lax.ppermute(value, axis, [(i, i ^ step) for i in range(count)])  34 us
    pallas_call x23, Pallas kernels, run(): pl.pallas_call(kernel, out_shape=outs, in_specs=specs, out_specs=jax.tree...  19.2 us
    unnamed x38, local copies, waits for them, and re-layouts  4.22 us
  transfers between devices with their start and end apart: 44, of which 23 were waited for; matrix products, arithmetic and copies ran while one was open for 0% of the time, Pallas kernels for 11%

profile of v2, /device:TPU:0, one launch (start us, length us, event | category | flops | bytes accessed | tf_op | source)
XLA Modules:
  0.0 104.1 jit_solution(14538016179554282707)
XLA Ops:
  0.7 1.8 %pack.1 = bf16[592,128]{1,0:T(8,128)(2,1)} custom-call(bf16[288,128]{1,0:T(8,128)(2,1)} %bitcast.11, bf16[288,128]{1,0:T(8,128)(2,1)} %bitcast.13, s32[1,32]{1,0:T(1,128)} %bitcast.22, s32[1,32]{1,0:T(1,128)} %bitcast.24, s32[8,128]{1,0:T(8,128)} %bitcast.18), custom_call_target="tpu_custom_call" | custom-call | bytes 3000000 | tf_op jit(solution)/shard_map/pack/pallas_call | solution.py:512
  2.6 4.0 %collective-permute-start.3 = (bf16[592,128]{1,0:T(8,128)(2,1)}, bf16[592,128]{1,0:T(8,128)(2,1)S(1)}, u32[]{:S(2)}, u32[]{:S(2)}) collective-permute-start(bf16[592,128]{1,0:T(8,128)(2,1)} %pack.1), channel_id=1, source_target_pairs={{0,24},{4,28},{8,16},{12,20},{16,8},{20,12},{24,0},{28,4},{1,25},{... | collective-permute-start | bytes 454664 | tf_op jit(solution)/shard_map/ppermute | solution.py:558
  12.6 1.4 %collective-permute-done.2.refs_1_ = bf16[592,128]{1,0:T(8,128)(2,1)S(1)} collective-permute-done((bf16[592,128]{1,0:T(8,128)(2,1)}, bf16[592,128]{1,0:T(8,128)(2,1)S(1)}, u32[]{:S(2)}, u32[]{:S(2)}) %collective-permute-start.2) | collective-permute-done | bytes 151584 | tf_op jit(solution)/shard_map/ppermute | solution.py:558
  14.2 1.5 %collective-permute-start.7 = (bf16[48,2048]{1,0:T(8,128)(2,1)S(1)}, bf16[48,2048]{1,0:T(8,128)(2,1)S(1)}, u32[]{:S(2)}, u32[]{:S(2)}) collective-permute-start(bf16[48,2048]{1,0:T(8,128)(2,1)S(1)} %get-tuple-element.73), channel_id=1, source_target_pairs={{0,8},{4,12},{8,0},{12,4},{16,24},{20,28},{24,16},{28,20},{1,9},{5... | collective-permute-start | bytes 589832 | tf_op jit(solution)/shard_map/ppermute | solution.py:558
  19.4 2.6 %attend.1 = (bf16[32,1152]{1,0:T(8,128)(2,1)S(1)}, bf16[128,128]{1,0:T(8,128)(2,1)S(1)}, bf16[48,1152]{1,0:T(8,128)(2,1)S(1)}, f32[32,128]{1,0:T(8,128)S(1)}) custom-call(bf16[4,72,128]{2,1,0:T(8,128)(2,1)S(1)} %copy-done.12, f32[4,288]{1,0:T(4,128)S(1)} %copy-done.15, bf16[288,128]{1,0:T(8,128)(2,1)S(1)} %bitcast.12, bf16[288,128]{1,0:T(8,128)(2,1)S(1)} %bitcast.14, ...), custom_call_target="tpu_custom_call" | custom-call | bytes 9000000 | tf_op jit(solution)/shard_map/attend/pallas_call | solution.py:512
  23.0 1.6 %collective-permute-start.10 = (bf16[8,2432]{1,0:T(8,128)(2,1)S(1)}, bf16[8,2432]{1,0:T(8,128)(2,1)S(1)}, u32[]{:S(2)}, u32[]{:S(2)}) collective-permute-start(bf16[8,2432]{1,0:T(8,128)(2,1)S(1)} %get-tuple-element.78), channel_id=1, source_target_pairs={{0,1},{1,0},{2,3},{3,2},{4,5},{5,4},{6,7},{7,6},{8,9},{9,8},{10,11... | collective-permute-start | bytes 116744 | tf_op jit(solution)/shard_map/ppermute | solution.py:558
  24.6 2.6 %collective-permute-start.11 = (bf16[8,2432]{1,0:T(8,128)(2,1)S(1)}, bf16[8,2432]{1,0:T(8,128)(2,1)S(1)}, u32[]{:S(2)}, u32[]{:S(2)}) collective-permute-start(bf16[8,2432]{1,0:T(8,128)(2,1)S(1)} %get-tuple-element.79), channel_id=1, source_target_pairs={{0,2},{1,3},{2,0},{3,1},{4,6},{5,7},{6,4},{7,5},{8,10},{9,11},{10,... | collective-permute-start | bytes 116744 | tf_op jit(solution)/shard_map/ppermute | solution.py:558
  27.4 2.8 %collective-permute-done.11.refs_4_.refs_2_ = bf16[8,2432]{1,0:T(8,128)(2,1)S(1)} collective-permute-done((bf16[8,2432]{1,0:T(8,128)(2,1)S(1)}, bf16[8,2432]{1,0:T(8,128)(2,1)S(1)}, u32[]{:S(2)}, u32[]{:S(2)}) %collective-permute-start.11) | collective-permute-done | bytes 38944 | tf_op jit(solution)/shard_map/ppermute | solution.py:558
  30.2 2.8 %collective-permute-done.12.refs_5_.refs_3_ = bf16[8,2432]{1,0:T(8,128)(2,1)S(1)} collective-permute-done((bf16[8,2432]{1,0:T(8,128)(2,1)S(1)}, bf16[8,2432]{1,0:T(8,128)(2,1)S(1)}, u32[]{:S(2)}, u32[]{:S(2)}) %collective-permute-start.12) | collective-permute-done | bytes 38944 | tf_op jit(solution)/shard_map/ppermute | solution.py:558
  33.9 3.7 %collective-permute-start.13 = (bf16[8,2176]{1,0:T(8,128)(2,1)S(1)}, bf16[8,2176]{1,0:T(8,128)(2,1)S(1)}, u32[]{:S(2)}, u32[]{:S(2)}) collective-permute-start(bf16[8,2176]{1,0:T(8,128)(2,1)S(1)} %get-tuple-element.85.refs_0_.own_ref), channel_id=1, source_target_pairs={{0,1},{1,0},{2,3},{3,2},{4,5},{5,4},{6,7},{7,6},{8,9},{9,8},{10,11... | collective-permute-start | bytes 104456 | tf_op jit(solution)/shard_map/ppermute | solution.py:558
  37.6 1.4 %collective-permute-done.15.refs_6_.refs_3_ = bf16[8,2176]{1,0:T(8,128)(2,1)S(1)} collective-permute-done((bf16[8,2176]{1,0:T(8,128)(2,1)S(1)}, bf16[8,2176]{1,0:T(8,128)(2,1)S(1)}, u32[]{:S(2)}, u32[]{:S(2)}) %collective-permute-start.15) | collective-permute-done | bytes 34848 | tf_op jit(solution)/shard_map/ppermute | solution.py:558
  39.7 1.9 %collective-permute-start.20 = (bf16[32,2176]{1,0:T(8,128)(2,1)S(1)}, bf16[32,2176]{1,0:T(8,128)(2,1)S(1)}, u32[]{:S(2)}, u32[]{:S(2)}) collective-permute-start(bf16[32,2176]{1,0:T(8,128)(2,1)S(1)} %stack.1.refs_6_.refs_0_.refs_2_), channel_id=1, source_target_pairs={{0,24},{4,28},{8,16},{12,20},{16,8},{20,12},{24,0},{28,4},{1,25},{... | collective-permute-start | bytes 417800 | tf_op jit(solution)/shard_map/ppermute | solution.py:558
  45.3 1.9 %collective-permute-done.20.refs_2_ = bf16[32,2176]{1,0:T(8,128)(2,1)S(1)} collective-permute-done((bf16[32,2176]{1,0:T(8,128)(2,1)S(1)}, bf16[32,2176]{1,0:T(8,128)(2,1)S(1)}, u32[]{:S(2)}, u32[]{:S(2)}) %collective-permute-start.20) | collective-permute-done | bytes 139296 | tf_op jit(solution)/shard_map/ppermute | solution.py:558
  47.2 2.5 %collective-permute-done.19.refs_1_ = bf16[32,2176]{1,0:T(8,128)(2,1)S(1)} collective-permute-done((bf16[32,2176]{1,0:T(8,128)(2,1)S(1)}, bf16[32,2176]{1,0:T(8,128)(2,1)S(1)}, u32[]{:S(2)}, u32[]{:S(2)}) %collective-permute-start.19) | collective-permute-done | bytes 139296 | tf_op jit(solution)/shard_map/ppermute | solution.py:558
  51.7 3.2 %forward.1 = (f32[96,768]{1,0:T(8,128)S(1)}, f32[96,768]{1,0:T(8,128)S(1)}, bf16[24,2048]{1,0:T(8,128)(2,1)S(1)}, bf16[24,2048]{1,0:T(8,128)(2,1)S(1)}, bf16[24,...) custom-call(bf16[96,256]{1,0:T(8,128)(2,1)S(1)} %get-tuple-element.71.refs_4_.refs_0_.slots_ref, ...), custom_call_target="tpu_custom_call" | custom-call | bytes 12000000 | tf_op jit(solution)/shard_map/forward/pallas_call | solution.py:512
  54.9 1.5 %backward.1 = (bf16[160,2048]{1,0:T(8,128)(2,1)S(1)}, bf16[160,2048]{1,0:T(8,128)(2,1)S(1)}) custom-call(bf16[96,256]{1,0:T(8,128)(2,1)S(1)} %get-tuple-element.71.refs_4_.refs_0_.slots_ref, f32[96,768]{1,0:T(8,128)S(1)} %get-tuple-element.94.grad_ref, f32[96,768]{1,0:T(8,128)S(1)} %get-tuple-element.95.gate_in, f32[96,768]{1,0:T(8,128)S(1)} %get-tuple-element.96.up_in, ...), custom_call_target="tpu_custom_call" | custom-call | bytes 12000000 | tf_op jit(solution)/shard_map/backward/pallas_call | solution.py:512
  56.7 1.4 %collective-permute-start.24 = (bf16[24,2048]{1,0:T(8,128)(2,1)S(1)}, bf16[24,2048]{1,0:T(8,128)(2,1)S(1)}, u32[]{:S(2)}, u32[]{:S(2)}) collective-permute-start(bf16[24,2048]{1,0:T(8,128)(2,1)S(1)} %get-tuple-element.91), channel_id=1, source_target_pairs={{0,8},{4,12},{8,0},{12,4},{16,24},{20,28},{24,16},{28,20},{1,9},{5... | collective-permute-start | bytes 294920 | tf_op jit(solution)/shard_map/ppermute | solution.py:558
  60.3 1.4 %collective-permute-done.24.refs_1_ = bf16[24,2048]{1,0:T(8,128)(2,1)S(1)} collective-permute-done((bf16[24,2048]{1,0:T(8,128)(2,1)S(1)}, bf16[24,2048]{1,0:T(8,128)(2,1)S(1)}, u32[]{:S(2)}, u32[]{:S(2)}) %collective-permute-start.24) | collective-permute-done | bytes 98336 | tf_op jit(solution)/shard_map/ppermute | solution.py:558
  61.7 3.2 %collective-permute-done.25.refs_2_ = bf16[24,2048]{1,0:T(8,128)(2,1)S(1)} collective-permute-done((bf16[24,2048]{1,0:T(8,128)(2,1)S(1)}, bf16[24,2048]{1,0:T(8,128)(2,1)S(1)}, u32[]{:S(2)}, u32[]{:S(2)}) %collective-permute-start.25) | collective-permute-done | bytes 98336 | tf_op jit(solution)/shard_map/ppermute | solution.py:558
  67.1 1.5 %collective-permute-start.32 = (bf16[40,2048]{1,0:T(8,128)(2,1)S(1)}, bf16[40,2048]{1,0:T(8,128)(2,1)S(1)}, u32[]{:S(2)}, u32[]{:S(2)}) collective-permute-start(bf16[40,2048]{1,0:T(8,128)(2,1)S(1)} %get-tuple-element.105), channel_id=1, source_target_pairs={{0,24},{4,28},{8,16},{12,20},{16,8},{20,12},{24,0},{28,4},{1,25},{... | collective-permute-start | bytes 491528 | tf_op jit(solution)/shard_map/ppermute | solution.py:558
  69.1 2.1 %collective-permute-start.36 = (bf16[32,2048]{1,0:T(8,128)(2,1)S(1)}, bf16[32,2048]{1,0:T(8,128)(2,1)S(1)}, u32[]{:S(2)}, u32[]{:S(2)}) collective-permute-start(bf16[32,2048]{1,0:T(8,128)(2,1)S(1)} %get-tuple-element.110), channel_id=1, source_target_pairs={{0,1},{1,0},{2,3},{3,2},{4,5},{5,4},{6,7},{7,6},{8,9},{9,8},{10,11... | collective-permute-start | bytes 393224 | tf_op jit(solution)/shard_map/ppermute | solution.py:558
  72.1 3.5 %collective-permute-done.31.refs_2_.refs_1_ = bf16[40,2048]{1,0:T(8,128)(2,1)S(1)} collective-permute-done((bf16[40,2048]{1,0:T(8,128)(2,1)S(1)}, bf16[40,2048]{1,0:T(8,128)(2,1)S(1)}, u32[]{:S(2)}, u32[]{:S(2)}) %collective-permute-start.31) | collective-permute-done | bytes 163872 | tf_op jit(solution)/shard_map/ppermute | solution.py:558
  75.7 2.1 %collective-permute-start.33 = (bf16[8,2048]{1,0:T(8,128)(2,1)S(1)}, bf16[8,2048]{1,0:T(8,128)(2,1)S(1)}, u32[]{:S(2)}, u32[]{:S(2)}) collective-permute-start(bf16[8,2048]{1,0:T(8,128)(2,1)S(1)} %get-tuple-element.106), channel_id=1, source_target_pairs={{0,1},{1,0},{2,3},{3,2},{4,5},{5,4},{6,7},{7,6},{8,9},{9,8},{10,11... | collective-permute-start | bytes 98312 | tf_op jit(solution)/shard_map/ppermute | solution.py:558
  78.6 1.5 %collective-permute-start.35 = (bf16[8,2048]{1,0:T(8,128)(2,1)S(1)}, bf16[8,2048]{1,0:T(8,128)(2,1)S(1)}, u32[]{:S(2)}, u32[]{:S(2)}) collective-permute-start(bf16[8,2048]{1,0:T(8,128)(2,1)S(1)} %get-tuple-element.108), channel_id=1, source_target_pairs={{0,3},{1,2},{2,1},{3,0},{4,7},{5,6},{6,5},{7,4},{8,11},{9,10},{10,... | collective-permute-start | bytes 98312 | tf_op jit(solution)/shard_map/ppermute | solution.py:558
  80.8 2.0 %collective-permute-done.34.refs_1_.refs_9_.refs_2_ = bf16[8,2048]{1,0:T(8,128)(2,1)S(1)} collective-permute-done((bf16[8,2048]{1,0:T(8,128)(2,1)S(1)}, bf16[8,2048]{1,0:T(8,128)(2,1)S(1)}, u32[]{:S(2)}, u32[]{:S(2)}) %collective-permute-start.34) | collective-permute-done | bytes 32800 | tf_op jit(solution)/shard_map/ppermute | solution.py:558
  82.8 2.0 %collective-permute-done.35.refs_2_.refs_10_.refs_3_ = bf16[8,2048]{1,0:T(8,128)(2,1)S(1)} collective-permute-done((bf16[8,2048]{1,0:T(8,128)(2,1)S(1)}, bf16[8,2048]{1,0:T(8,128)(2,1)S(1)}, u32[]{:S(2)}, u32[]{:S(2)}) %collective-permute-start.35) | collective-permute-done | bytes 32800 | tf_op jit(solution)/shard_map/ppermute | solution.py:558
  84.8 4.6 %collective-permute-start.39 = (bf16[32,2048]{1,0:T(8,128)(2,1)S(1)}, bf16[32,2048]{1,0:T(8,128)(2,1)S(1)}, u32[]{:S(2)}, u32[]{:S(2)}) collective-permute-start(bf16[32,2048]{1,0:T(8,128)(2,1)S(1)} %add_low.1.own_ref), channel_id=1, source_target_pairs={{0,2},{1,3},{2,0},{3,1},{4,6},{5,7},{6,4},{7,5},{8,10},{9,11},{10,... | collective-permute-start | bytes 393224 | tf_op jit(solution)/shard_map/ppermute | solution.py:558
  89.6 2.1 %collective-permute-start.42 = (bf16[8,2176]{1,0:T(8,128)(2,1)S(1)}, bf16[8,2176]{1,0:T(8,128)(2,1)S(1)}, u32[]{:S(2)}, u32[]{:S(2)}) collective-permute-start(bf16[8,2176]{1,0:T(8,128)(2,1)S(1)} %norm_grad.1.refs_4_), channel_id=1, source_target_pairs={{0,3},{1,2},{2,1},{3,0},{4,7},{5,6},{6,5},{7,4},{8,11},{9,10},{10,... | collective-permute-start | bytes 104456 | tf_op jit(solution)/shard_map/ppermute | solution.py:558
  91.7 2.3 %collective-permute-start.40 = (bf16[8,2176]{1,0:T(8,128)(2,1)S(1)}, bf16[8,2176]{1,0:T(8,128)(2,1)S(1)}, u32[]{:S(2)}, u32[]{:S(2)}) collective-permute-start(bf16[8,2176]{1,0:T(8,128)(2,1)S(1)} %norm_grad.1.refs_4_), channel_id=1, source_target_pairs={{0,1},{1,0},{2,3},{3,2},{4,5},{5,4},{6,7},{7,6},{8,9},{9,8},{10,11... | collective-permute-start | bytes 104456 | tf_op jit(solution)/shard_map/ppermute | solution.py:558
  95.7 2.0 %collective-permute-done.41.refs_9_.refs_6_ = bf16[8,2176]{1,0:T(8,128)(2,1)S(1)} collective-permute-done((bf16[8,2176]{1,0:T(8,128)(2,1)S(1)}, bf16[8,2176]{1,0:T(8,128)(2,1)S(1)}, u32[]{:S(2)}, u32[]{:S(2)}) %collective-permute-start.41) | collective-permute-done | bytes 34848 | tf_op jit(solution)/shard_map/ppermute | solution.py:558
  98.5 3.0 %merge_grad.1 = f32[288,128]{1,0:T(8,128)} custom-call(f32[4,288]{1,0:T(4,128)S(1)} %copy-done.15, bf16[32,1152]{1,0:T(8,128)(2,1)S(1)} %get-tuple-element.115.refs_1_, bf16[32,2176]{1,0:T(8,128)(2,1)S(1)} %stack.1.refs_6_.refs_0_.refs_2_, bf16[1152,2048]{1,0:T(8,128)(2,1)S(1)} %bitcast.10, bf16[8,2176]{1,0:T(8,128)(2,1)S(1)} %norm_grad.1.refs_4_, ...), custom_call_target="tpu_custom_call" | custom-call | bytes 12000000 | tf_op jit(solution)/shard_map/merge_grad/pallas_call | solution.py:512
  101.5 1.8 %collective-permute-done.43.refs_3_ = bf16[32,2048]{1,0:T(8,128)(2,1)S(1)} collective-permute-done((bf16[32,2048]{1,0:T(8,128)(2,1)S(1)}, bf16[32,2048]{1,0:T(8,128)(2,1)S(1)}, u32[]{:S(2)}, u32[]{:S(2)}) %collective-permute-start.43) | collective-permute-done | bytes 131104 | tf_op jit(solution)/shard_map/ppermute | solution.py:558
  (121 shorter events, 29.5 us)
Async XLA Ops:
  2.6 10.0 %collective-permute-start.3 = (bf16[592,128]{1,0:T(8,128)(2,1)}, bf16[592,128]{1,0:T(8,128)(2,1)S(1)}, u32[]{:S(2)}, u32[]{:S(2)}) collective-permute-start(bf16[592,128]{1,0:T(8,128)(2,1)} %pack.1), channel_id=1, source_target_pairs={{0,24},{4,28},{8,16},{12,20},{16,8},{20,12},{24,0},{28,4},{1,25},{... | collective-permute-start | bytes 454664 | tf_op jit(solution)/shard_map/ppermute | solution.py:558
  6.5 7.4 %collective-permute-start.2 = (bf16[592,128]{1,0:T(8,128)(2,1)}, bf16[592,128]{1,0:T(8,128)(2,1)S(1)}, u32[]{:S(2)}, u32[]{:S(2)}) collective-permute-start(bf16[592,128]{1,0:T(8,128)(2,1)} %pack.1), channel_id=1, source_target_pairs={{0,16},{4,20},{8,24},{12,28},{16,0},{20,4},{24,8},{28,12},{1,17},{... | collective-permute-start | bytes 454664 | tf_op jit(solution)/shard_map/ppermute | solution.py:558
  7.0 7.2 %collective-permute-start.1 = (bf16[592,128]{1,0:T(8,128)(2,1)}, bf16[592,128]{1,0:T(8,128)(2,1)S(1)}, u32[]{:S(2)}, u32[]{:S(2)}) collective-permute-start(bf16[592,128]{1,0:T(8,128)(2,1)} %pack.1), channel_id=1, source_target_pairs={{0,8},{4,12},{8,0},{12,4},{16,24},{20,28},{24,16},{28,20},{1,9},{5... | collective-permute-start | bytes 454664 | tf_op jit(solution)/shard_map/ppermute | solution.py:558
  7.2 10.5 %collective-permute-start = (bf16[592,128]{1,0:T(8,128)(2,1)}, bf16[592,128]{1,0:T(8,128)(2,1)S(1)}, u32[]{:S(2)}, u32[]{:S(2)}) collective-permute-start(bf16[592,128]{1,0:T(8,128)(2,1)} %pack.1), channel_id=1, source_target_pairs={{0,4},{4,0},{8,12},{12,8},{16,20},{20,16},{24,28},{28,24},{1,5},{5... | collective-permute-start | bytes 454664 | tf_op jit(solution)/shard_map/ppermute | solution.py:558
  14.2 7.8 %collective-permute-start.7 = (bf16[48,2048]{1,0:T(8,128)(2,1)S(1)}, bf16[48,2048]{1,0:T(8,128)(2,1)S(1)}, u32[]{:S(2)}, u32[]{:S(2)}) collective-permute-start(bf16[48,2048]{1,0:T(8,128)(2,1)S(1)} %get-tuple-element.73), channel_id=1, source_target_pairs={{0,8},{4,12},{8,0},{12,4},{16,24},{20,28},{24,16},{28,20},{1,9},{5... | collective-permute-start | bytes 589832 | tf_op jit(solution)/shard_map/ppermute | solution.py:558
  15.7 11.7 %collective-permute-start.8 = (bf16[48,2048]{1,0:T(8,128)(2,1)S(1)}, bf16[48,2048]{1,0:T(8,128)(2,1)S(1)}, u32[]{:S(2)}, u32[]{:S(2)}) collective-permute-start(bf16[48,2048]{1,0:T(8,128)(2,1)S(1)} %get-tuple-element.74), channel_id=1, source_target_pairs={{0,16},{4,20},{8,24},{12,28},{16,0},{20,4},{24,8},{28,12},{1,17},{... | collective-permute-start | bytes 589832 | tf_op jit(solution)/shard_map/ppermute | solution.py:558
  16.6 10.9 %collective-permute-start.9 = (bf16[48,2048]{1,0:T(8,128)(2,1)S(1)}, bf16[48,2048]{1,0:T(8,128)(2,1)S(1)}, u32[]{:S(2)}, u32[]{:S(2)}) collective-permute-start(bf16[48,2048]{1,0:T(8,128)(2,1)S(1)} %get-tuple-element.75), channel_id=1, source_target_pairs={{0,24},{4,28},{8,16},{12,20},{16,8},{20,12},{24,0},{28,4},{1,25},{... | collective-permute-start | bytes 589832 | tf_op jit(solution)/shard_map/ppermute | solution.py:558
  24.6 5.6 %collective-permute-start.11 = (bf16[8,2432]{1,0:T(8,128)(2,1)S(1)}, bf16[8,2432]{1,0:T(8,128)(2,1)S(1)}, u32[]{:S(2)}, u32[]{:S(2)}) collective-permute-start(bf16[8,2432]{1,0:T(8,128)(2,1)S(1)} %get-tuple-element.79), channel_id=1, source_target_pairs={{0,2},{1,3},{2,0},{3,1},{4,6},{5,7},{6,4},{7,5},{8,10},{9,11},{10,... | collective-permute-start | bytes 116744 | tf_op jit(solution)/shard_map/ppermute | solution.py:558
  27.2 5.8 %collective-permute-start.12 = (bf16[8,2432]{1,0:T(8,128)(2,1)S(1)}, bf16[8,2432]{1,0:T(8,128)(2,1)S(1)}, u32[]{:S(2)}, u32[]{:S(2)}) collective-permute-start(bf16[8,2432]{1,0:T(8,128)(2,1)S(1)} %get-tuple-element.80), channel_id=1, source_target_pairs={{0,3},{1,2},{2,1},{3,0},{4,7},{5,6},{6,5},{7,4},{8,11},{9,10},{10,... | collective-permute-start | bytes 116744 | tf_op jit(solution)/shard_map/ppermute | solution.py:558
  33.1 5.9 %collective-permute-start.15 = (bf16[8,2176]{1,0:T(8,128)(2,1)S(1)}, bf16[8,2176]{1,0:T(8,128)(2,1)S(1)}, u32[]{:S(2)}, u32[]{:S(2)}) collective-permute-start(bf16[8,2176]{1,0:T(8,128)(2,1)S(1)} %get-tuple-element.85.refs_0_.own_ref), channel_id=1, source_target_pairs={{0,3},{1,2},{2,1},{3,0},{4,7},{5,6},{6,5},{7,4},{8,11},{9,10},{10,... | collective-permute-start | bytes 104456 | tf_op jit(solution)/shard_map/ppermute | solution.py:558
  33.9 5.7 %collective-permute-start.14 = (bf16[8,2176]{1,0:T(8,128)(2,1)S(1)}, bf16[8,2176]{1,0:T(8,128)(2,1)S(1)}, u32[]{:S(2)}, u32[]{:S(2)}) collective-permute-start(bf16[8,2176]{1,0:T(8,128)(2,1)S(1)} %get-tuple-element.85.refs_0_.own_ref), channel_id=1, source_target_pairs={{0,2},{1,3},{2,0},{3,1},{4,6},{5,7},{6,4},{7,5},{8,10},{9,11},{10,... | collective-permute-start | bytes 104456 | tf_op jit(solution)/shard_map/ppermute | solution.py:558
  33.9 5.7 %collective-permute-start.13 = (bf16[8,2176]{1,0:T(8,128)(2,1)S(1)}, bf16[8,2176]{1,0:T(8,128)(2,1)S(1)}, u32[]{:S(2)}, u32[]{:S(2)}) collective-permute-start(bf16[8,2176]{1,0:T(8,128)(2,1)S(1)} %get-tuple-element.85.refs_0_.own_ref), channel_id=1, source_target_pairs={{0,1},{1,0},{2,3},{3,2},{4,5},{5,4},{6,7},{7,6},{8,9},{9,8},{10,11... | collective-permute-start | bytes 104456 | tf_op jit(solution)/shard_map/ppermute | solution.py:558
  39.7 7.5 %collective-permute-start.20 = (bf16[32,2176]{1,0:T(8,128)(2,1)S(1)}, bf16[32,2176]{1,0:T(8,128)(2,1)S(1)}, u32[]{:S(2)}, u32[]{:S(2)}) collective-permute-start(bf16[32,2176]{1,0:T(8,128)(2,1)S(1)} %stack.1.refs_6_.refs_0_.refs_2_), channel_id=1, source_target_pairs={{0,24},{4,28},{8,16},{12,20},{16,8},{20,12},{24,0},{28,4},{1,25},{... | collective-permute-start | bytes 417800 | tf_op jit(solution)/shard_map/ppermute | solution.py:558
  41.6 8.1 %collective-permute-start.19 = (bf16[32,2176]{1,0:T(8,128)(2,1)S(1)}, bf16[32,2176]{1,0:T(8,128)(2,1)S(1)}, u32[]{:S(2)}, u32[]{:S(2)}) collective-permute-start(bf16[32,2176]{1,0:T(8,128)(2,1)S(1)} %stack.1.refs_6_.refs_0_.refs_2_), channel_id=1, source_target_pairs={{0,16},{4,20},{8,24},{12,28},{16,0},{20,4},{24,8},{28,12},{1,17},{... | collective-permute-start | bytes 417800 | tf_op jit(solution)/shard_map/ppermute | solution.py:558
  42.7 7.1 %collective-permute-start.18 = (bf16[32,2176]{1,0:T(8,128)(2,1)S(1)}, bf16[32,2176]{1,0:T(8,128)(2,1)S(1)}, u32[]{:S(2)}, u32[]{:S(2)}) collective-permute-start(bf16[32,2176]{1,0:T(8,128)(2,1)S(1)} %stack.1.refs_6_.refs_0_.refs_2_), channel_id=1, source_target_pairs={{0,8},{4,12},{8,0},{12,4},{16,24},{20,28},{24,16},{28,20},{1,9},{5... | collective-permute-start | bytes 417800 | tf_op jit(solution)/shard_map/ppermute | solution.py:558
  43.9 6.4 %collective-permute-start.17 = (bf16[32,2176]{1,0:T(8,128)(2,1)S(1)}, bf16[32,2176]{1,0:T(8,128)(2,1)S(1)}, u32[]{:S(2)}, u32[]{:S(2)}) collective-permute-start(bf16[32,2176]{1,0:T(8,128)(2,1)S(1)} %stack.1.refs_6_.refs_0_.refs_2_), channel_id=1, source_target_pairs={{0,4},{4,0},{8,12},{12,8},{16,20},{20,16},{24,28},{28,24},{1,5},{5... | collective-permute-start | bytes 417800 | tf_op jit(solution)/shard_map/ppermute | solution.py:558
  58.1 6.8 %collective-permute-start.25 = (bf16[24,2048]{1,0:T(8,128)(2,1)S(1)}, bf16[24,2048]{1,0:T(8,128)(2,1)S(1)}, u32[]{:S(2)}, u32[]{:S(2)}) collective-permute-start(bf16[24,2048]{1,0:T(8,128)(2,1)S(1)} %get-tuple-element.92), channel_id=1, source_target_pairs={{0,16},{4,20},{8,24},{12,28},{16,0},{20,4},{24,8},{28,12},{1,17},{... | collective-permute-start | bytes 294920 | tf_op jit(solution)/shard_map/ppermute | solution.py:558
  58.9 6.0 %collective-permute-start.26 = (bf16[24,2048]{1,0:T(8,128)(2,1)S(1)}, bf16[24,2048]{1,0:T(8,128)(2,1)S(1)}, u32[]{:S(2)}, u32[]{:S(2)}) collective-permute-start(bf16[24,2048]{1,0:T(8,128)(2,1)S(1)} %get-tuple-element.93), channel_id=1, source_target_pairs={{0,24},{4,28},{8,16},{12,20},{16,8},{20,12},{24,0},{28,4},{1,25},{... | collective-permute-start | bytes 294920 | tf_op jit(solution)/shard_map/ppermute | solution.py:558
  65.0 7.1 %collective-permute-start.30 = (bf16[40,2048]{1,0:T(8,128)(2,1)S(1)}, bf16[40,2048]{1,0:T(8,128)(2,1)S(1)}, u32[]{:S(2)}, u32[]{:S(2)}) collective-permute-start(bf16[40,2048]{1,0:T(8,128)(2,1)S(1)} %get-tuple-element.103), channel_id=1, source_target_pairs={{0,8},{4,12},{8,0},{12,4},{16,24},{20,28},{24,16},{28,20},{1,9},{5... | collective-permute-start | bytes 491528 | tf_op jit(solution)/shard_map/ppermute | solution.py:558
  65.8 9.8 %collective-permute-start.31 = (bf16[40,2048]{1,0:T(8,128)(2,1)S(1)}, bf16[40,2048]{1,0:T(8,128)(2,1)S(1)}, u32[]{:S(2)}, u32[]{:S(2)}) collective-permute-start(bf16[40,2048]{1,0:T(8,128)(2,1)S(1)} %get-tuple-element.104), channel_id=1, source_target_pairs={{0,16},{4,20},{8,24},{12,28},{16,0},{20,4},{24,8},{28,12},{1,17},{... | collective-permute-start | bytes 491528 | tf_op jit(solution)/shard_map/ppermute | solution.py:558
  67.1 8.5 %collective-permute-start.32 = (bf16[40,2048]{1,0:T(8,128)(2,1)S(1)}, bf16[40,2048]{1,0:T(8,128)(2,1)S(1)}, u32[]{:S(2)}, u32[]{:S(2)}) collective-permute-start(bf16[40,2048]{1,0:T(8,128)(2,1)S(1)} %get-tuple-element.105), channel_id=1, source_target_pairs={{0,24},{4,28},{8,16},{12,20},{16,8},{20,12},{24,0},{28,4},{1,25},{... | collective-permute-start | bytes 491528 | tf_op jit(solution)/shard_map/ppermute | solution.py:558
  69.1 11.1 %collective-permute-start.36 = (bf16[32,2048]{1,0:T(8,128)(2,1)S(1)}, bf16[32,2048]{1,0:T(8,128)(2,1)S(1)}, u32[]{:S(2)}, u32[]{:S(2)}) collective-permute-start(bf16[32,2048]{1,0:T(8,128)(2,1)S(1)} %get-tuple-element.110), channel_id=1, source_target_pairs={{0,1},{1,0},{2,3},{3,2},{4,5},{5,4},{6,7},{7,6},{8,9},{9,8},{10,11... | collective-permute-start | bytes 393224 | tf_op jit(solution)/shard_map/ppermute | solution.py:558
  71.1 13.6 %collective-permute-start.29 = (bf16[32,2048]{1,0:T(8,128)(2,1)S(1)}, bf16[32,2048]{1,0:T(8,128)(2,1)S(1)}, u32[]{:S(2)}, u32[]{:S(2)}) collective-permute-start(bf16[32,2048]{1,0:T(8,128)(2,1)S(1)} %get-tuple-element.102.refs_4_), channel_id=1, source_target_pairs={{0,1},{1,0},{2,3},{3,2},{4,5},{5,4},{6,7},{7,6},{8,9},{9,8},{10,11... | collective-permute-start | bytes 393224 | tf_op jit(solution)/shard_map/ppermute | solution.py:558
  75.7 5.1 %collective-permute-start.33 = (bf16[8,2048]{1,0:T(8,128)(2,1)S(1)}, bf16[8,2048]{1,0:T(8,128)(2,1)S(1)}, u32[]{:S(2)}, u32[]{:S(2)}) collective-permute-start(bf16[8,2048]{1,0:T(8,128)(2,1)S(1)} %get-tuple-element.106), channel_id=1, source_target_pairs={{0,1},{1,0},{2,3},{3,2},{4,5},{5,4},{6,7},{7,6},{8,9},{9,8},{10,11... | collective-permute-start | bytes 98312 | tf_op jit(solution)/shard_map/ppermute | solution.py:558
  77.7 5.1 %collective-permute-start.34 = (bf16[8,2048]{1,0:T(8,128)(2,1)S(1)}, bf16[8,2048]{1,0:T(8,128)(2,1)S(1)}, u32[]{:S(2)}, u32[]{:S(2)}) collective-permute-start(bf16[8,2048]{1,0:T(8,128)(2,1)S(1)} %get-tuple-element.107), channel_id=1, source_target_pairs={{0,2},{1,3},{2,0},{3,1},{4,6},{5,7},{6,4},{7,5},{8,10},{9,11},{10,... | collective-permute-start | bytes 98312 | tf_op jit(solution)/shard_map/ppermute | solution.py:558
  78.6 6.1 %collective-permute-start.35 = (bf16[8,2048]{1,0:T(8,128)(2,1)S(1)}, bf16[8,2048]{1,0:T(8,128)(2,1)S(1)}, u32[]{:S(2)}, u32[]{:S(2)}) collective-permute-start(bf16[8,2048]{1,0:T(8,128)(2,1)S(1)} %get-tuple-element.108), channel_id=1, source_target_pairs={{0,3},{1,2},{2,1},{3,0},{4,7},{5,6},{6,5},{7,4},{8,11},{9,10},{10,... | collective-permute-start | bytes 98312 | tf_op jit(solution)/shard_map/ppermute | solution.py:558
  80.2 13.8 %collective-permute-start.37 = (bf16[32,2048]{1,0:T(8,128)(2,1)S(1)}, bf16[32,2048]{1,0:T(8,128)(2,1)S(1)}, u32[]{:S(2)}, u32[]{:S(2)}) collective-permute-start(bf16[32,2048]{1,0:T(8,128)(2,1)S(1)} %add_high.1.own_ref), channel_id=1, source_target_pairs={{0,2},{1,3},{2,0},{3,1},{4,6},{5,7},{6,4},{7,5},{8,10},{9,11},{10,... | collective-permute-start | bytes 393224 | tf_op jit(solution)/shard_map/ppermute | solution.py:558
  84.8 12.9 %collective-permute-start.39 = (bf16[32,2048]{1,0:T(8,128)(2,1)S(1)}, bf16[32,2048]{1,0:T(8,128)(2,1)S(1)}, u32[]{:S(2)}, u32[]{:S(2)}) collective-permute-start(bf16[32,2048]{1,0:T(8,128)(2,1)S(1)} %add_low.1.own_ref), channel_id=1, source_target_pairs={{0,2},{1,3},{2,0},{3,1},{4,6},{5,7},{6,4},{7,5},{8,10},{9,11},{10,... | collective-permute-start | bytes 393224 | tf_op jit(solution)/shard_map/ppermute | solution.py:558
  89.6 6.1 %collective-permute-start.42 = (bf16[8,2176]{1,0:T(8,128)(2,1)S(1)}, bf16[8,2176]{1,0:T(8,128)(2,1)S(1)}, u32[]{:S(2)}, u32[]{:S(2)}) collective-permute-start(bf16[8,2176]{1,0:T(8,128)(2,1)S(1)} %norm_grad.1.refs_4_), channel_id=1, source_target_pairs={{0,3},{1,2},{2,1},{3,0},{4,7},{5,6},{6,5},{7,4},{8,11},{9,10},{10,... | collective-permute-start | bytes 104456 | tf_op jit(solution)/shard_map/ppermute | solution.py:558
  91.7 6.0 %collective-permute-start.41 = (bf16[8,2176]{1,0:T(8,128)(2,1)S(1)}, bf16[8,2176]{1,0:T(8,128)(2,1)S(1)}, u32[]{:S(2)}, u32[]{:S(2)}) collective-permute-start(bf16[8,2176]{1,0:T(8,128)(2,1)S(1)} %norm_grad.1.refs_4_), channel_id=1, source_target_pairs={{0,2},{1,3},{2,0},{3,1},{4,6},{5,7},{6,4},{7,5},{8,10},{9,11},{10,... | collective-permute-start | bytes 104456 | tf_op jit(solution)/shard_map/ppermute | solution.py:558
  91.7 6.0 %collective-permute-start.40 = (bf16[8,2176]{1,0:T(8,128)(2,1)S(1)}, bf16[8,2176]{1,0:T(8,128)(2,1)S(1)}, u32[]{:S(2)}, u32[]{:S(2)}) collective-permute-start(bf16[8,2176]{1,0:T(8,128)(2,1)S(1)} %norm_grad.1.refs_4_), channel_id=1, source_target_pairs={{0,1},{1,0},{2,3},{3,2},{4,5},{5,4},{6,7},{7,6},{8,9},{9,8},{10,11... | collective-permute-start | bytes 104456 | tf_op jit(solution)/shard_map/ppermute | solution.py:558
  94.5 7.0 %collective-permute-start.38 = (bf16[32,2048]{1,0:T(8,128)(2,1)S(1)}, bf16[32,2048]{1,0:T(8,128)(2,1)S(1)}, u32[]{:S(2)}, u32[]{:S(2)}) collective-permute-start(bf16[32,2048]{1,0:T(8,128)(2,1)S(1)} %finish.2.refs_0_), channel_id=1, source_target_pairs={{0,1},{1,0},{2,3},{3,2},{4,5},{5,4},{6,7},{7,6},{8,9},{9,8},{10,11... | collective-permute-start | bytes 393224 | tf_op jit(solution)/shard_map/ppermute | solution.py:558
  (31 other events, 308.5 us)

commit v3 on v2

--- a/solution.py
+++ b/solution.py
@@ -255,7 +255,7 @@
 
 
 def merge_kernel(_, *refs, width, features):
-    *message_refs, out_ref, vision_ref, gain_ref = refs
+    *message_refs, out_ref, gain_ref = refs
     share, row_share = len(message_refs), out_ref.shape[0]
     piece = width // row_share
     parts = [ref[...].astype(F32) for ref in message_refs]
@@ -272,7 +272,6 @@
         gain_sum = jnp.concatenate([tail[j : j + 1] for j in range(row_share)], axis=1)
         total = total + part[:, :width] + (local - mean) * gain_sum
         gain_total = gain_total + gain_sum
-    vision_ref[...] = total * inv_std
     gain_ref[...] = gain_total
     out_ref[:, :width] = (total * inv_std).astype(BF16)
     out_ref[:, width:] = put_scalars([mean, inv_std], row_share).astype(BF16)
@@ -400,13 +399,24 @@
     return total
 
 
-def chip_sum_kernel(*refs, count):
-    cot_ref, *out_refs = refs[count + 1 :]
+def chip_sum_kernel(*refs, count, order):
+    cot_ref, keep_ref, send_ref = refs[count + 1 :]
     total = total_of(refs[:count])
     rows = cot_ref.shape[0]
-    for k, out_ref in enumerate(out_refs):
-        out_ref[...] = total[k * rows : (k + 1) * rows].astype(BF16)
-    cot_ref[...] = total[len(out_refs) * rows :].astype(BF16)
+    turned = jnp.concatenate([total[k * rows : (k + 1) * rows] for k in order], axis=0)
+    half = turned.shape[0] // 2
+    keep_ref[...] = turned[:half]
+    send_ref[...] = turned[half:].astype(BF16)
+    cot_ref[...] = total[len(order) * rows :].astype(BF16)
+
+
+def grad_halve_kernel(keep_ref, arrived_ref, *refs):
+    quarters(keep_ref[...] + arrived_ref[...].astype(F32), refs)
+
+
+def grad_join_kernel(keep_ref, arrived_ref, cot_ref, out_ref):
+    total = keep_ref[...] + arrived_ref[...].astype(F32)
+    out_ref[...] = jnp.concatenate([total, cot_ref[...].astype(F32)], axis=0).astype(BF16)
 
 
 def quarters(total, out_refs):
@@ -453,13 +463,17 @@
 
 
 def norm_grad_kernel(
-    own_ref, gain_ref, cot_ref, vision_ref, total_ref, *refs, features
+    joined_ref, other_ref, rows_ref, gain_ref, total_ref, out_ref, *, features
 ):
-    *part_refs, out_ref = refs
     width = gain_ref.shape[1]
-    hidden = total_of(part_refs)
-    cotangent = cot_ref[...].astype(F32)
-    inputs = own_ref[:, :width].astype(F32)
+    count = out_ref.shape[0] // 2
+    far = rows_ref.shape[0] // 2
+    joined, other = joined_ref[...].astype(F32), other_ref[...].astype(F32)
+    turned = jnp.concatenate([other[count : 2 * count], other[:count]], axis=0)
+    hidden = joined[: 2 * count] + turned
+    cotangent = jnp.concatenate([joined[2 * count :], other[2 * count :]], axis=0)
+    rows = rows_ref[:, :width].astype(F32)
+    inputs = jnp.concatenate([rows[:count], rows[far : far + count]], axis=0)
     scale = lax.rsqrt(jnp.mean(inputs * inputs, axis=1, keepdims=True) + EPS)
     pulled = hidden * gain_ref[...]
     cross = jnp.mean(pulled * inputs, axis=1, keepdims=True)
@@ -468,17 +482,22 @@
     out_ref[:, :width] = grad
     grad = grad.astype(F32)
     grad_mean = jnp.sum(grad * total_ref[...], axis=1, keepdims=True) / features
-    cross_mean = jnp.sum(grad * vision_ref[...], axis=1, keepdims=True) / features
-    out_ref[:, width:] = put_scalars([grad_mean, cross_mean], grad.shape[0]).astype(BF16)
-
-
-def merge_grad_kernel(*refs, size):
+    cross_mean = jnp.sum(grad * inputs, axis=1, keepdims=True) / features
+    out_ref[:, width:] = put_scalars([grad_mean, cross_mean], 2 * count).astype(BF16)
+
+
+def merge_grad_kernel(*refs, size, bases):
     gain_ref, merged_ref, scalar_ref, weight_ref, *part_refs, out_ref = refs
     rows, features = merged_ref.shape
     width = weight_ref.shape[1]
     depth, patches = out_ref.shape
-    row_share = part_refs[0].shape[0]
-    parts = stacked(part_refs)
+    row_share = part_refs[0].shape[0] // 2
+    blocks = {}
+    for base, ref in zip(bases, part_refs):
+        part = ref[...].astype(F32)
+        blocks[base] = part[:row_share]
+        blocks[base ^ len(bases)] = part[row_share:]
+    parts = jnp.concatenate([blocks[k] for k in sorted(blocks)], axis=0).astype(BF16)
     normed_grad = dot_nt(parts[:, :width], weight_ref[...]) * flat_gain(gain_ref)
     means = parts[:, width:].astype(F32)
     scalars = scalar_ref[:, width:].astype(F32)
@@ -648,11 +667,10 @@
     )
     message = trade(message, "expert")
     early = early[:1] + list(after(early[1:], message[1:]))
-    own, vision_exact, gain_total = run(
+    own, gain_total = run(
         functools.partial(merge_kernel, width=width, features=features),
         [
-            shape((row_share, width + 128)), shape((row_share, width), F32),
-            shape((1, width), F32),
+            shape((row_share, width + 128)), shape((1, width), F32),
         ],
         early[1], *message, far=(0,), cost=0.2, name="merge",
     )
@@ -695,8 +713,9 @@
         combine_kernel, pieces, comb, *returned,
         to_sibling(returned, grads[:1], "returned_half"), cost=0.01, name="combine",
     )
-    first_sent, step = sent_low, 1
+    step = 1
     arrived_high = swap(sent_high, "expert", step)
+    first_arrived = arrived_high
     arrived_low = swap(sent_low, "expert", step)
     while count > part:
         count //= 2
@@ -716,31 +735,51 @@
         )
 
     sum_high = add(high, arrived_high, grads[1:], "add_high")
-    cot_rows, *grads = run(
-        functools.partial(chip_sum_kernel, count=blocks // 2),
-        [shape((row_share, width))] * (share + 1), *grads, first_sent, far=(blocks // 2,), cost=0.2,
-        name="chip_sum",
-    )
-    grads = trade(grads, "expert")
-    sums = [add(low, arrived_low, grads[1:], "add_low"), sum_high]
+    cot_rows, keep, sent = run(
+        functools.partial(chip_sum_kernel, count=blocks // 2, order=halving_order(share)),
+        [
+            shape((row_share, width)), shape((rows // 2, width), F32), shape((rows // 2, width)),
+        ],
+        *grads, first_arrived, far=(blocks // 2,), cost=0.2, name="chip_sum",
+    )
+    bit, kept_rows = 1, rows // 2
+    while kept_rows > 2 * row_share:
+        kept_rows //= 2
+        keep, sent = run(
+            grad_halve_kernel, [shape((kept_rows, width), F32), shape((kept_rows, width))],
+            keep, swap(sent, "expert", bit), cost=0.2, name="grad_halve",
+        )
+        bit *= 2
+    joined = run(
+        grad_join_kernel, shape((3 * row_share, width)),
+        keep, swap(sent, "expert", bit), cot_rows, cost=0.2, name="grad_join",
+    )
+    other = swap(joined, "expert", share // 2)
+    sums = [add(low, arrived_low, [other], "add_low"), sum_high]
     others = [swap(value, "expert", step) for value in sums][::-1]
     vision_grad = run(
         functools.partial(norm_grad_kernel, features=share * features),
-        shape((row_share, width + 128)),
-        own, gain_row, cot_rows, vision_exact, gain_total, *grads, cost=0.3, name="norm_grad",
-    )
-    vision_grads = spread_out(vision_grad, "expert")
+        shape((2 * row_share, width + 128)),
+        joined, other, block_rows, gain_row, gain_total, cost=0.3, name="norm_grad",
+    )
+    vision_grads, bit = {0: vision_grad}, share // 4
+    while bit:
+        vision_grads.update({k + bit: swap(vision_grads[k], "expert", bit) for k in list(vision_grads)})
+        bit //= 2
+    bases = sorted(vision_grads)
+    vision_grads = [vision_grads[k] for k in bases]
     attn_grad = run(
-        functools.partial(merge_grad_kernel, size=size), shape((depth, patches), F32),
+        functools.partial(merge_grad_kernel, size=size, bases=tuple(bases)),
+        shape((depth, patches), F32),
         merge_gain, merged, block_rows, weight_flat, *vision_grads, cost=4.0, name="merge_grad",
     )
 
     laid = {}
-    for turn, value, other, gate in zip((0, step), sums, others, (grads, vision_grads)):
+    for turn, value, other, gate in zip((0, step), sums, others, ([other], vision_grads[1:])):
         laid[turn] = run(
             functools.partial(finish_kernel, blocks=blocks, turn=turn), shape((part, width)),
-            placed, text, value, other, *vision, *gate[1:],
-            far=range(4 + blocks, 3 + blocks + share), cost=1.0, name="finish",
+            placed, text, value, other, *vision, *gate,
+            far=range(4 + blocks, 4 + blocks + len(gate)), cost=1.0, name="finish",
         )
     while step > 1:
         step //= 2

time: 104 us -> 106 us (1.019)
  waiting for transfers between devices: 34 us -> 40.2 us
  starting transfers between devices: 45.6 us -> 40.9 us
    ppermute x44 -> x41, waiting for transfers between devices: 34 us -> 40.2 us  [swap(): return lax.ppermute(value, axis, [(i, i ^ step) for i in range(count)])]
    ppermute x44 -> x41, starting transfers between devices: 45.6 us -> 40.9 us  [swap(): return lax.ppermute(value, axis, [(i, i ^ step) for i in range(count)])]
    pallas_call x23 -> x24, Pallas kernels: 19.2 us -> 19.2 us  [run(): pl.pallas_call(kernel, out_shape=outs, in_specs=specs, out_specs=jax.tree...]
  transfers between devices with their start and end apart: 44 -> 41, of which waited for: 23 -> 24; matrix products, arithmetic and copies ran while one was open for 0% -> 0% of each run, Pallas kernels for 11% -> 11%
where the time goes in v3:
time: 106 us
  starting transfers between devices  40.9 us (39%)
  waiting for transfers between devices  40.2 us (38%)
  Pallas kernels  19.2 us (18%)
  local copies, waits for them, and re-layouts  4.22 us (4%)
    ppermute x41, starting transfers between devices, swap(): return lax.ppermute(value, axis, [(i, i ^ step) for i in range(count)])  40.9 us
    ppermute x41, waiting for transfers between devices, swap(): return lax.ppermute(value, axis, [(i, i ^ step) for i in range(count)])  40.2 us
    pallas_call x24, Pallas kernels, run(): pl.pallas_call(kernel, out_shape=outs, in_specs=specs, out_specs=jax.tree...  19.2 us
    unnamed x38, local copies, waits for them, and re-layouts  4.22 us
  transfers between devices with their start and end apart: 41, of which 24 were waited for; matrix products, arithmetic and copies ran while one was open for 0% of the time, Pallas kernels for 11%

profile of v3, /device:TPU:0, one launch (start us, length us, event | category | flops | bytes accessed | tf_op | source)
XLA Modules:
  0.0 105.6 jit_solution(11168136378743962777)
XLA Ops:
  0.7 1.8 %pack.1 = bf16[592,128]{1,0:T(8,128)(2,1)} custom-call(bf16[288,128]{1,0:T(8,128)(2,1)} %bitcast.11, bf16[288,128]{1,0:T(8,128)(2,1)} %bitcast.13, s32[1,32]{1,0:T(1,128)} %bitcast.22, s32[1,32]{1,0:T(1,128)} %bitcast.24, s32[8,128]{1,0:T(8,128)} %bitcast.18), custom_call_target="tpu_custom_call" | custom-call | bytes 3000000 | tf_op jit(solution)/shard_map/pack/pallas_call | solution.py:531
  2.6 4.0 %collective-permute-start.3 = (bf16[592,128]{1,0:T(8,128)(2,1)}, bf16[592,128]{1,0:T(8,128)(2,1)S(1)}, u32[]{:S(2)}, u32[]{:S(2)}) collective-permute-start(bf16[592,128]{1,0:T(8,128)(2,1)} %pack.1), channel_id=1, source_target_pairs={{0,24},{4,28},{8,16},{12,20},{16,8},{20,12},{24,0},{28,4},{1,25},{... | collective-permute-start | bytes 454664 | tf_op jit(solution)/shard_map/ppermute | solution.py:577
  12.6 1.4 %collective-permute-done.2.refs_1_ = bf16[592,128]{1,0:T(8,128)(2,1)S(1)} collective-permute-done((bf16[592,128]{1,0:T(8,128)(2,1)}, bf16[592,128]{1,0:T(8,128)(2,1)S(1)}, u32[]{:S(2)}, u32[]{:S(2)}) %collective-permute-start.2) | collective-permute-done | bytes 151584 | tf_op jit(solution)/shard_map/ppermute | solution.py:577
  14.2 1.5 %collective-permute-start.7 = (bf16[48,2048]{1,0:T(8,128)(2,1)S(1)}, bf16[48,2048]{1,0:T(8,128)(2,1)S(1)}, u32[]{:S(2)}, u32[]{:S(2)}) collective-permute-start(bf16[48,2048]{1,0:T(8,128)(2,1)S(1)} %get-tuple-element.70), channel_id=1, source_target_pairs={{0,8},{4,12},{8,0},{12,4},{16,24},{20,28},{24,16},{28,20},{1,9},{5... | collective-permute-start | bytes 589832 | tf_op jit(solution)/shard_map/ppermute | solution.py:577
  19.4 2.6 %attend.1 = (bf16[32,1152]{1,0:T(8,128)(2,1)S(1)}, bf16[128,128]{1,0:T(8,128)(2,1)S(1)}, bf16[48,1152]{1,0:T(8,128)(2,1)S(1)}, f32[32,128]{1,0:T(8,128)S(1)}) custom-call(bf16[4,72,128]{2,1,0:T(8,128)(2,1)S(1)} %copy-done.12, f32[4,288]{1,0:T(4,128)S(1)} %copy-done.15, bf16[288,128]{1,0:T(8,128)(2,1)S(1)} %bitcast.12, bf16[288,128]{1,0:T(8,128)(2,1)S(1)} %bitcast.14, ...), custom_call_target="tpu_custom_call" | custom-call | bytes 9000000 | tf_op jit(solution)/shard_map/attend/pallas_call | solution.py:531
  23.0 1.6 %collective-permute-start.10 = (bf16[8,2432]{1,0:T(8,128)(2,1)S(1)}, bf16[8,2432]{1,0:T(8,128)(2,1)S(1)}, u32[]{:S(2)}, u32[]{:S(2)}) collective-permute-start(bf16[8,2432]{1,0:T(8,128)(2,1)S(1)} %get-tuple-element.75), channel_id=1, source_target_pairs={{0,1},{1,0},{2,3},{3,2},{4,5},{5,4},{6,7},{7,6},{8,9},{9,8},{10,11... | collective-permute-start | bytes 116744 | tf_op jit(solution)/shard_map/ppermute | solution.py:577
  24.6 2.6 %collective-permute-start.11 = (bf16[8,2432]{1,0:T(8,128)(2,1)S(1)}, bf16[8,2432]{1,0:T(8,128)(2,1)S(1)}, u32[]{:S(2)}, u32[]{:S(2)}) collective-permute-start(bf16[8,2432]{1,0:T(8,128)(2,1)S(1)} %get-tuple-element.76), channel_id=1, source_target_pairs={{0,2},{1,3},{2,0},{3,1},{4,6},{5,7},{6,4},{7,5},{8,10},{9,11},{10,... | collective-permute-start | bytes 116744 | tf_op jit(solution)/shard_map/ppermute | solution.py:577
  27.4 2.8 %collective-permute-done.11.refs_4_.refs_2_ = bf16[8,2432]{1,0:T(8,128)(2,1)S(1)} collective-permute-done((bf16[8,2432]{1,0:T(8,128)(2,1)S(1)}, bf16[8,2432]{1,0:T(8,128)(2,1)S(1)}, u32[]{:S(2)}, u32[]{:S(2)}) %collective-permute-start.11) | collective-permute-done | bytes 38944 | tf_op jit(solution)/shard_map/ppermute | solution.py:577
  30.2 2.8 %collective-permute-done.12.refs_5_.refs_3_ = bf16[8,2432]{1,0:T(8,128)(2,1)S(1)} collective-permute-done((bf16[8,2432]{1,0:T(8,128)(2,1)S(1)}, bf16[8,2432]{1,0:T(8,128)(2,1)S(1)}, u32[]{:S(2)}, u32[]{:S(2)}) %collective-permute-start.12) | collective-permute-done | bytes 38944 | tf_op jit(solution)/shard_map/ppermute | solution.py:577
  33.9 3.7 %collective-permute-start.13 = (bf16[8,2176]{1,0:T(8,128)(2,1)S(1)}, bf16[8,2176]{1,0:T(8,128)(2,1)S(1)}, u32[]{:S(2)}, u32[]{:S(2)}) collective-permute-start(bf16[8,2176]{1,0:T(8,128)(2,1)S(1)} %get-tuple-element.82.refs_0_), channel_id=1, source_target_pairs={{0,1},{1,0},{2,3},{3,2},{4,5},{5,4},{6,7},{7,6},{8,9},{9,8},{10,11... | collective-permute-start | bytes 104456 | tf_op jit(solution)/shard_map/ppermute | solution.py:577
  37.6 1.4 %collective-permute-done.15.refs_6_.refs_3_ = bf16[8,2176]{1,0:T(8,128)(2,1)S(1)} collective-permute-done((bf16[8,2176]{1,0:T(8,128)(2,1)S(1)}, bf16[8,2176]{1,0:T(8,128)(2,1)S(1)}, u32[]{:S(2)}, u32[]{:S(2)}) %collective-permute-start.15) | collective-permute-done | bytes 34848 | tf_op jit(solution)/shard_map/ppermute | solution.py:577
  39.7 1.9 %collective-permute-start.20 = (bf16[32,2176]{1,0:T(8,128)(2,1)S(1)}, bf16[32,2176]{1,0:T(8,128)(2,1)S(1)}, u32[]{:S(2)}, u32[]{:S(2)}) collective-permute-start(bf16[32,2176]{1,0:T(8,128)(2,1)S(1)} %stack.1.refs_6_.refs_0_.rows_ref.refs_2_), channel_id=1, source_target_pairs={{0,24},{4,28},{8,16},{12,20},{16,8},{20,12},{24,0},{28,4},{1,25},{... | collective-permute-start | bytes 417800 | tf_op jit(solution)/shard_map/ppermute | solution.py:577
  45.3 1.9 %collective-permute-done.20.refs_2_ = bf16[32,2176]{1,0:T(8,128)(2,1)S(1)} collective-permute-done((bf16[32,2176]{1,0:T(8,128)(2,1)S(1)}, bf16[32,2176]{1,0:T(8,128)(2,1)S(1)}, u32[]{:S(2)}, u32[]{:S(2)}) %collective-permute-start.20) | collective-permute-done | bytes 139296 | tf_op jit(solution)/shard_map/ppermute | solution.py:577
  47.2 2.5 %collective-permute-done.19.refs_1_ = bf16[32,2176]{1,0:T(8,128)(2,1)S(1)} collective-permute-done((bf16[32,2176]{1,0:T(8,128)(2,1)S(1)}, bf16[32,2176]{1,0:T(8,128)(2,1)S(1)}, u32[]{:S(2)}, u32[]{:S(2)}) %collective-permute-start.19) | collective-permute-done | bytes 139296 | tf_op jit(solution)/shard_map/ppermute | solution.py:577
  51.7 3.2 %forward.1 = (f32[96,768]{1,0:T(8,128)S(1)}, f32[96,768]{1,0:T(8,128)S(1)}, bf16[24,2048]{1,0:T(8,128)(2,1)S(1)}, bf16[24,2048]{1,0:T(8,128)(2,1)S(1)}, bf16[24,...) custom-call(bf16[96,256]{1,0:T(8,128)(2,1)S(1)} %get-tuple-element.68.refs_4_.refs_0_.slots_ref, ...), custom_call_target="tpu_custom_call" | custom-call | bytes 12000000 | tf_op jit(solution)/shard_map/forward/pallas_call | solution.py:531
  54.9 1.5 %backward.1 = (bf16[160,2048]{1,0:T(8,128)(2,1)S(1)}, bf16[160,2048]{1,0:T(8,128)(2,1)S(1)}) custom-call(bf16[96,256]{1,0:T(8,128)(2,1)S(1)} %get-tuple-element.68.refs_4_.refs_0_.slots_ref, f32[96,768]{1,0:T(8,128)S(1)} %get-tuple-element.91.grad_ref, f32[96,768]{1,0:T(8,128)S(1)} %get-tuple-element.92.gate_in, f32[96,768]{1,0:T(8,128)S(1)} %get-tuple-element.93.up_in, ...), custom_call_target="tpu_custom_call" | custom-call | bytes 12000000 | tf_op jit(solution)/shard_map/backward/pallas_call | solution.py:531
  56.6 1.4 %collective-permute-start.24 = (bf16[24,2048]{1,0:T(8,128)(2,1)S(1)}, bf16[24,2048]{1,0:T(8,128)(2,1)S(1)}, u32[]{:S(2)}, u32[]{:S(2)}) collective-permute-start(bf16[24,2048]{1,0:T(8,128)(2,1)S(1)} %get-tuple-element.88), channel_id=1, source_target_pairs={{0,8},{4,12},{8,0},{12,4},{16,24},{20,28},{24,16},{28,20},{1,9},{5... | collective-permute-start | bytes 294920 | tf_op jit(solution)/shard_map/ppermute | solution.py:577
  60.3 1.4 %collective-permute-done.24.refs_1_ = bf16[24,2048]{1,0:T(8,128)(2,1)S(1)} collective-permute-done((bf16[24,2048]{1,0:T(8,128)(2,1)S(1)}, bf16[24,2048]{1,0:T(8,128)(2,1)S(1)}, u32[]{:S(2)}, u32[]{:S(2)}) %collective-permute-start.24) | collective-permute-done | bytes 98336 | tf_op jit(solution)/shard_map/ppermute | solution.py:577
  61.7 3.2 %collective-permute-done.25.refs_2_ = bf16[24,2048]{1,0:T(8,128)(2,1)S(1)} collective-permute-done((bf16[24,2048]{1,0:T(8,128)(2,1)S(1)}, bf16[24,2048]{1,0:T(8,128)(2,1)S(1)}, u32[]{:S(2)}, u32[]{:S(2)}) %collective-permute-start.25) | collective-permute-done | bytes 98336 | tf_op jit(solution)/shard_map/ppermute | solution.py:577
  65.8 1.3 %collective-permute-start.31 = (bf16[40,2048]{1,0:T(8,128)(2,1)S(1)}, bf16[40,2048]{1,0:T(8,128)(2,1)S(1)}, u32[]{:S(2)}, u32[]{:S(2)}) collective-permute-start(bf16[40,2048]{1,0:T(8,128)(2,1)S(1)} %get-tuple-element.101), channel_id=1, source_target_pairs={{0,16},{4,20},{8,24},{12,28},{16,0},{20,4},{24,8},{28,12},{1,17},{... | collective-permute-start | bytes 491528 | tf_op jit(solution)/shard_map/ppermute | solution.py:577
  67.1 1.4 %collective-permute-start.32 = (bf16[40,2048]{1,0:T(8,128)(2,1)S(1)}, bf16[40,2048]{1,0:T(8,128)(2,1)S(1)}, u32[]{:S(2)}, u32[]{:S(2)}) collective-permute-start(bf16[40,2048]{1,0:T(8,128)(2,1)S(1)} %get-tuple-element.102), channel_id=1, source_target_pairs={{0,24},{4,28},{8,16},{12,20},{16,8},{20,12},{24,0},{28,4},{1,25},{... | collective-permute-start | bytes 491528 | tf_op jit(solution)/shard_map/ppermute | solution.py:577
  69.0 2.1 %collective-permute-start.33 = (bf16[32,2048]{1,0:T(8,128)(2,1)S(1)}, bf16[32,2048]{1,0:T(8,128)(2,1)S(1)}, u32[]{:S(2)}, u32[]{:S(2)}) collective-permute-start(bf16[32,2048]{1,0:T(8,128)(2,1)S(1)} %get-tuple-element.103), channel_id=1, source_target_pairs={{0,1},{1,0},{2,3},{3,2},{4,5},{5,4},{6,7},{7,6},{8,9},{9,8},{10,11... | collective-permute-start | bytes 393224 | tf_op jit(solution)/shard_map/ppermute | solution.py:577
  72.1 3.5 %collective-permute-done.31.refs_2_.refs_1_ = bf16[40,2048]{1,0:T(8,128)(2,1)S(1)} collective-permute-done((bf16[40,2048]{1,0:T(8,128)(2,1)S(1)}, bf16[40,2048]{1,0:T(8,128)(2,1)S(1)}, u32[]{:S(2)}, u32[]{:S(2)}) %collective-permute-start.31) | collective-permute-done | bytes 163872 | tf_op jit(solution)/shard_map/ppermute | solution.py:577
  75.7 2.0 %collective-permute-start.34 = (bf16[16,2048]{1,0:T(8,128)(2,1)S(1)}, bf16[16,2048]{1,0:T(8,128)(2,1)S(1)}, u32[]{:S(2)}, u32[]{:S(2)}) collective-permute-start(bf16[16,2048]{1,0:T(8,128)(2,1)S(1)} %get-tuple-element.105), channel_id=1, source_target_pairs={{0,1},{1,0},{2,3},{3,2},{4,5},{5,4},{6,7},{7,6},{8,9},{9,8},{10,11... | collective-permute-start | bytes 196616 | tf_op jit(solution)/shard_map/ppermute | solution.py:577
  77.8 2.6 %collective-permute-done.34.arrived_ref = bf16[16,2048]{1,0:T(8,128)(2,1)S(1)} collective-permute-done((bf16[16,2048]{1,0:T(8,128)(2,1)S(1)}, bf16[16,2048]{1,0:T(8,128)(2,1)S(1)}, u32[]{:S(2)}, u32[]{:S(2)}) %collective-permute-start.34) | collective-permute-done | bytes 65568 | tf_op jit(solution)/shard_map/ppermute | solution.py:577
  80.5 1.5 %collective-permute-start.35 = (bf16[24,2048]{1,0:T(8,128)(2,1)S(1)}, bf16[24,2048]{1,0:T(8,128)(2,1)S(1)}, u32[]{:S(2)}, u32[]{:S(2)}) collective-permute-start(bf16[24,2048]{1,0:T(8,128)(2,1)S(1)} %grad_join.1.joined_ref), channel_id=1, source_target_pairs={{0,2},{1,3},{2,0},{3,1},{4,6},{5,7},{6,4},{7,5},{8,10},{9,11},{10,... | collective-permute-start | bytes 294920 | tf_op jit(solution)/shard_map/ppermute | solution.py:577
  82.0 1.5 %collective-permute-start.36 = (bf16[32,2048]{1,0:T(8,128)(2,1)S(1)}, bf16[32,2048]{1,0:T(8,128)(2,1)S(1)}, u32[]{:S(2)}, u32[]{:S(2)}) collective-permute-start(bf16[32,2048]{1,0:T(8,128)(2,1)S(1)} %add_high.1.own_ref), channel_id=1, source_target_pairs={{0,2},{1,3},{2,0},{3,1},{4,6},{5,7},{6,4},{7,5},{8,10},{9,11},{10,... | collective-permute-start | bytes 393224 | tf_op jit(solution)/shard_map/ppermute | solution.py:577
  84.1 7.9 %collective-permute-done.35.refs_0_.refs_8_.other_ref = bf16[24,2048]{1,0:T(8,128)(2,1)S(1)} collective-permute-done((bf16[24,2048]{1,0:T(8,128)(2,1)S(1)}, bf16[24,2048]{1,0:T(8,128)(2,1)S(1)}, u32[]{:S(2)}, u32[]{:S(2)}) %collective-permute-start.35) | collective-permute-done | bytes 98336 | tf_op jit(solution)/shard_map/ppermute | solution.py:577
  92.4 3.0 %collective-permute-start.39 = (bf16[16,2176]{1,0:T(8,128)(2,1)S(1)}, bf16[16,2176]{1,0:T(8,128)(2,1)S(1)}, u32[]{:S(2)}, u32[]{:S(2)}) collective-permute-start(bf16[16,2176]{1,0:T(8,128)(2,1)S(1)} %norm_grad.1.refs_4_), channel_id=1, source_target_pairs={{0,1},{1,0},{2,3},{3,2},{4,5},{5,4},{6,7},{7,6},{8,9},{9,8},{10,11... | collective-permute-start | bytes 208904 | tf_op jit(solution)/shard_map/ppermute | solution.py:577
  96.0 2.1 %collective-permute-done.39.refs_8_.refs_5_ = bf16[16,2176]{1,0:T(8,128)(2,1)S(1)} collective-permute-done((bf16[16,2176]{1,0:T(8,128)(2,1)S(1)}, bf16[16,2176]{1,0:T(8,128)(2,1)S(1)}, u32[]{:S(2)}, u32[]{:S(2)}) %collective-permute-start.39) | collective-permute-done | bytes 69664 | tf_op jit(solution)/shard_map/ppermute | solution.py:577
  99.7 1.4 %collective-permute-start.40 = (bf16[32,2048]{1,0:T(8,128)(2,1)S(1)}, bf16[32,2048]{1,0:T(8,128)(2,1)S(1)}, u32[]{:S(2)}, u32[]{:S(2)}) collective-permute-start(bf16[32,2048]{1,0:T(8,128)(2,1)S(1)} %finish.3.refs_2_), channel_id=1, source_target_pairs={{0,1},{1,0},{2,3},{3,2},{4,5},{5,4},{6,7},{7,6},{8,9},{9,8},{10,11... | collective-permute-start | bytes 393224 | tf_op jit(solution)/shard_map/ppermute | solution.py:577
  101.1 3.0 %merge_grad.1 = f32[288,128]{1,0:T(8,128)} custom-call(f32[4,288]{1,0:T(4,128)S(1)} %copy-done.15, bf16[32,1152]{1,0:T(8,128)(2,1)S(1)} %get-tuple-element.109.refs_1_, bf16[32,2176]{1,0:T(8,128)(2,1)S(1)} %stack.1.refs_6_.refs_0_.rows_ref.refs_2_, bf16[1152,2048]{1,0:T(8,128)(2,1)S(1)} %bitcast.10, bf16[16,2176]{1,0:T(8,128)(2,1)S(1)} %norm_grad.1.refs_4_, ...), custom_call_target="tpu_custom_call" | custom-call | bytes 12000000 | tf_op jit(solution)/shard_map/merge_grad/pallas_call | solution.py:531
  (116 shorter events, 27.8 us)
Async XLA Ops:
  2.6 10.0 %collective-permute-start.3 = (bf16[592,128]{1,0:T(8,128)(2,1)}, bf16[592,128]{1,0:T(8,128)(2,1)S(1)}, u32[]{:S(2)}, u32[]{:S(2)}) collective-permute-start(bf16[592,128]{1,0:T(8,128)(2,1)} %pack.1), channel_id=1, source_target_pairs={{0,24},{4,28},{8,16},{12,20},{16,8},{20,12},{24,0},{28,4},{1,25},{... | collective-permute-start | bytes 454664 | tf_op jit(solution)/shard_map/ppermute | solution.py:577
  6.5 7.4 %collective-permute-start.2 = (bf16[592,128]{1,0:T(8,128)(2,1)}, bf16[592,128]{1,0:T(8,128)(2,1)S(1)}, u32[]{:S(2)}, u32[]{:S(2)}) collective-permute-start(bf16[592,128]{1,0:T(8,128)(2,1)} %pack.1), channel_id=1, source_target_pairs={{0,16},{4,20},{8,24},{12,28},{16,0},{20,4},{24,8},{28,12},{1,17},{... | collective-permute-start | bytes 454664 | tf_op jit(solution)/shard_map/ppermute | solution.py:577
  7.0 7.2 %collective-permute-start.1 = (bf16[592,128]{1,0:T(8,128)(2,1)}, bf16[592,128]{1,0:T(8,128)(2,1)S(1)}, u32[]{:S(2)}, u32[]{:S(2)}) collective-permute-start(bf16[592,128]{1,0:T(8,128)(2,1)} %pack.1), channel_id=1, source_target_pairs={{0,8},{4,12},{8,0},{12,4},{16,24},{20,28},{24,16},{28,20},{1,9},{5... | collective-permute-start | bytes 454664 | tf_op jit(solution)/shard_map/ppermute | solution.py:577
  7.2 10.5 %collective-permute-start = (bf16[592,128]{1,0:T(8,128)(2,1)}, bf16[592,128]{1,0:T(8,128)(2,1)S(1)}, u32[]{:S(2)}, u32[]{:S(2)}) collective-permute-start(bf16[592,128]{1,0:T(8,128)(2,1)} %pack.1), channel_id=1, source_target_pairs={{0,4},{4,0},{8,12},{12,8},{16,20},{20,16},{24,28},{28,24},{1,5},{5... | collective-permute-start | bytes 454664 | tf_op jit(solution)/shard_map/ppermute | solution.py:577
  14.2 7.8 %collective-permute-start.7 = (bf16[48,2048]{1,0:T(8,128)(2,1)S(1)}, bf16[48,2048]{1,0:T(8,128)(2,1)S(1)}, u32[]{:S(2)}, u32[]{:S(2)}) collective-permute-start(bf16[48,2048]{1,0:T(8,128)(2,1)S(1)} %get-tuple-element.70), channel_id=1, source_target_pairs={{0,8},{4,12},{8,0},{12,4},{16,24},{20,28},{24,16},{28,20},{1,9},{5... | collective-permute-start | bytes 589832 | tf_op jit(solution)/shard_map/ppermute | solution.py:577
  15.7 11.7 %collective-permute-start.8 = (bf16[48,2048]{1,0:T(8,128)(2,1)S(1)}, bf16[48,2048]{1,0:T(8,128)(2,1)S(1)}, u32[]{:S(2)}, u32[]{:S(2)}) collective-permute-start(bf16[48,2048]{1,0:T(8,128)(2,1)S(1)} %get-tuple-element.71), channel_id=1, source_target_pairs={{0,16},{4,20},{8,24},{12,28},{16,0},{20,4},{24,8},{28,12},{1,17},{... | collective-permute-start | bytes 589832 | tf_op jit(solution)/shard_map/ppermute | solution.py:577
  16.6 10.9 %collective-permute-start.9 = (bf16[48,2048]{1,0:T(8,128)(2,1)S(1)}, bf16[48,2048]{1,0:T(8,128)(2,1)S(1)}, u32[]{:S(2)}, u32[]{:S(2)}) collective-permute-start(bf16[48,2048]{1,0:T(8,128)(2,1)S(1)} %get-tuple-element.72), channel_id=1, source_target_pairs={{0,24},{4,28},{8,16},{12,20},{16,8},{20,12},{24,0},{28,4},{1,25},{... | collective-permute-start | bytes 589832 | tf_op jit(solution)/shard_map/ppermute | solution.py:577
  23.0 4.5 %collective-permute-start.10 = (bf16[8,2432]{1,0:T(8,128)(2,1)S(1)}, bf16[8,2432]{1,0:T(8,128)(2,1)S(1)}, u32[]{:S(2)}, u32[]{:S(2)}) collective-permute-start(bf16[8,2432]{1,0:T(8,128)(2,1)S(1)} %get-tuple-element.75), channel_id=1, source_target_pairs={{0,1},{1,0},{2,3},{3,2},{4,5},{5,4},{6,7},{7,6},{8,9},{9,8},{10,11... | collective-permute-start | bytes 116744 | tf_op jit(solution)/shard_map/ppermute | solution.py:577
  24.6 5.6 %collective-permute-start.11 = (bf16[8,2432]{1,0:T(8,128)(2,1)S(1)}, bf16[8,2432]{1,0:T(8,128)(2,1)S(1)}, u32[]{:S(2)}, u32[]{:S(2)}) collective-permute-start(bf16[8,2432]{1,0:T(8,128)(2,1)S(1)} %get-tuple-element.76), channel_id=1, source_target_pairs={{0,2},{1,3},{2,0},{3,1},{4,6},{5,7},{6,4},{7,5},{8,10},{9,11},{10,... | collective-permute-start | bytes 116744 | tf_op jit(solution)/shard_map/ppermute | solution.py:577
  27.2 5.8 %collective-permute-start.12 = (bf16[8,2432]{1,0:T(8,128)(2,1)S(1)}, bf16[8,2432]{1,0:T(8,128)(2,1)S(1)}, u32[]{:S(2)}, u32[]{:S(2)}) collective-permute-start(bf16[8,2432]{1,0:T(8,128)(2,1)S(1)} %get-tuple-element.77), channel_id=1, source_target_pairs={{0,3},{1,2},{2,1},{3,0},{4,7},{5,6},{6,5},{7,4},{8,11},{9,10},{10,... | collective-permute-start | bytes 116744 | tf_op jit(solution)/shard_map/ppermute | solution.py:577
  33.1 5.9 %collective-permute-start.15 = (bf16[8,2176]{1,0:T(8,128)(2,1)S(1)}, bf16[8,2176]{1,0:T(8,128)(2,1)S(1)}, u32[]{:S(2)}, u32[]{:S(2)}) collective-permute-start(bf16[8,2176]{1,0:T(8,128)(2,1)S(1)} %get-tuple-element.82.refs_0_), channel_id=1, source_target_pairs={{0,3},{1,2},{2,1},{3,0},{4,7},{5,6},{6,5},{7,4},{8,11},{9,10},{10,... | collective-permute-start | bytes 104456 | tf_op jit(solution)/shard_map/ppermute | solution.py:577
  33.9 5.7 %collective-permute-start.14 = (bf16[8,2176]{1,0:T(8,128)(2,1)S(1)}, bf16[8,2176]{1,0:T(8,128)(2,1)S(1)}, u32[]{:S(2)}, u32[]{:S(2)}) collective-permute-start(bf16[8,2176]{1,0:T(8,128)(2,1)S(1)} %get-tuple-element.82.refs_0_), channel_id=1, source_target_pairs={{0,2},{1,3},{2,0},{3,1},{4,6},{5,7},{6,4},{7,5},{8,10},{9,11},{10,... | collective-permute-start | bytes 104456 | tf_op jit(solution)/shard_map/ppermute | solution.py:577
  33.9 5.7 %collective-permute-start.13 = (bf16[8,2176]{1,0:T(8,128)(2,1)S(1)}, bf16[8,2176]{1,0:T(8,128)(2,1)S(1)}, u32[]{:S(2)}, u32[]{:S(2)}) collective-permute-start(bf16[8,2176]{1,0:T(8,128)(2,1)S(1)} %get-tuple-element.82.refs_0_), channel_id=1, source_target_pairs={{0,1},{1,0},{2,3},{3,2},{4,5},{5,4},{6,7},{7,6},{8,9},{9,8},{10,11... | collective-permute-start | bytes 104456 | tf_op jit(solution)/shard_map/ppermute | solution.py:577
  39.7 7.5 %collective-permute-start.20 = (bf16[32,2176]{1,0:T(8,128)(2,1)S(1)}, bf16[32,2176]{1,0:T(8,128)(2,1)S(1)}, u32[]{:S(2)}, u32[]{:S(2)}) collective-permute-start(bf16[32,2176]{1,0:T(8,128)(2,1)S(1)} %stack.1.refs_6_.refs_0_.rows_ref.refs_2_), channel_id=1, source_target_pairs={{0,24},{4,28},{8,16},{12,20},{16,8},{20,12},{24,0},{28,4},{1,25},{... | collective-permute-start | bytes 417800 | tf_op jit(solution)/shard_map/ppermute | solution.py:577
  41.6 8.1 %collective-permute-start.19 = (bf16[32,2176]{1,0:T(8,128)(2,1)S(1)}, bf16[32,2176]{1,0:T(8,128)(2,1)S(1)}, u32[]{:S(2)}, u32[]{:S(2)}) collective-permute-start(bf16[32,2176]{1,0:T(8,128)(2,1)S(1)} %stack.1.refs_6_.refs_0_.rows_ref.refs_2_), channel_id=1, source_target_pairs={{0,16},{4,20},{8,24},{12,28},{16,0},{20,4},{24,8},{28,12},{1,17},{... | collective-permute-start | bytes 417800 | tf_op jit(solution)/shard_map/ppermute | solution.py:577
  42.7 7.1 %collective-permute-start.18 = (bf16[32,2176]{1,0:T(8,128)(2,1)S(1)}, bf16[32,2176]{1,0:T(8,128)(2,1)S(1)}, u32[]{:S(2)}, u32[]{:S(2)}) collective-permute-start(bf16[32,2176]{1,0:T(8,128)(2,1)S(1)} %stack.1.refs_6_.refs_0_.rows_ref.refs_2_), channel_id=1, source_target_pairs={{0,8},{4,12},{8,0},{12,4},{16,24},{20,28},{24,16},{28,20},{1,9},{5... | collective-permute-start | bytes 417800 | tf_op jit(solution)/shard_map/ppermute | solution.py:577
  43.9 6.4 %collective-permute-start.17 = (bf16[32,2176]{1,0:T(8,128)(2,1)S(1)}, bf16[32,2176]{1,0:T(8,128)(2,1)S(1)}, u32[]{:S(2)}, u32[]{:S(2)}) collective-permute-start(bf16[32,2176]{1,0:T(8,128)(2,1)S(1)} %stack.1.refs_6_.refs_0_.rows_ref.refs_2_), channel_id=1, source_target_pairs={{0,4},{4,0},{8,12},{12,8},{16,20},{20,16},{24,28},{28,24},{1,5},{5... | collective-permute-start | bytes 417800 | tf_op jit(solution)/shard_map/ppermute | solution.py:577
  56.6 5.0 %collective-permute-start.24 = (bf16[24,2048]{1,0:T(8,128)(2,1)S(1)}, bf16[24,2048]{1,0:T(8,128)(2,1)S(1)}, u32[]{:S(2)}, u32[]{:S(2)}) collective-permute-start(bf16[24,2048]{1,0:T(8,128)(2,1)S(1)} %get-tuple-element.88), channel_id=1, source_target_pairs={{0,8},{4,12},{8,0},{12,4},{16,24},{20,28},{24,16},{28,20},{1,9},{5... | collective-permute-start | bytes 294920 | tf_op jit(solution)/shard_map/ppermute | solution.py:577
  58.1 6.8 %collective-permute-start.25 = (bf16[24,2048]{1,0:T(8,128)(2,1)S(1)}, bf16[24,2048]{1,0:T(8,128)(2,1)S(1)}, u32[]{:S(2)}, u32[]{:S(2)}) collective-permute-start(bf16[24,2048]{1,0:T(8,128)(2,1)S(1)} %get-tuple-element.89), channel_id=1, source_target_pairs={{0,16},{4,20},{8,24},{12,28},{16,0},{20,4},{24,8},{28,12},{1,17},{... | collective-permute-start | bytes 294920 | tf_op jit(solution)/shard_map/ppermute | solution.py:577
  58.9 6.0 %collective-permute-start.26 = (bf16[24,2048]{1,0:T(8,128)(2,1)S(1)}, bf16[24,2048]{1,0:T(8,128)(2,1)S(1)}, u32[]{:S(2)}, u32[]{:S(2)}) collective-permute-start(bf16[24,2048]{1,0:T(8,128)(2,1)S(1)} %get-tuple-element.90), channel_id=1, source_target_pairs={{0,24},{4,28},{8,16},{12,20},{16,8},{20,12},{24,0},{28,4},{1,25},{... | collective-permute-start | bytes 294920 | tf_op jit(solution)/shard_map/ppermute | solution.py:577
  65.0 7.1 %collective-permute-start.30 = (bf16[40,2048]{1,0:T(8,128)(2,1)S(1)}, bf16[40,2048]{1,0:T(8,128)(2,1)S(1)}, u32[]{:S(2)}, u32[]{:S(2)}) collective-permute-start(bf16[40,2048]{1,0:T(8,128)(2,1)S(1)} %get-tuple-element.100), channel_id=1, source_target_pairs={{0,8},{4,12},{8,0},{12,4},{16,24},{20,28},{24,16},{28,20},{1,9},{5... | collective-permute-start | bytes 491528 | tf_op jit(solution)/shard_map/ppermute | solution.py:577
  65.8 9.8 %collective-permute-start.31 = (bf16[40,2048]{1,0:T(8,128)(2,1)S(1)}, bf16[40,2048]{1,0:T(8,128)(2,1)S(1)}, u32[]{:S(2)}, u32[]{:S(2)}) collective-permute-start(bf16[40,2048]{1,0:T(8,128)(2,1)S(1)} %get-tuple-element.101), channel_id=1, source_target_pairs={{0,16},{4,20},{8,24},{12,28},{16,0},{20,4},{24,8},{28,12},{1,17},{... | collective-permute-start | bytes 491528 | tf_op jit(solution)/shard_map/ppermute | solution.py:577
  67.1 8.5 %collective-permute-start.32 = (bf16[40,2048]{1,0:T(8,128)(2,1)S(1)}, bf16[40,2048]{1,0:T(8,128)(2,1)S(1)}, u32[]{:S(2)}, u32[]{:S(2)}) collective-permute-start(bf16[40,2048]{1,0:T(8,128)(2,1)S(1)} %get-tuple-element.102), channel_id=1, source_target_pairs={{0,24},{4,28},{8,16},{12,20},{16,8},{20,12},{24,0},{28,4},{1,25},{... | collective-permute-start | bytes 491528 | tf_op jit(solution)/shard_map/ppermute | solution.py:577
  69.0 6.5 %collective-permute-start.33 = (bf16[32,2048]{1,0:T(8,128)(2,1)S(1)}, bf16[32,2048]{1,0:T(8,128)(2,1)S(1)}, u32[]{:S(2)}, u32[]{:S(2)}) collective-permute-start(bf16[32,2048]{1,0:T(8,128)(2,1)S(1)} %get-tuple-element.103), channel_id=1, source_target_pairs={{0,1},{1,0},{2,3},{3,2},{4,5},{5,4},{6,7},{7,6},{8,9},{9,8},{10,11... | collective-permute-start | bytes 393224 | tf_op jit(solution)/shard_map/ppermute | solution.py:577
  75.7 4.8 %collective-permute-start.34 = (bf16[16,2048]{1,0:T(8,128)(2,1)S(1)}, bf16[16,2048]{1,0:T(8,128)(2,1)S(1)}, u32[]{:S(2)}, u32[]{:S(2)}) collective-permute-start(bf16[16,2048]{1,0:T(8,128)(2,1)S(1)} %get-tuple-element.105), channel_id=1, source_target_pairs={{0,1},{1,0},{2,3},{3,2},{4,5},{5,4},{6,7},{7,6},{8,9},{9,8},{10,11... | collective-permute-start | bytes 196616 | tf_op jit(solution)/shard_map/ppermute | solution.py:577
  77.7 6.4 %collective-permute-start.29 = (bf16[32,2048]{1,0:T(8,128)(2,1)S(1)}, bf16[32,2048]{1,0:T(8,128)(2,1)S(1)}, u32[]{:S(2)}, u32[]{:S(2)}) collective-permute-start(bf16[32,2048]{1,0:T(8,128)(2,1)S(1)} %get-tuple-element.99), channel_id=1, source_target_pairs={{0,1},{1,0},{2,3},{3,2},{4,5},{5,4},{6,7},{7,6},{8,9},{9,8},{10,11... | collective-permute-start | bytes 393224 | tf_op jit(solution)/shard_map/ppermute | solution.py:577
  80.5 11.6 %collective-permute-start.35 = (bf16[24,2048]{1,0:T(8,128)(2,1)S(1)}, bf16[24,2048]{1,0:T(8,128)(2,1)S(1)}, u32[]{:S(2)}, u32[]{:S(2)}) collective-permute-start(bf16[24,2048]{1,0:T(8,128)(2,1)S(1)} %grad_join.1.joined_ref), channel_id=1, source_target_pairs={{0,2},{1,3},{2,0},{3,1},{4,6},{5,7},{6,4},{7,5},{8,10},{9,11},{10,... | collective-permute-start | bytes 294920 | tf_op jit(solution)/shard_map/ppermute | solution.py:577
  82.0 13.4 %collective-permute-start.36 = (bf16[32,2048]{1,0:T(8,128)(2,1)S(1)}, bf16[32,2048]{1,0:T(8,128)(2,1)S(1)}, u32[]{:S(2)}, u32[]{:S(2)}) collective-permute-start(bf16[32,2048]{1,0:T(8,128)(2,1)S(1)} %add_high.1.own_ref), channel_id=1, source_target_pairs={{0,2},{1,3},{2,0},{3,1},{4,6},{5,7},{6,4},{7,5},{8,10},{9,11},{10,... | collective-permute-start | bytes 393224 | tf_op jit(solution)/shard_map/ppermute | solution.py:577
  92.0 7.2 %collective-permute-start.38 = (bf16[32,2048]{1,0:T(8,128)(2,1)S(1)}, bf16[32,2048]{1,0:T(8,128)(2,1)S(1)}, u32[]{:S(2)}, u32[]{:S(2)}) collective-permute-start(bf16[32,2048]{1,0:T(8,128)(2,1)S(1)} %add_low.1.own_ref), channel_id=1, source_target_pairs={{0,2},{1,3},{2,0},{3,1},{4,6},{5,7},{6,4},{7,5},{8,10},{9,11},{10,... | collective-permute-start | bytes 393224 | tf_op jit(solution)/shard_map/ppermute | solution.py:577
  92.4 5.8 %collective-permute-start.39 = (bf16[16,2176]{1,0:T(8,128)(2,1)S(1)}, bf16[16,2176]{1,0:T(8,128)(2,1)S(1)}, u32[]{:S(2)}, u32[]{:S(2)}) collective-permute-start(bf16[16,2176]{1,0:T(8,128)(2,1)S(1)} %norm_grad.1.refs_4_), channel_id=1, source_target_pairs={{0,1},{1,0},{2,3},{3,2},{4,5},{5,4},{6,7},{7,6},{8,9},{9,8},{10,11... | collective-permute-start | bytes 208904 | tf_op jit(solution)/shard_map/ppermute | solution.py:577
  95.9 8.1 %collective-permute-start.37 = (bf16[32,2048]{1,0:T(8,128)(2,1)S(1)}, bf16[32,2048]{1,0:T(8,128)(2,1)S(1)}, u32[]{:S(2)}, u32[]{:S(2)}) collective-permute-start(bf16[32,2048]{1,0:T(8,128)(2,1)S(1)} %finish.2.refs_0_), channel_id=1, source_target_pairs={{0,1},{1,0},{2,3},{3,2},{4,5},{5,4},{6,7},{7,6},{8,9},{9,8},{10,11... | collective-permute-start | bytes 393224 | tf_op jit(solution)/shard_map/ppermute | solution.py:577
  99.7 5.0 %collective-permute-start.40 = (bf16[32,2048]{1,0:T(8,128)(2,1)S(1)}, bf16[32,2048]{1,0:T(8,128)(2,1)S(1)}, u32[]{:S(2)}, u32[]{:S(2)}) collective-permute-start(bf16[32,2048]{1,0:T(8,128)(2,1)S(1)} %finish.3.refs_2_), channel_id=1, source_target_pairs={{0,1},{1,0},{2,3},{3,2},{4,5},{5,4},{6,7},{7,6},{8,9},{9,8},{10,11... | collective-permute-start | bytes 393224 | tf_op jit(solution)/shard_map/ppermute | solution.py:577
  (28 other events, 295.4 us)

commit v4 on v3

--- a/solution.py
+++ b/solution.py
@@ -734,7 +734,8 @@
             far=range(2, 2 + len(gate)), cost=0.3, name=name,
         )
 
-    sum_high = add(high, arrived_high, grads[1:], "add_high")
+    sum_high = add(high, arrived_high, [], "add_high")
+    other_low = swap(sum_high, "expert", step)
     cot_rows, keep, sent = run(
         functools.partial(chip_sum_kernel, count=blocks // 2, order=halving_order(share)),
         [
@@ -755,8 +756,8 @@
         keep, swap(sent, "expert", bit), cot_rows, cost=0.2, name="grad_join",
     )
     other = swap(joined, "expert", share // 2)
-    sums = [add(low, arrived_low, [other], "add_low"), sum_high]
-    others = [swap(value, "expert", step) for value in sums][::-1]
+    sums = [add(low, arrived_low, [other_low], "add_low"), sum_high]
+    others = [other_low, swap(sums[0], "expert", step)]
     vision_grad = run(
         functools.partial(norm_grad_kernel, features=share * features),
         shape((2 * row_share, width + 128)),

time: 106 us -> 103 us (0.972)
  waiting for transfers between devices: 40.2 us -> 38.3 us
  starting transfers between devices: 40.9 us -> 39.7 us
    ppermute x41, waiting for transfers between devices: 40.2 us -> 38.3 us  [swap(): return lax.ppermute(value, axis, [(i, i ^ step) for i in range(count)])]
    ppermute x41, starting transfers between devices: 40.9 us -> 39.7 us  [swap(): return lax.ppermute(value, axis, [(i, i ^ step) for i in range(count)])]
  transfers between devices with their start and end apart: 41 -> 41, of which waited for: 24 -> 21; matrix products, arithmetic and copies ran while one was open for 0% -> 0% of each run, Pallas kernels for 11% -> 11%
where the time goes in v4:
time: 103 us; the launch traced here: 102 us
  starting transfers between devices  39.7 us (39%)
  waiting for transfers between devices  38.3 us (37%)
  Pallas kernels  19.2 us (19%)
  local copies, waits for them, and re-layouts  4.22 us (4%)
  between operations  1.03 us (1%)
    ppermute x41, starting transfers between devices, swap(): return lax.ppermute(value, axis, [(i, i ^ step) for i in range(count)])  39.7 us
    ppermute x41, waiting for transfers between devices, swap(): return lax.ppermute(value, axis, [(i, i ^ step) for i in range(count)])  38.3 us
    pallas_call x24, Pallas kernels, run(): pl.pallas_call(kernel, out_shape=outs, in_specs=specs, out_specs=jax.tree...  19.2 us
    unnamed x38, local copies, waits for them, and re-layouts  4.22 us
  transfers between devices with their start and end apart: 41, of which 21 were waited for; matrix products, arithmetic and copies ran while one was open for 0% of the time, Pallas kernels for 11%

profile of v4, /device:TPU:0, one launch (start us, length us, event | category | flops | bytes accessed | tf_op | source)
XLA Modules:
  0.0 102.4 jit_solution(10686351931475322399)
XLA Ops:
  0.7 1.8 %pack.1 = bf16[592,128]{1,0:T(8,128)(2,1)} custom-call(bf16[288,128]{1,0:T(8,128)(2,1)} %bitcast.11, bf16[288,128]{1,0:T(8,128)(2,1)} %bitcast.13, s32[1,32]{1,0:T(1,128)} %bitcast.22, s32[1,32]{1,0:T(1,128)} %bitcast.24, s32[8,128]{1,0:T(8,128)} %bitcast.18), custom_call_target="tpu_custom_call" | custom-call | bytes 3000000 | tf_op jit(solution)/shard_map/pack/pallas_call | solution.py:531
  2.6 4.0 %collective-permute-start.3 = (bf16[592,128]{1,0:T(8,128)(2,1)}, bf16[592,128]{1,0:T(8,128)(2,1)S(1)}, u32[]{:S(2)}, u32[]{:S(2)}) collective-permute-start(bf16[592,128]{1,0:T(8,128)(2,1)} %pack.1), channel_id=1, source_target_pairs={{0,24},{4,28},{8,16},{12,20},{16,8},{20,12},{24,0},{28,4},{1,25},{... | collective-permute-start | bytes 454664 | tf_op jit(solution)/shard_map/ppermute | solution.py:577
  12.6 1.4 %collective-permute-done.2.refs_1_ = bf16[592,128]{1,0:T(8,128)(2,1)S(1)} collective-permute-done((bf16[592,128]{1,0:T(8,128)(2,1)}, bf16[592,128]{1,0:T(8,128)(2,1)S(1)}, u32[]{:S(2)}, u32[]{:S(2)}) %collective-permute-start.2) | collective-permute-done | bytes 151584 | tf_op jit(solution)/shard_map/ppermute | solution.py:577
  14.2 1.5 %collective-permute-start.7 = (bf16[48,2048]{1,0:T(8,128)(2,1)S(1)}, bf16[48,2048]{1,0:T(8,128)(2,1)S(1)}, u32[]{:S(2)}, u32[]{:S(2)}) collective-permute-start(bf16[48,2048]{1,0:T(8,128)(2,1)S(1)} %get-tuple-element.70), channel_id=1, source_target_pairs={{0,8},{4,12},{8,0},{12,4},{16,24},{20,28},{24,16},{28,20},{1,9},{5... | collective-permute-start | bytes 589832 | tf_op jit(solution)/shard_map/ppermute | solution.py:577
  19.4 2.6 %attend.1 = (bf16[32,1152]{1,0:T(8,128)(2,1)S(1)}, bf16[128,128]{1,0:T(8,128)(2,1)S(1)}, bf16[48,1152]{1,0:T(8,128)(2,1)S(1)}, f32[32,128]{1,0:T(8,128)S(1)}) custom-call(bf16[4,72,128]{2,1,0:T(8,128)(2,1)S(1)} %copy-done.12, f32[4,288]{1,0:T(4,128)S(1)} %copy-done.15, bf16[288,128]{1,0:T(8,128)(2,1)S(1)} %bitcast.12, bf16[288,128]{1,0:T(8,128)(2,1)S(1)} %bitcast.14, ...), custom_call_target="tpu_custom_call" | custom-call | bytes 9000000 | tf_op jit(solution)/shard_map/attend/pallas_call | solution.py:531
  23.0 1.6 %collective-permute-start.10 = (bf16[8,2432]{1,0:T(8,128)(2,1)S(1)}, bf16[8,2432]{1,0:T(8,128)(2,1)S(1)}, u32[]{:S(2)}, u32[]{:S(2)}) collective-permute-start(bf16[8,2432]{1,0:T(8,128)(2,1)S(1)} %get-tuple-element.75), channel_id=1, source_target_pairs={{0,1},{1,0},{2,3},{3,2},{4,5},{5,4},{6,7},{7,6},{8,9},{9,8},{10,11... | collective-permute-start | bytes 116744 | tf_op jit(solution)/shard_map/ppermute | solution.py:577
  24.6 2.6 %collective-permute-start.11 = (bf16[8,2432]{1,0:T(8,128)(2,1)S(1)}, bf16[8,2432]{1,0:T(8,128)(2,1)S(1)}, u32[]{:S(2)}, u32[]{:S(2)}) collective-permute-start(bf16[8,2432]{1,0:T(8,128)(2,1)S(1)} %get-tuple-element.76), channel_id=1, source_target_pairs={{0,2},{1,3},{2,0},{3,1},{4,6},{5,7},{6,4},{7,5},{8,10},{9,11},{10,... | collective-permute-start | bytes 116744 | tf_op jit(solution)/shard_map/ppermute | solution.py:577
  27.4 2.8 %collective-permute-done.11.refs_4_.refs_2_ = bf16[8,2432]{1,0:T(8,128)(2,1)S(1)} collective-permute-done((bf16[8,2432]{1,0:T(8,128)(2,1)S(1)}, bf16[8,2432]{1,0:T(8,128)(2,1)S(1)}, u32[]{:S(2)}, u32[]{:S(2)}) %collective-permute-start.11) | collective-permute-done | bytes 38944 | tf_op jit(solution)/shard_map/ppermute | solution.py:577
  30.2 2.8 %collective-permute-done.12.refs_5_.refs_3_ = bf16[8,2432]{1,0:T(8,128)(2,1)S(1)} collective-permute-done((bf16[8,2432]{1,0:T(8,128)(2,1)S(1)}, bf16[8,2432]{1,0:T(8,128)(2,1)S(1)}, u32[]{:S(2)}, u32[]{:S(2)}) %collective-permute-start.12) | collective-permute-done | bytes 38944 | tf_op jit(solution)/shard_map/ppermute | solution.py:577
  33.9 3.7 %collective-permute-start.13 = (bf16[8,2176]{1,0:T(8,128)(2,1)S(1)}, bf16[8,2176]{1,0:T(8,128)(2,1)S(1)}, u32[]{:S(2)}, u32[]{:S(2)}) collective-permute-start(bf16[8,2176]{1,0:T(8,128)(2,1)S(1)} %get-tuple-element.82.refs_0_), channel_id=1, source_target_pairs={{0,1},{1,0},{2,3},{3,2},{4,5},{5,4},{6,7},{7,6},{8,9},{9,8},{10,11... | collective-permute-start | bytes 104456 | tf_op jit(solution)/shard_map/ppermute | solution.py:577
  37.6 1.4 %collective-permute-done.15.refs_6_.refs_3_ = bf16[8,2176]{1,0:T(8,128)(2,1)S(1)} collective-permute-done((bf16[8,2176]{1,0:T(8,128)(2,1)S(1)}, bf16[8,2176]{1,0:T(8,128)(2,1)S(1)}, u32[]{:S(2)}, u32[]{:S(2)}) %collective-permute-start.15) | collective-permute-done | bytes 34848 | tf_op jit(solution)/shard_map/ppermute | solution.py:577
  39.7 1.9 %collective-permute-start.20 = (bf16[32,2176]{1,0:T(8,128)(2,1)S(1)}, bf16[32,2176]{1,0:T(8,128)(2,1)S(1)}, u32[]{:S(2)}, u32[]{:S(2)}) collective-permute-start(bf16[32,2176]{1,0:T(8,128)(2,1)S(1)} %stack.1.refs_6_.refs_0_.rows_ref.refs_2_), channel_id=1, source_target_pairs={{0,24},{4,28},{8,16},{12,20},{16,8},{20,12},{24,0},{28,4},{1,25},{... | collective-permute-start | bytes 417800 | tf_op jit(solution)/shard_map/ppermute | solution.py:577
  44.0 1.3 %early.1 = (bf16[96,2048]{1,0:T(8,128)(2,1)S(1)}, f32[96,768]{1,0:T(8,128)S(1)}) custom-call(bf16[1,768,2048]{2,1,0:T(8,128)(2,1)S(1)} %copy-done.3, bf16[48,2048]{1,0:T(8,128)(2,1)S(1)} %get-tuple-element.69.refs_0_, bf16[48,2048]{1,0:T(8,128)(2,1)S(1)} %get-tuple-element.78._.refs_1_, bf16[48,2048]{1,0:T(8,128)(2,1)S(1)} %get-tuple-element.79.refs_2_, ...), custom_call_target="tpu_custom_call" | custom-call | bytes 9000000 | tf_op jit(solution)/shard_map/early/pallas_call | solution.py:531
  45.3 1.9 %collective-permute-done.20.refs_2_ = bf16[32,2176]{1,0:T(8,128)(2,1)S(1)} collective-permute-done((bf16[32,2176]{1,0:T(8,128)(2,1)S(1)}, bf16[32,2176]{1,0:T(8,128)(2,1)S(1)}, u32[]{:S(2)}, u32[]{:S(2)}) %collective-permute-start.20) | collective-permute-done | bytes 139296 | tf_op jit(solution)/shard_map/ppermute | solution.py:577
  47.2 2.5 %collective-permute-done.19.refs_1_ = bf16[32,2176]{1,0:T(8,128)(2,1)S(1)} collective-permute-done((bf16[32,2176]{1,0:T(8,128)(2,1)S(1)}, bf16[32,2176]{1,0:T(8,128)(2,1)S(1)}, u32[]{:S(2)}, u32[]{:S(2)}) %collective-permute-start.19) | collective-permute-done | bytes 139296 | tf_op jit(solution)/shard_map/ppermute | solution.py:577
  51.7 3.2 %forward.1 = (f32[96,768]{1,0:T(8,128)S(1)}, f32[96,768]{1,0:T(8,128)S(1)}, bf16[24,2048]{1,0:T(8,128)(2,1)S(1)}, bf16[24,2048]{1,0:T(8,128)(2,1)S(1)}, bf16[24,...) custom-call(bf16[96,256]{1,0:T(8,128)(2,1)S(1)} %get-tuple-element.68.refs_4_.refs_0_.slots_ref, ...), custom_call_target="tpu_custom_call" | custom-call | bytes 12000000 | tf_op jit(solution)/shard_map/forward/pallas_call | solution.py:531
  54.9 1.5 %backward.1 = (bf16[160,2048]{1,0:T(8,128)(2,1)S(1)}, bf16[160,2048]{1,0:T(8,128)(2,1)S(1)}) custom-call(bf16[96,256]{1,0:T(8,128)(2,1)S(1)} %get-tuple-element.68.refs_4_.refs_0_.slots_ref, f32[96,768]{1,0:T(8,128)S(1)} %get-tuple-element.91.grad_ref, f32[96,768]{1,0:T(8,128)S(1)} %get-tuple-element.92.gate_in, f32[96,768]{1,0:T(8,128)S(1)} %get-tuple-element.93.up_in, ...), custom_call_target="tpu_custom_call" | custom-call | bytes 12000000 | tf_op jit(solution)/shard_map/backward/pallas_call | solution.py:531
  56.6 1.4 %collective-permute-start.24 = (bf16[24,2048]{1,0:T(8,128)(2,1)S(1)}, bf16[24,2048]{1,0:T(8,128)(2,1)S(1)}, u32[]{:S(2)}, u32[]{:S(2)}) collective-permute-start(bf16[24,2048]{1,0:T(8,128)(2,1)S(1)} %get-tuple-element.88), channel_id=1, source_target_pairs={{0,8},{4,12},{8,0},{12,4},{16,24},{20,28},{24,16},{28,20},{1,9},{5... | collective-permute-start | bytes 294920 | tf_op jit(solution)/shard_map/ppermute | solution.py:577
  60.3 1.4 %collective-permute-done.24.refs_1_ = bf16[24,2048]{1,0:T(8,128)(2,1)S(1)} collective-permute-done((bf16[24,2048]{1,0:T(8,128)(2,1)S(1)}, bf16[24,2048]{1,0:T(8,128)(2,1)S(1)}, u32[]{:S(2)}, u32[]{:S(2)}) %collective-permute-start.24) | collective-permute-done | bytes 98336 | tf_op jit(solution)/shard_map/ppermute | solution.py:577
  61.6 3.2 %collective-permute-done.25.refs_2_ = bf16[24,2048]{1,0:T(8,128)(2,1)S(1)} collective-permute-done((bf16[24,2048]{1,0:T(8,128)(2,1)S(1)}, bf16[24,2048]{1,0:T(8,128)(2,1)S(1)}, u32[]{:S(2)}, u32[]{:S(2)}) %collective-permute-start.25) | collective-permute-done | bytes 98336 | tf_op jit(solution)/shard_map/ppermute | solution.py:577
  65.8 1.3 %collective-permute-start.33 = (bf16[40,2048]{1,0:T(8,128)(2,1)S(1)}, bf16[40,2048]{1,0:T(8,128)(2,1)S(1)}, u32[]{:S(2)}, u32[]{:S(2)}) collective-permute-start(bf16[40,2048]{1,0:T(8,128)(2,1)S(1)} %get-tuple-element.103), channel_id=1, source_target_pairs={{0,16},{4,20},{8,24},{12,28},{16,0},{20,4},{24,8},{28,12},{1,17},{... | collective-permute-start | bytes 491528 | tf_op jit(solution)/shard_map/ppermute | solution.py:577
  67.1 1.4 %collective-permute-start.34 = (bf16[40,2048]{1,0:T(8,128)(2,1)S(1)}, bf16[40,2048]{1,0:T(8,128)(2,1)S(1)}, u32[]{:S(2)}, u32[]{:S(2)}) collective-permute-start(bf16[40,2048]{1,0:T(8,128)(2,1)S(1)} %get-tuple-element.104), channel_id=1, source_target_pairs={{0,24},{4,28},{8,16},{12,20},{16,8},{20,12},{24,0},{28,4},{1,25},{... | collective-permute-start | bytes 491528 | tf_op jit(solution)/shard_map/ppermute | solution.py:577
  69.0 2.1 %collective-permute-start.30 = (bf16[32,2048]{1,0:T(8,128)(2,1)S(1)}, bf16[32,2048]{1,0:T(8,128)(2,1)S(1)}, u32[]{:S(2)}, u32[]{:S(2)}) collective-permute-start(bf16[32,2048]{1,0:T(8,128)(2,1)S(1)} %get-tuple-element.101), channel_id=1, source_target_pairs={{0,1},{1,0},{2,3},{3,2},{4,5},{5,4},{6,7},{7,6},{8,9},{9,8},{10,11... | collective-permute-start | bytes 393224 | tf_op jit(solution)/shard_map/ppermute | solution.py:577
  71.2 4.3 %collective-permute-done.30.arrived_ref.refs_4_ = bf16[32,2048]{1,0:T(8,128)(2,1)S(1)} collective-permute-done((bf16[32,2048]{1,0:T(8,128)(2,1)S(1)}, bf16[32,2048]{1,0:T(8,128)(2,1)S(1)}, u32[]{:S(2)}, u32[]{:S(2)}) %collective-permute-start.30) | collective-permute-done | bytes 131104 | tf_op jit(solution)/shard_map/ppermute | solution.py:577
  76.9 1.8 %collective-permute-start.35 = (bf16[16,2048]{1,0:T(8,128)(2,1)S(1)}, bf16[16,2048]{1,0:T(8,128)(2,1)S(1)}, u32[]{:S(2)}, u32[]{:S(2)}) collective-permute-start(bf16[16,2048]{1,0:T(8,128)(2,1)S(1)} %get-tuple-element.106), channel_id=1, source_target_pairs={{0,1},{1,0},{2,3},{3,2},{4,5},{5,4},{6,7},{7,6},{8,9},{9,8},{10,11... | collective-permute-start | bytes 196616 | tf_op jit(solution)/shard_map/ppermute | solution.py:577
  78.7 3.5 %collective-permute-done.35.arrived_ref = bf16[16,2048]{1,0:T(8,128)(2,1)S(1)} collective-permute-done((bf16[16,2048]{1,0:T(8,128)(2,1)S(1)}, bf16[16,2048]{1,0:T(8,128)(2,1)S(1)}, u32[]{:S(2)}, u32[]{:S(2)}) %collective-permute-start.35) | collective-permute-done | bytes 65568 | tf_op jit(solution)/shard_map/ppermute | solution.py:577
  82.2 2.1 %collective-permute-start.36 = (bf16[24,2048]{1,0:T(8,128)(2,1)S(1)}, bf16[24,2048]{1,0:T(8,128)(2,1)S(1)}, u32[]{:S(2)}, u32[]{:S(2)}) collective-permute-start(bf16[24,2048]{1,0:T(8,128)(2,1)S(1)} %grad_join.1.joined_ref), channel_id=1, source_target_pairs={{0,2},{1,3},{2,0},{3,1},{4,6},{5,7},{6,4},{7,5},{8,10},{9,11},{10,... | collective-permute-start | bytes 294920 | tf_op jit(solution)/shard_map/ppermute | solution.py:577
  85.3 6.2 %collective-permute-done.36.refs_8_.other_ref = bf16[24,2048]{1,0:T(8,128)(2,1)S(1)} collective-permute-done((bf16[24,2048]{1,0:T(8,128)(2,1)S(1)}, bf16[24,2048]{1,0:T(8,128)(2,1)S(1)}, u32[]{:S(2)}, u32[]{:S(2)}) %collective-permute-start.36) | collective-permute-done | bytes 98336 | tf_op jit(solution)/shard_map/ppermute | solution.py:577
  92.3 2.1 %collective-permute-start.37 = (bf16[32,2048]{1,0:T(8,128)(2,1)S(1)}, bf16[32,2048]{1,0:T(8,128)(2,1)S(1)}, u32[]{:S(2)}, u32[]{:S(2)}) collective-permute-start(bf16[32,2048]{1,0:T(8,128)(2,1)S(1)} %finish.2.refs_0_), channel_id=1, source_target_pairs={{0,1},{1,0},{2,3},{3,2},{4,5},{5,4},{6,7},{7,6},{8,9},{9,8},{10,11... | collective-permute-start | bytes 393224 | tf_op jit(solution)/shard_map/ppermute | solution.py:577
  94.3 1.7 %collective-permute-done.39.refs_8_.refs_5_ = bf16[16,2176]{1,0:T(8,128)(2,1)S(1)} collective-permute-done((bf16[16,2176]{1,0:T(8,128)(2,1)S(1)}, bf16[16,2176]{1,0:T(8,128)(2,1)S(1)}, u32[]{:S(2)}, u32[]{:S(2)}) %collective-permute-start.39) | collective-permute-done | bytes 69664 | tf_op jit(solution)/shard_map/ppermute | solution.py:577
  96.7 3.0 %merge_grad.1 = f32[288,128]{1,0:T(8,128)} custom-call(f32[4,288]{1,0:T(4,128)S(1)} %copy-done.15, bf16[32,1152]{1,0:T(8,128)(2,1)S(1)} %get-tuple-element.109.refs_1_, bf16[32,2176]{1,0:T(8,128)(2,1)S(1)} %stack.1.refs_6_.refs_0_.rows_ref.refs_2_, bf16[1152,2048]{1,0:T(8,128)(2,1)S(1)} %bitcast.10, bf16[16,2176]{1,0:T(8,128)(2,1)S(1)} %norm_grad.1.refs_4_, ...), custom_call_target="tpu_custom_call" | custom-call | bytes 12000000 | tf_op jit(solution)/shard_map/merge_grad/pallas_call | solution.py:531
  99.7 1.9 %collective-permute-done.40.refs_3_ = bf16[32,2048]{1,0:T(8,128)(2,1)S(1)} collective-permute-done((bf16[32,2048]{1,0:T(8,128)(2,1)S(1)}, bf16[32,2048]{1,0:T(8,128)(2,1)S(1)}, u32[]{:S(2)}, u32[]{:S(2)}) %collective-permute-start.40) | collective-permute-done | bytes 131104 | tf_op jit(solution)/shard_map/ppermute | solution.py:577
  (116 shorter events, 25.6 us)
Async XLA Ops:
  2.6 10.0 %collective-permute-start.3 = (bf16[592,128]{1,0:T(8,128)(2,1)}, bf16[592,128]{1,0:T(8,128)(2,1)S(1)}, u32[]{:S(2)}, u32[]{:S(2)}) collective-permute-start(bf16[592,128]{1,0:T(8,128)(2,1)} %pack.1), channel_id=1, source_target_pairs={{0,24},{4,28},{8,16},{12,20},{16,8},{20,12},{24,0},{28,4},{1,25},{... | collective-permute-start | bytes 454664 | tf_op jit(solution)/shard_map/ppermute | solution.py:577
  6.5 7.4 %collective-permute-start.2 = (bf16[592,128]{1,0:T(8,128)(2,1)}, bf16[592,128]{1,0:T(8,128)(2,1)S(1)}, u32[]{:S(2)}, u32[]{:S(2)}) collective-permute-start(bf16[592,128]{1,0:T(8,128)(2,1)} %pack.1), channel_id=1, source_target_pairs={{0,16},{4,20},{8,24},{12,28},{16,0},{20,4},{24,8},{28,12},{1,17},{... | collective-permute-start | bytes 454664 | tf_op jit(solution)/shard_map/ppermute | solution.py:577
  7.0 7.2 %collective-permute-start.1 = (bf16[592,128]{1,0:T(8,128)(2,1)}, bf16[592,128]{1,0:T(8,128)(2,1)S(1)}, u32[]{:S(2)}, u32[]{:S(2)}) collective-permute-start(bf16[592,128]{1,0:T(8,128)(2,1)} %pack.1), channel_id=1, source_target_pairs={{0,8},{4,12},{8,0},{12,4},{16,24},{20,28},{24,16},{28,20},{1,9},{5... | collective-permute-start | bytes 454664 | tf_op jit(solution)/shard_map/ppermute | solution.py:577
  7.2 10.5 %collective-permute-start = (bf16[592,128]{1,0:T(8,128)(2,1)}, bf16[592,128]{1,0:T(8,128)(2,1)S(1)}, u32[]{:S(2)}, u32[]{:S(2)}) collective-permute-start(bf16[592,128]{1,0:T(8,128)(2,1)} %pack.1), channel_id=1, source_target_pairs={{0,4},{4,0},{8,12},{12,8},{16,20},{20,16},{24,28},{28,24},{1,5},{5... | collective-permute-start | bytes 454664 | tf_op jit(solution)/shard_map/ppermute | solution.py:577
  14.2 7.8 %collective-permute-start.7 = (bf16[48,2048]{1,0:T(8,128)(2,1)S(1)}, bf16[48,2048]{1,0:T(8,128)(2,1)S(1)}, u32[]{:S(2)}, u32[]{:S(2)}) collective-permute-start(bf16[48,2048]{1,0:T(8,128)(2,1)S(1)} %get-tuple-element.70), channel_id=1, source_target_pairs={{0,8},{4,12},{8,0},{12,4},{16,24},{20,28},{24,16},{28,20},{1,9},{5... | collective-permute-start | bytes 589832 | tf_op jit(solution)/shard_map/ppermute | solution.py:577
  15.7 11.7 %collective-permute-start.8 = (bf16[48,2048]{1,0:T(8,128)(2,1)S(1)}, bf16[48,2048]{1,0:T(8,128)(2,1)S(1)}, u32[]{:S(2)}, u32[]{:S(2)}) collective-permute-start(bf16[48,2048]{1,0:T(8,128)(2,1)S(1)} %get-tuple-element.71), channel_id=1, source_target_pairs={{0,16},{4,20},{8,24},{12,28},{16,0},{20,4},{24,8},{28,12},{1,17},{... | collective-permute-start | bytes 589832 | tf_op jit(solution)/shard_map/ppermute | solution.py:577
  16.6 10.9 %collective-permute-start.9 = (bf16[48,2048]{1,0:T(8,128)(2,1)S(1)}, bf16[48,2048]{1,0:T(8,128)(2,1)S(1)}, u32[]{:S(2)}, u32[]{:S(2)}) collective-permute-start(bf16[48,2048]{1,0:T(8,128)(2,1)S(1)} %get-tuple-element.72), channel_id=1, source_target_pairs={{0,24},{4,28},{8,16},{12,20},{16,8},{20,12},{24,0},{28,4},{1,25},{... | collective-permute-start | bytes 589832 | tf_op jit(solution)/shard_map/ppermute | solution.py:577
  23.0 4.5 %collective-permute-start.10 = (bf16[8,2432]{1,0:T(8,128)(2,1)S(1)}, bf16[8,2432]{1,0:T(8,128)(2,1)S(1)}, u32[]{:S(2)}, u32[]{:S(2)}) collective-permute-start(bf16[8,2432]{1,0:T(8,128)(2,1)S(1)} %get-tuple-element.75), channel_id=1, source_target_pairs={{0,1},{1,0},{2,3},{3,2},{4,5},{5,4},{6,7},{7,6},{8,9},{9,8},{10,11... | collective-permute-start | bytes 116744 | tf_op jit(solution)/shard_map/ppermute | solution.py:577
  24.6 5.6 %collective-permute-start.11 = (bf16[8,2432]{1,0:T(8,128)(2,1)S(1)}, bf16[8,2432]{1,0:T(8,128)(2,1)S(1)}, u32[]{:S(2)}, u32[]{:S(2)}) collective-permute-start(bf16[8,2432]{1,0:T(8,128)(2,1)S(1)} %get-tuple-element.76), channel_id=1, source_target_pairs={{0,2},{1,3},{2,0},{3,1},{4,6},{5,7},{6,4},{7,5},{8,10},{9,11},{10,... | collective-permute-start | bytes 116744 | tf_op jit(solution)/shard_map/ppermute | solution.py:577
  27.2 5.8 %collective-permute-start.12 = (bf16[8,2432]{1,0:T(8,128)(2,1)S(1)}, bf16[8,2432]{1,0:T(8,128)(2,1)S(1)}, u32[]{:S(2)}, u32[]{:S(2)}) collective-permute-start(bf16[8,2432]{1,0:T(8,128)(2,1)S(1)} %get-tuple-element.77), channel_id=1, source_target_pairs={{0,3},{1,2},{2,1},{3,0},{4,7},{5,6},{6,5},{7,4},{8,11},{9,10},{10,... | collective-permute-start | bytes 116744 | tf_op jit(solution)/shard_map/ppermute | solution.py:577
  33.1 5.9 %collective-permute-start.15 = (bf16[8,2176]{1,0:T(8,128)(2,1)S(1)}, bf16[8,2176]{1,0:T(8,128)(2,1)S(1)}, u32[]{:S(2)}, u32[]{:S(2)}) collective-permute-start(bf16[8,2176]{1,0:T(8,128)(2,1)S(1)} %get-tuple-element.82.refs_0_), channel_id=1, source_target_pairs={{0,3},{1,2},{2,1},{3,0},{4,7},{5,6},{6,5},{7,4},{8,11},{9,10},{10,... | collective-permute-start | bytes 104456 | tf_op jit(solution)/shard_map/ppermute | solution.py:577
  33.9 5.7 %collective-permute-start.14 = (bf16[8,2176]{1,0:T(8,128)(2,1)S(1)}, bf16[8,2176]{1,0:T(8,128)(2,1)S(1)}, u32[]{:S(2)}, u32[]{:S(2)}) collective-permute-start(bf16[8,2176]{1,0:T(8,128)(2,1)S(1)} %get-tuple-element.82.refs_0_), channel_id=1, source_target_pairs={{0,2},{1,3},{2,0},{3,1},{4,6},{5,7},{6,4},{7,5},{8,10},{9,11},{10,... | collective-permute-start | bytes 104456 | tf_op jit(solution)/shard_map/ppermute | solution.py:577
  33.9 5.7 %collective-permute-start.13 = (bf16[8,2176]{1,0:T(8,128)(2,1)S(1)}, bf16[8,2176]{1,0:T(8,128)(2,1)S(1)}, u32[]{:S(2)}, u32[]{:S(2)}) collective-permute-start(bf16[8,2176]{1,0:T(8,128)(2,1)S(1)} %get-tuple-element.82.refs_0_), channel_id=1, source_target_pairs={{0,1},{1,0},{2,3},{3,2},{4,5},{5,4},{6,7},{7,6},{8,9},{9,8},{10,11... | collective-permute-start | bytes 104456 | tf_op jit(solution)/shard_map/ppermute | solution.py:577
  39.6 4.4 %collective-permute-start.16 = (bf16[96,2048]{1,0:T(8,128)(2,1)S(1)}, bf16[96,2048]{1,0:T(8,128)(2,1)S(1)}, u32[]{:S(2)}, u32[]{:S(2)}) collective-permute-start(bf16[96,2048]{1,0:T(8,128)(2,1)S(1)} %early_half.1), channel_id=1, source_target_pairs={{0,4},{4,0},{8,12},{12,8},{16,20},{20,16},{24,28},{28,24},{1,5},{5... | collective-permute-start | bytes 1179656 | tf_op jit(solution)/shard_map/ppermute | solution.py:577
  39.7 7.5 %collective-permute-start.20 = (bf16[32,2176]{1,0:T(8,128)(2,1)S(1)}, bf16[32,2176]{1,0:T(8,128)(2,1)S(1)}, u32[]{:S(2)}, u32[]{:S(2)}) collective-permute-start(bf16[32,2176]{1,0:T(8,128)(2,1)S(1)} %stack.1.refs_6_.refs_0_.rows_ref.refs_2_), channel_id=1, source_target_pairs={{0,24},{4,28},{8,16},{12,20},{16,8},{20,12},{24,0},{28,4},{1,25},{... | collective-permute-start | bytes 417800 | tf_op jit(solution)/shard_map/ppermute | solution.py:577
  41.6 8.1 %collective-permute-start.19 = (bf16[32,2176]{1,0:T(8,128)(2,1)S(1)}, bf16[32,2176]{1,0:T(8,128)(2,1)S(1)}, u32[]{:S(2)}, u32[]{:S(2)}) collective-permute-start(bf16[32,2176]{1,0:T(8,128)(2,1)S(1)} %stack.1.refs_6_.refs_0_.rows_ref.refs_2_), channel_id=1, source_target_pairs={{0,16},{4,20},{8,24},{12,28},{16,0},{20,4},{24,8},{28,12},{1,17},{... | collective-permute-start | bytes 417800 | tf_op jit(solution)/shard_map/ppermute | solution.py:577
  42.7 7.1 %collective-permute-start.18 = (bf16[32,2176]{1,0:T(8,128)(2,1)S(1)}, bf16[32,2176]{1,0:T(8,128)(2,1)S(1)}, u32[]{:S(2)}, u32[]{:S(2)}) collective-permute-start(bf16[32,2176]{1,0:T(8,128)(2,1)S(1)} %stack.1.refs_6_.refs_0_.rows_ref.refs_2_), channel_id=1, source_target_pairs={{0,8},{4,12},{8,0},{12,4},{16,24},{20,28},{24,16},{28,20},{1,9},{5... | collective-permute-start | bytes 417800 | tf_op jit(solution)/shard_map/ppermute | solution.py:577
  43.9 6.4 %collective-permute-start.17 = (bf16[32,2176]{1,0:T(8,128)(2,1)S(1)}, bf16[32,2176]{1,0:T(8,128)(2,1)S(1)}, u32[]{:S(2)}, u32[]{:S(2)}) collective-permute-start(bf16[32,2176]{1,0:T(8,128)(2,1)S(1)} %stack.1.refs_6_.refs_0_.rows_ref.refs_2_), channel_id=1, source_target_pairs={{0,4},{4,0},{8,12},{12,8},{16,20},{20,16},{24,28},{28,24},{1,5},{5... | collective-permute-start | bytes 417800 | tf_op jit(solution)/shard_map/ppermute | solution.py:577
  56.6 5.0 %collective-permute-start.24 = (bf16[24,2048]{1,0:T(8,128)(2,1)S(1)}, bf16[24,2048]{1,0:T(8,128)(2,1)S(1)}, u32[]{:S(2)}, u32[]{:S(2)}) collective-permute-start(bf16[24,2048]{1,0:T(8,128)(2,1)S(1)} %get-tuple-element.88), channel_id=1, source_target_pairs={{0,8},{4,12},{8,0},{12,4},{16,24},{20,28},{24,16},{28,20},{1,9},{5... | collective-permute-start | bytes 294920 | tf_op jit(solution)/shard_map/ppermute | solution.py:577
  58.1 6.8 %collective-permute-start.25 = (bf16[24,2048]{1,0:T(8,128)(2,1)S(1)}, bf16[24,2048]{1,0:T(8,128)(2,1)S(1)}, u32[]{:S(2)}, u32[]{:S(2)}) collective-permute-start(bf16[24,2048]{1,0:T(8,128)(2,1)S(1)} %get-tuple-element.89), channel_id=1, source_target_pairs={{0,16},{4,20},{8,24},{12,28},{16,0},{20,4},{24,8},{28,12},{1,17},{... | collective-permute-start | bytes 294920 | tf_op jit(solution)/shard_map/ppermute | solution.py:577
  58.9 6.0 %collective-permute-start.26 = (bf16[24,2048]{1,0:T(8,128)(2,1)S(1)}, bf16[24,2048]{1,0:T(8,128)(2,1)S(1)}, u32[]{:S(2)}, u32[]{:S(2)}) collective-permute-start(bf16[24,2048]{1,0:T(8,128)(2,1)S(1)} %get-tuple-element.90), channel_id=1, source_target_pairs={{0,24},{4,28},{8,16},{12,20},{16,8},{20,12},{24,0},{28,4},{1,25},{... | collective-permute-start | bytes 294920 | tf_op jit(solution)/shard_map/ppermute | solution.py:577
  65.0 11.7 %collective-permute-start.32 = (bf16[40,2048]{1,0:T(8,128)(2,1)S(1)}, bf16[40,2048]{1,0:T(8,128)(2,1)S(1)}, u32[]{:S(2)}, u32[]{:S(2)}) collective-permute-start(bf16[40,2048]{1,0:T(8,128)(2,1)S(1)} %get-tuple-element.102), channel_id=1, source_target_pairs={{0,8},{4,12},{8,0},{12,4},{16,24},{20,28},{24,16},{28,20},{1,9},{5... | collective-permute-start | bytes 491528 | tf_op jit(solution)/shard_map/ppermute | solution.py:577
  65.8 11.0 %collective-permute-start.33 = (bf16[40,2048]{1,0:T(8,128)(2,1)S(1)}, bf16[40,2048]{1,0:T(8,128)(2,1)S(1)}, u32[]{:S(2)}, u32[]{:S(2)}) collective-permute-start(bf16[40,2048]{1,0:T(8,128)(2,1)S(1)} %get-tuple-element.103), channel_id=1, source_target_pairs={{0,16},{4,20},{8,24},{12,28},{16,0},{20,4},{24,8},{28,12},{1,17},{... | collective-permute-start | bytes 491528 | tf_op jit(solution)/shard_map/ppermute | solution.py:577
  67.1 9.6 %collective-permute-start.34 = (bf16[40,2048]{1,0:T(8,128)(2,1)S(1)}, bf16[40,2048]{1,0:T(8,128)(2,1)S(1)}, u32[]{:S(2)}, u32[]{:S(2)}) collective-permute-start(bf16[40,2048]{1,0:T(8,128)(2,1)S(1)} %get-tuple-element.104), channel_id=1, source_target_pairs={{0,24},{4,28},{8,16},{12,20},{16,8},{20,12},{24,0},{28,4},{1,25},{... | collective-permute-start | bytes 491528 | tf_op jit(solution)/shard_map/ppermute | solution.py:577
  69.0 6.4 %collective-permute-start.30 = (bf16[32,2048]{1,0:T(8,128)(2,1)S(1)}, bf16[32,2048]{1,0:T(8,128)(2,1)S(1)}, u32[]{:S(2)}, u32[]{:S(2)}) collective-permute-start(bf16[32,2048]{1,0:T(8,128)(2,1)S(1)} %get-tuple-element.101), channel_id=1, source_target_pairs={{0,1},{1,0},{2,3},{3,2},{4,5},{5,4},{6,7},{7,6},{8,9},{9,8},{10,11... | collective-permute-start | bytes 393224 | tf_op jit(solution)/shard_map/ppermute | solution.py:577
  71.1 13.2 %collective-permute-start.29 = (bf16[32,2048]{1,0:T(8,128)(2,1)S(1)}, bf16[32,2048]{1,0:T(8,128)(2,1)S(1)}, u32[]{:S(2)}, u32[]{:S(2)}) collective-permute-start(bf16[32,2048]{1,0:T(8,128)(2,1)S(1)} %get-tuple-element.99), channel_id=1, source_target_pairs={{0,1},{1,0},{2,3},{3,2},{4,5},{5,4},{6,7},{7,6},{8,9},{9,8},{10,11... | collective-permute-start | bytes 393224 | tf_op jit(solution)/shard_map/ppermute | solution.py:577
  75.5 8.8 %collective-permute-start.31 = (bf16[32,2048]{1,0:T(8,128)(2,1)S(1)}, bf16[32,2048]{1,0:T(8,128)(2,1)S(1)}, u32[]{:S(2)}, u32[]{:S(2)}) collective-permute-start(bf16[32,2048]{1,0:T(8,128)(2,1)S(1)} %add_high.1.own_ref), channel_id=1, source_target_pairs={{0,2},{1,3},{2,0},{3,1},{4,6},{5,7},{6,4},{7,5},{8,10},{9,11},{10,... | collective-permute-start | bytes 393224 | tf_op jit(solution)/shard_map/ppermute | solution.py:577
  76.9 5.3 %collective-permute-start.35 = (bf16[16,2048]{1,0:T(8,128)(2,1)S(1)}, bf16[16,2048]{1,0:T(8,128)(2,1)S(1)}, u32[]{:S(2)}, u32[]{:S(2)}) collective-permute-start(bf16[16,2048]{1,0:T(8,128)(2,1)S(1)} %get-tuple-element.106), channel_id=1, source_target_pairs={{0,1},{1,0},{2,3},{3,2},{4,5},{5,4},{6,7},{7,6},{8,9},{9,8},{10,11... | collective-permute-start | bytes 196616 | tf_op jit(solution)/shard_map/ppermute | solution.py:577
  82.2 9.3 %collective-permute-start.36 = (bf16[24,2048]{1,0:T(8,128)(2,1)S(1)}, bf16[24,2048]{1,0:T(8,128)(2,1)S(1)}, u32[]{:S(2)}, u32[]{:S(2)}) collective-permute-start(bf16[24,2048]{1,0:T(8,128)(2,1)S(1)} %grad_join.1.joined_ref), channel_id=1, source_target_pairs={{0,2},{1,3},{2,0},{3,1},{4,6},{5,7},{6,4},{7,5},{8,10},{9,11},{10,... | collective-permute-start | bytes 294920 | tf_op jit(solution)/shard_map/ppermute | solution.py:577
  84.3 11.8 %collective-permute-start.38 = (bf16[32,2048]{1,0:T(8,128)(2,1)S(1)}, bf16[32,2048]{1,0:T(8,128)(2,1)S(1)}, u32[]{:S(2)}, u32[]{:S(2)}) collective-permute-start(bf16[32,2048]{1,0:T(8,128)(2,1)S(1)} %add_low.1.own_ref), channel_id=1, source_target_pairs={{0,2},{1,3},{2,0},{3,1},{4,6},{5,7},{6,4},{7,5},{8,10},{9,11},{10,... | collective-permute-start | bytes 393224 | tf_op jit(solution)/shard_map/ppermute | solution.py:577
  92.3 7.4 %collective-permute-start.37 = (bf16[32,2048]{1,0:T(8,128)(2,1)S(1)}, bf16[32,2048]{1,0:T(8,128)(2,1)S(1)}, u32[]{:S(2)}, u32[]{:S(2)}) collective-permute-start(bf16[32,2048]{1,0:T(8,128)(2,1)S(1)} %finish.2.refs_0_), channel_id=1, source_target_pairs={{0,1},{1,0},{2,3},{3,2},{4,5},{5,4},{6,7},{7,6},{8,9},{9,8},{10,11... | collective-permute-start | bytes 393224 | tf_op jit(solution)/shard_map/ppermute | solution.py:577
  96.6 5.0 %collective-permute-start.40 = (bf16[32,2048]{1,0:T(8,128)(2,1)S(1)}, bf16[32,2048]{1,0:T(8,128)(2,1)S(1)}, u32[]{:S(2)}, u32[]{:S(2)}) collective-permute-start(bf16[32,2048]{1,0:T(8,128)(2,1)S(1)} %finish.3.refs_2_), channel_id=1, source_target_pairs={{0,1},{1,0},{2,3},{3,2},{4,5},{5,4},{6,7},{7,6},{8,9},{9,8},{10,11... | collective-permute-start | bytes 393224 | tf_op jit(solution)/shard_map/ppermute | solution.py:577
  (28 other events, 291.7 us)

commit v5 on v4

--- a/solution.py
+++ b/solution.py
@@ -278,12 +278,11 @@
 
 
 def stack_kernel(*refs):
-    *part_refs, out_ref = refs
-    out_ref[...] = stacked(part_refs)
-
-
-def stacked(part_refs):
-    return jnp.concatenate([ref[...].astype(F32) for ref in part_refs], axis=0).astype(BF16)
+    *part_refs, out_ref, scalar_ref = refs
+    width = out_ref.shape[1]
+    rows = jnp.concatenate([ref[...].astype(F32) for ref in part_refs], axis=0)
+    out_ref[...] = rows[:, :width].astype(BF16)
+    scalar_ref[...] = rows[:, width:].astype(BF16)
 
 
 def by_chip(own_refs, sibling_ref):
@@ -500,7 +499,7 @@
     parts = jnp.concatenate([blocks[k] for k in sorted(blocks)], axis=0).astype(BF16)
     normed_grad = dot_nt(parts[:, :width], weight_ref[...]) * flat_gain(gain_ref)
     means = parts[:, width:].astype(F32)
-    scalars = scalar_ref[:, width:].astype(F32)
+    scalars = scalar_ref[...].astype(F32)
     inv_std = get_scalar(scalars, 1)
     normed = (merged_ref[...].astype(F32) - get_scalar(scalars, 0)) * inv_std
     grad = inv_std * (normed_grad - get_scalar(means, 0) - normed * get_scalar(means, 1))
@@ -675,8 +674,8 @@
         early[1], *message, far=(0,), cost=0.2, name="merge",
     )
     owns = spread_out(own, "expert")
-    block_rows = run(
-        stack_kernel, shape((rows, width + 128)), *owns, cost=0.2, name="stack",
+    block_rows, row_scalars = run(
+        stack_kernel, [shape((rows, width)), shape((rows, 128))], *owns, cost=0.2, name="stack",
     )
     text_rows, act_grad = run(
         early_kernel, [shape((slot_count, width)), shape((slot_count, hidden), F32)],
@@ -772,7 +771,7 @@
     attn_grad = run(
         functools.partial(merge_grad_kernel, size=size, bases=tuple(bases)),
         shape((depth, patches), F32),
-        merge_gain, merged, block_rows, weight_flat, *vision_grads, cost=4.0, name="merge_grad",
+        merge_gain, merged, row_scalars, weight_flat, *vision_grads, cost=4.0, name="merge_grad",
     )
 
     laid = {}

time: 103 us -> 102 us (level)
  no operation moved by 1% of the time
where the time goes in v5:
time: 102 us
  starting transfers between devices  39.7 us (39%)
  waiting for transfers between devices  38 us (37%)
  Pallas kernels  19.2 us (19%)
  local copies, waits for them, and re-layouts  4.22 us (4%)
  between operations  1.03 us (1%)
    ppermute x41, starting transfers between devices, swap(): return lax.ppermute(value, axis, [(i, i ^ step) for i in range(count)])  39.7 us
    ppermute x41, waiting for transfers between devices, swap(): return lax.ppermute(value, axis, [(i, i ^ step) for i in range(count)])  38 us
    pallas_call x24, Pallas kernels, run(): pl.pallas_call(kernel, out_shape=outs, in_specs=specs, out_specs=jax.tree...  19.2 us
    unnamed x38, local copies, waits for them, and re-layouts  4.22 us
  transfers between devices with their start and end apart: 41, of which 21 were waited for; matrix products, arithmetic and copies ran while one was open for 0% of the time, Pallas kernels for 11%

profile of v5, /device:TPU:0, one launch (start us, length us, event | category | flops | bytes accessed | tf_op | source)
XLA Modules:
  0.0 102.1 jit_solution(13161903687607905888)
XLA Ops:
  0.7 1.8 %pack.1 = bf16[592,128]{1,0:T(8,128)(2,1)} custom-call(bf16[288,128]{1,0:T(8,128)(2,1)} %bitcast.11, bf16[288,128]{1,0:T(8,128)(2,1)} %bitcast.13, s32[1,32]{1,0:T(1,128)} %bitcast.22, s32[1,32]{1,0:T(1,128)} %bitcast.24, s32[8,128]{1,0:T(8,128)} %bitcast.18), custom_call_target="tpu_custom_call" | custom-call | bytes 3000000 | tf_op jit(solution)/shard_map/pack/pallas_call | solution.py:530
  2.6 4.0 %collective-permute-start.3 = (bf16[592,128]{1,0:T(8,128)(2,1)}, bf16[592,128]{1,0:T(8,128)(2,1)S(1)}, u32[]{:S(2)}, u32[]{:S(2)}) collective-permute-start(bf16[592,128]{1,0:T(8,128)(2,1)} %pack.1), channel_id=1, source_target_pairs={{0,24},{4,28},{8,16},{12,20},{16,8},{20,12},{24,0},{28,4},{1,25},{... | collective-permute-start | bytes 454664 | tf_op jit(solution)/shard_map/ppermute | solution.py:576
  12.5 1.4 %collective-permute-done.2.refs_1_ = bf16[592,128]{1,0:T(8,128)(2,1)S(1)} collective-permute-done((bf16[592,128]{1,0:T(8,128)(2,1)}, bf16[592,128]{1,0:T(8,128)(2,1)S(1)}, u32[]{:S(2)}, u32[]{:S(2)}) %collective-permute-start.2) | collective-permute-done | bytes 151584 | tf_op jit(solution)/shard_map/ppermute | solution.py:576
  14.2 1.5 %collective-permute-start.7 = (bf16[48,2048]{1,0:T(8,128)(2,1)S(1)}, bf16[48,2048]{1,0:T(8,128)(2,1)S(1)}, u32[]{:S(2)}, u32[]{:S(2)}) collective-permute-start(bf16[48,2048]{1,0:T(8,128)(2,1)S(1)} %get-tuple-element.72), channel_id=1, source_target_pairs={{0,8},{4,12},{8,0},{12,4},{16,24},{20,28},{24,16},{28,20},{1,9},{5... | collective-permute-start | bytes 589832 | tf_op jit(solution)/shard_map/ppermute | solution.py:576
  19.4 2.6 %attend.1 = (bf16[32,1152]{1,0:T(8,128)(2,1)S(1)}, bf16[128,128]{1,0:T(8,128)(2,1)S(1)}, bf16[48,1152]{1,0:T(8,128)(2,1)S(1)}, f32[32,128]{1,0:T(8,128)S(1)}) custom-call(bf16[4,72,128]{2,1,0:T(8,128)(2,1)S(1)} %copy-done.12, f32[4,288]{1,0:T(4,128)S(1)} %copy-done.15, bf16[288,128]{1,0:T(8,128)(2,1)S(1)} %bitcast.12, bf16[288,128]{1,0:T(8,128)(2,1)S(1)} %bitcast.14, ...), custom_call_target="tpu_custom_call" | custom-call | bytes 9000000 | tf_op jit(solution)/shard_map/attend/pallas_call | solution.py:530
  23.0 1.6 %collective-permute-start.10 = (bf16[8,2432]{1,0:T(8,128)(2,1)S(1)}, bf16[8,2432]{1,0:T(8,128)(2,1)S(1)}, u32[]{:S(2)}, u32[]{:S(2)}) collective-permute-start(bf16[8,2432]{1,0:T(8,128)(2,1)S(1)} %get-tuple-element.77), channel_id=1, source_target_pairs={{0,1},{1,0},{2,3},{3,2},{4,5},{5,4},{6,7},{7,6},{8,9},{9,8},{10,11... | collective-permute-start | bytes 116744 | tf_op jit(solution)/shard_map/ppermute | solution.py:576
  24.6 2.6 %collective-permute-start.11 = (bf16[8,2432]{1,0:T(8,128)(2,1)S(1)}, bf16[8,2432]{1,0:T(8,128)(2,1)S(1)}, u32[]{:S(2)}, u32[]{:S(2)}) collective-permute-start(bf16[8,2432]{1,0:T(8,128)(2,1)S(1)} %get-tuple-element.78), channel_id=1, source_target_pairs={{0,2},{1,3},{2,0},{3,1},{4,6},{5,7},{6,4},{7,5},{8,10},{9,11},{10,... | collective-permute-start | bytes 116744 | tf_op jit(solution)/shard_map/ppermute | solution.py:576
  27.4 2.8 %collective-permute-done.11.refs_4_.refs_2_ = bf16[8,2432]{1,0:T(8,128)(2,1)S(1)} collective-permute-done((bf16[8,2432]{1,0:T(8,128)(2,1)S(1)}, bf16[8,2432]{1,0:T(8,128)(2,1)S(1)}, u32[]{:S(2)}, u32[]{:S(2)}) %collective-permute-start.11) | collective-permute-done | bytes 38944 | tf_op jit(solution)/shard_map/ppermute | solution.py:576
  30.2 2.8 %collective-permute-done.12.refs_5_.refs_3_ = bf16[8,2432]{1,0:T(8,128)(2,1)S(1)} collective-permute-done((bf16[8,2432]{1,0:T(8,128)(2,1)S(1)}, bf16[8,2432]{1,0:T(8,128)(2,1)S(1)}, u32[]{:S(2)}, u32[]{:S(2)}) %collective-permute-start.12) | collective-permute-done | bytes 38944 | tf_op jit(solution)/shard_map/ppermute | solution.py:576
  33.9 3.7 %collective-permute-start.13 = (bf16[8,2176]{1,0:T(8,128)(2,1)S(1)}, bf16[8,2176]{1,0:T(8,128)(2,1)S(1)}, u32[]{:S(2)}, u32[]{:S(2)}) collective-permute-start(bf16[8,2176]{1,0:T(8,128)(2,1)S(1)} %get-tuple-element.84.refs_0_), channel_id=1, source_target_pairs={{0,1},{1,0},{2,3},{3,2},{4,5},{5,4},{6,7},{7,6},{8,9},{9,8},{10,11... | collective-permute-start | bytes 104456 | tf_op jit(solution)/shard_map/ppermute | solution.py:576
  37.6 1.4 %collective-permute-done.15.refs_6_.refs_3_ = bf16[8,2176]{1,0:T(8,128)(2,1)S(1)} collective-permute-done((bf16[8,2176]{1,0:T(8,128)(2,1)S(1)}, bf16[8,2176]{1,0:T(8,128)(2,1)S(1)}, u32[]{:S(2)}, u32[]{:S(2)}) %collective-permute-start.15) | collective-permute-done | bytes 34848 | tf_op jit(solution)/shard_map/ppermute | solution.py:576
  39.7 1.9 %collective-permute-start.20 = (bf16[32,2048]{1,0:T(8,128)(2,1)S(1)}, bf16[32,2048]{1,0:T(8,128)(2,1)S(1)}, u32[]{:S(2)}, u32[]{:S(2)}) collective-permute-start(bf16[32,2048]{1,0:T(8,128)(2,1)S(1)} %get-tuple-element.86.refs_6_.refs_0_.rows_ref), channel_id=1, source_target_pairs={{0,24},{4,28},{8,16},{12,20},{16,8},{20,12},{24,0},{28,4},{1,25},{... | collective-permute-start | bytes 393224 | tf_op jit(solution)/shard_map/ppermute | solution.py:576
  44.0 1.3 %early.1 = (bf16[96,2048]{1,0:T(8,128)(2,1)S(1)}, f32[96,768]{1,0:T(8,128)S(1)}) custom-call(bf16[1,768,2048]{2,1,0:T(8,128)(2,1)S(1)} %copy-done.3, bf16[48,2048]{1,0:T(8,128)(2,1)S(1)} %get-tuple-element.71.refs_0_, bf16[48,2048]{1,0:T(8,128)(2,1)S(1)} %get-tuple-element.80._.refs_1_, bf16[48,2048]{1,0:T(8,128)(2,1)S(1)} %get-tuple-element.81.refs_2_, ...), custom_call_target="tpu_custom_call" | custom-call | bytes 9000000 | tf_op jit(solution)/shard_map/early/pallas_call | solution.py:530
  45.3 1.7 %collective-permute-done.20.refs_2_ = bf16[32,2048]{1,0:T(8,128)(2,1)S(1)} collective-permute-done((bf16[32,2048]{1,0:T(8,128)(2,1)S(1)}, bf16[32,2048]{1,0:T(8,128)(2,1)S(1)}, u32[]{:S(2)}, u32[]{:S(2)}) %collective-permute-start.20) | collective-permute-done | bytes 131104 | tf_op jit(solution)/shard_map/ppermute | solution.py:576
  47.0 2.4 %collective-permute-done.19.refs_1_ = bf16[32,2048]{1,0:T(8,128)(2,1)S(1)} collective-permute-done((bf16[32,2048]{1,0:T(8,128)(2,1)S(1)}, bf16[32,2048]{1,0:T(8,128)(2,1)S(1)}, u32[]{:S(2)}, u32[]{:S(2)}) %collective-permute-start.19) | collective-permute-done | bytes 131104 | tf_op jit(solution)/shard_map/ppermute | solution.py:576
  51.3 3.2 %forward.1 = (f32[96,768]{1,0:T(8,128)S(1)}, f32[96,768]{1,0:T(8,128)S(1)}, bf16[24,2048]{1,0:T(8,128)(2,1)S(1)}, bf16[24,2048]{1,0:T(8,128)(2,1)S(1)}, bf16[24,...) custom-call(bf16[96,256]{1,0:T(8,128)(2,1)S(1)} %get-tuple-element.70.refs_4_.refs_0_.slots_ref, ...), custom_call_target="tpu_custom_call" | custom-call | bytes 12000000 | tf_op jit(solution)/shard_map/forward/pallas_call | solution.py:530
  54.5 1.5 %backward.1 = (bf16[160,2048]{1,0:T(8,128)(2,1)S(1)}, bf16[160,2048]{1,0:T(8,128)(2,1)S(1)}) custom-call(bf16[96,256]{1,0:T(8,128)(2,1)S(1)} %get-tuple-element.70.refs_4_.refs_0_.slots_ref, f32[96,768]{1,0:T(8,128)S(1)} %get-tuple-element.94.grad_ref, f32[96,768]{1,0:T(8,128)S(1)} %get-tuple-element.95.gate_in, f32[96,768]{1,0:T(8,128)S(1)} %get-tuple-element.96.up_in, ...), custom_call_target="tpu_custom_call" | custom-call | bytes 12000000 | tf_op jit(solution)/shard_map/backward/pallas_call | solution.py:530
  56.3 1.4 %collective-permute-start.24 = (bf16[24,2048]{1,0:T(8,128)(2,1)S(1)}, bf16[24,2048]{1,0:T(8,128)(2,1)S(1)}, u32[]{:S(2)}, u32[]{:S(2)}) collective-permute-start(bf16[24,2048]{1,0:T(8,128)(2,1)S(1)} %get-tuple-element.91), channel_id=1, source_target_pairs={{0,8},{4,12},{8,0},{12,4},{16,24},{20,28},{24,16},{28,20},{1,9},{5... | collective-permute-start | bytes 294920 | tf_op jit(solution)/shard_map/ppermute | solution.py:576
  59.9 1.4 %collective-permute-done.24.refs_1_ = bf16[24,2048]{1,0:T(8,128)(2,1)S(1)} collective-permute-done((bf16[24,2048]{1,0:T(8,128)(2,1)S(1)}, bf16[24,2048]{1,0:T(8,128)(2,1)S(1)}, u32[]{:S(2)}, u32[]{:S(2)}) %collective-permute-start.24) | collective-permute-done | bytes 98336 | tf_op jit(solution)/shard_map/ppermute | solution.py:576
  61.3 3.3 %collective-permute-done.25.refs_2_ = bf16[24,2048]{1,0:T(8,128)(2,1)S(1)} collective-permute-done((bf16[24,2048]{1,0:T(8,128)(2,1)S(1)}, bf16[24,2048]{1,0:T(8,128)(2,1)S(1)}, u32[]{:S(2)}, u32[]{:S(2)}) %collective-permute-start.25) | collective-permute-done | bytes 98336 | tf_op jit(solution)/shard_map/ppermute | solution.py:576
  65.4 1.3 %collective-permute-start.33 = (bf16[40,2048]{1,0:T(8,128)(2,1)S(1)}, bf16[40,2048]{1,0:T(8,128)(2,1)S(1)}, u32[]{:S(2)}, u32[]{:S(2)}) collective-permute-start(bf16[40,2048]{1,0:T(8,128)(2,1)S(1)} %get-tuple-element.106), channel_id=1, source_target_pairs={{0,16},{4,20},{8,24},{12,28},{16,0},{20,4},{24,8},{28,12},{1,17},{... | collective-permute-start | bytes 491528 | tf_op jit(solution)/shard_map/ppermute | solution.py:576
  66.7 1.5 %collective-permute-start.34 = (bf16[40,2048]{1,0:T(8,128)(2,1)S(1)}, bf16[40,2048]{1,0:T(8,128)(2,1)S(1)}, u32[]{:S(2)}, u32[]{:S(2)}) collective-permute-start(bf16[40,2048]{1,0:T(8,128)(2,1)S(1)} %get-tuple-element.107), channel_id=1, source_target_pairs={{0,24},{4,28},{8,16},{12,20},{16,8},{20,12},{24,0},{28,4},{1,25},{... | collective-permute-start | bytes 491528 | tf_op jit(solution)/shard_map/ppermute | solution.py:576
  68.7 2.1 %collective-permute-start.30 = (bf16[32,2048]{1,0:T(8,128)(2,1)S(1)}, bf16[32,2048]{1,0:T(8,128)(2,1)S(1)}, u32[]{:S(2)}, u32[]{:S(2)}) collective-permute-start(bf16[32,2048]{1,0:T(8,128)(2,1)S(1)} %get-tuple-element.104), channel_id=1, source_target_pairs={{0,1},{1,0},{2,3},{3,2},{4,5},{5,4},{6,7},{7,6},{8,9},{9,8},{10,11... | collective-permute-start | bytes 393224 | tf_op jit(solution)/shard_map/ppermute | solution.py:576
  70.8 4.3 %collective-permute-done.30.arrived_ref.refs_4_ = bf16[32,2048]{1,0:T(8,128)(2,1)S(1)} collective-permute-done((bf16[32,2048]{1,0:T(8,128)(2,1)S(1)}, bf16[32,2048]{1,0:T(8,128)(2,1)S(1)}, u32[]{:S(2)}, u32[]{:S(2)}) %collective-permute-start.30) | collective-permute-done | bytes 131104 | tf_op jit(solution)/shard_map/ppermute | solution.py:576
  76.5 1.8 %collective-permute-start.35 = (bf16[16,2048]{1,0:T(8,128)(2,1)S(1)}, bf16[16,2048]{1,0:T(8,128)(2,1)S(1)}, u32[]{:S(2)}, u32[]{:S(2)}) collective-permute-start(bf16[16,2048]{1,0:T(8,128)(2,1)S(1)} %get-tuple-element.109), channel_id=1, source_target_pairs={{0,1},{1,0},{2,3},{3,2},{4,5},{5,4},{6,7},{7,6},{8,9},{9,8},{10,11... | collective-permute-start | bytes 196616 | tf_op jit(solution)/shard_map/ppermute | solution.py:576
  78.3 3.5 %collective-permute-done.35.arrived_ref = bf16[16,2048]{1,0:T(8,128)(2,1)S(1)} collective-permute-done((bf16[16,2048]{1,0:T(8,128)(2,1)S(1)}, bf16[16,2048]{1,0:T(8,128)(2,1)S(1)}, u32[]{:S(2)}, u32[]{:S(2)}) %collective-permute-start.35) | collective-permute-done | bytes 65568 | tf_op jit(solution)/shard_map/ppermute | solution.py:576
  81.8 2.1 %collective-permute-start.36 = (bf16[24,2048]{1,0:T(8,128)(2,1)S(1)}, bf16[24,2048]{1,0:T(8,128)(2,1)S(1)}, u32[]{:S(2)}, u32[]{:S(2)}) collective-permute-start(bf16[24,2048]{1,0:T(8,128)(2,1)S(1)} %grad_join.1.joined_ref), channel_id=1, source_target_pairs={{0,2},{1,3},{2,0},{3,1},{4,6},{5,7},{6,4},{7,5},{8,10},{9,11},{10,... | collective-permute-start | bytes 294920 | tf_op jit(solution)/shard_map/ppermute | solution.py:576
  84.9 6.2 %collective-permute-done.36.refs_8_.other_ref = bf16[24,2048]{1,0:T(8,128)(2,1)S(1)} collective-permute-done((bf16[24,2048]{1,0:T(8,128)(2,1)S(1)}, bf16[24,2048]{1,0:T(8,128)(2,1)S(1)}, u32[]{:S(2)}, u32[]{:S(2)}) %collective-permute-start.36) | collective-permute-done | bytes 98336 | tf_op jit(solution)/shard_map/ppermute | solution.py:576
  91.9 2.1 %collective-permute-start.37 = (bf16[32,2048]{1,0:T(8,128)(2,1)S(1)}, bf16[32,2048]{1,0:T(8,128)(2,1)S(1)}, u32[]{:S(2)}, u32[]{:S(2)}) collective-permute-start(bf16[32,2048]{1,0:T(8,128)(2,1)S(1)} %finish.2.refs_0_), channel_id=1, source_target_pairs={{0,1},{1,0},{2,3},{3,2},{4,5},{5,4},{6,7},{7,6},{8,9},{9,8},{10,11... | collective-permute-start | bytes 393224 | tf_op jit(solution)/shard_map/ppermute | solution.py:576
  94.0 1.7 %collective-permute-done.39.refs_8_.refs_5_ = bf16[16,2176]{1,0:T(8,128)(2,1)S(1)} collective-permute-done((bf16[16,2176]{1,0:T(8,128)(2,1)S(1)}, bf16[16,2176]{1,0:T(8,128)(2,1)S(1)}, u32[]{:S(2)}, u32[]{:S(2)}) %collective-permute-start.39) | collective-permute-done | bytes 69664 | tf_op jit(solution)/shard_map/ppermute | solution.py:576
  96.4 3.0 %merge_grad.1 = f32[288,128]{1,0:T(8,128)} custom-call(f32[4,288]{1,0:T(4,128)S(1)} %copy-done.15, bf16[32,1152]{1,0:T(8,128)(2,1)S(1)} %get-tuple-element.112.refs_1_, bf16[32,128]{1,0:T(8,128)(2,1)S(1)} %get-tuple-element.113.refs_2_, bf16[1152,2048]{1,0:T(8,128)(2,1)S(1)} %bitcast.10, bf16[16,2176]{1,0:T(8,128)(2,1)S(1)} %norm_grad.1.refs_4_, ...), custom_call_target="tpu_custom_call" | custom-call | bytes 12000000 | tf_op jit(solution)/shard_map/merge_grad/pallas_call | solution.py:530
  99.3 1.9 %collective-permute-done.40.refs_3_ = bf16[32,2048]{1,0:T(8,128)(2,1)S(1)} collective-permute-done((bf16[32,2048]{1,0:T(8,128)(2,1)S(1)}, bf16[32,2048]{1,0:T(8,128)(2,1)S(1)}, u32[]{:S(2)}, u32[]{:S(2)}) %collective-permute-start.40) | collective-permute-done | bytes 131104 | tf_op jit(solution)/shard_map/ppermute | solution.py:576
  (116 shorter events, 25.6 us)
Async XLA Ops:
  2.6 10.0 %collective-permute-start.3 = (bf16[592,128]{1,0:T(8,128)(2,1)}, bf16[592,128]{1,0:T(8,128)(2,1)S(1)}, u32[]{:S(2)}, u32[]{:S(2)}) collective-permute-start(bf16[592,128]{1,0:T(8,128)(2,1)} %pack.1), channel_id=1, source_target_pairs={{0,24},{4,28},{8,16},{12,20},{16,8},{20,12},{24,0},{28,4},{1,25},{... | collective-permute-start | bytes 454664 | tf_op jit(solution)/shard_map/ppermute | solution.py:576
  6.5 7.4 %collective-permute-start.2 = (bf16[592,128]{1,0:T(8,128)(2,1)}, bf16[592,128]{1,0:T(8,128)(2,1)S(1)}, u32[]{:S(2)}, u32[]{:S(2)}) collective-permute-start(bf16[592,128]{1,0:T(8,128)(2,1)} %pack.1), channel_id=1, source_target_pairs={{0,16},{4,20},{8,24},{12,28},{16,0},{20,4},{24,8},{28,12},{1,17},{... | collective-permute-start | bytes 454664 | tf_op jit(solution)/shard_map/ppermute | solution.py:576
  7.0 7.2 %collective-permute-start.1 = (bf16[592,128]{1,0:T(8,128)(2,1)}, bf16[592,128]{1,0:T(8,128)(2,1)S(1)}, u32[]{:S(2)}, u32[]{:S(2)}) collective-permute-start(bf16[592,128]{1,0:T(8,128)(2,1)} %pack.1), channel_id=1, source_target_pairs={{0,8},{4,12},{8,0},{12,4},{16,24},{20,28},{24,16},{28,20},{1,9},{5... | collective-permute-start | bytes 454664 | tf_op jit(solution)/shard_map/ppermute | solution.py:576
  7.2 10.5 %collective-permute-start = (bf16[592,128]{1,0:T(8,128)(2,1)}, bf16[592,128]{1,0:T(8,128)(2,1)S(1)}, u32[]{:S(2)}, u32[]{:S(2)}) collective-permute-start(bf16[592,128]{1,0:T(8,128)(2,1)} %pack.1), channel_id=1, source_target_pairs={{0,4},{4,0},{8,12},{12,8},{16,20},{20,16},{24,28},{28,24},{1,5},{5... | collective-permute-start | bytes 454664 | tf_op jit(solution)/shard_map/ppermute | solution.py:576
  14.2 7.8 %collective-permute-start.7 = (bf16[48,2048]{1,0:T(8,128)(2,1)S(1)}, bf16[48,2048]{1,0:T(8,128)(2,1)S(1)}, u32[]{:S(2)}, u32[]{:S(2)}) collective-permute-start(bf16[48,2048]{1,0:T(8,128)(2,1)S(1)} %get-tuple-element.72), channel_id=1, source_target_pairs={{0,8},{4,12},{8,0},{12,4},{16,24},{20,28},{24,16},{28,20},{1,9},{5... | collective-permute-start | bytes 589832 | tf_op jit(solution)/shard_map/ppermute | solution.py:576
  15.7 11.7 %collective-permute-start.8 = (bf16[48,2048]{1,0:T(8,128)(2,1)S(1)}, bf16[48,2048]{1,0:T(8,128)(2,1)S(1)}, u32[]{:S(2)}, u32[]{:S(2)}) collective-permute-start(bf16[48,2048]{1,0:T(8,128)(2,1)S(1)} %get-tuple-element.73), channel_id=1, source_target_pairs={{0,16},{4,20},{8,24},{12,28},{16,0},{20,4},{24,8},{28,12},{1,17},{... | collective-permute-start | bytes 589832 | tf_op jit(solution)/shard_map/ppermute | solution.py:576
  16.6 10.9 %collective-permute-start.9 = (bf16[48,2048]{1,0:T(8,128)(2,1)S(1)}, bf16[48,2048]{1,0:T(8,128)(2,1)S(1)}, u32[]{:S(2)}, u32[]{:S(2)}) collective-permute-start(bf16[48,2048]{1,0:T(8,128)(2,1)S(1)} %get-tuple-element.74), channel_id=1, source_target_pairs={{0,24},{4,28},{8,16},{12,20},{16,8},{20,12},{24,0},{28,4},{1,25},{... | collective-permute-start | bytes 589832 | tf_op jit(solution)/shard_map/ppermute | solution.py:576
  23.0 4.5 %collective-permute-start.10 = (bf16[8,2432]{1,0:T(8,128)(2,1)S(1)}, bf16[8,2432]{1,0:T(8,128)(2,1)S(1)}, u32[]{:S(2)}, u32[]{:S(2)}) collective-permute-start(bf16[8,2432]{1,0:T(8,128)(2,1)S(1)} %get-tuple-element.77), channel_id=1, source_target_pairs={{0,1},{1,0},{2,3},{3,2},{4,5},{5,4},{6,7},{7,6},{8,9},{9,8},{10,11... | collective-permute-start | bytes 116744 | tf_op jit(solution)/shard_map/ppermute | solution.py:576
  24.6 5.6 %collective-permute-start.11 = (bf16[8,2432]{1,0:T(8,128)(2,1)S(1)}, bf16[8,2432]{1,0:T(8,128)(2,1)S(1)}, u32[]{:S(2)}, u32[]{:S(2)}) collective-permute-start(bf16[8,2432]{1,0:T(8,128)(2,1)S(1)} %get-tuple-element.78), channel_id=1, source_target_pairs={{0,2},{1,3},{2,0},{3,1},{4,6},{5,7},{6,4},{7,5},{8,10},{9,11},{10,... | collective-permute-start | bytes 116744 | tf_op jit(solution)/shard_map/ppermute | solution.py:576
  27.2 5.8 %collective-permute-start.12 = (bf16[8,2432]{1,0:T(8,128)(2,1)S(1)}, bf16[8,2432]{1,0:T(8,128)(2,1)S(1)}, u32[]{:S(2)}, u32[]{:S(2)}) collective-permute-start(bf16[8,2432]{1,0:T(8,128)(2,1)S(1)} %get-tuple-element.79), channel_id=1, source_target_pairs={{0,3},{1,2},{2,1},{3,0},{4,7},{5,6},{6,5},{7,4},{8,11},{9,10},{10,... | collective-permute-start | bytes 116744 | tf_op jit(solution)/shard_map/ppermute | solution.py:576
  33.1 5.9 %collective-permute-start.15 = (bf16[8,2176]{1,0:T(8,128)(2,1)S(1)}, bf16[8,2176]{1,0:T(8,128)(2,1)S(1)}, u32[]{:S(2)}, u32[]{:S(2)}) collective-permute-start(bf16[8,2176]{1,0:T(8,128)(2,1)S(1)} %get-tuple-element.84.refs_0_), channel_id=1, source_target_pairs={{0,3},{1,2},{2,1},{3,0},{4,7},{5,6},{6,5},{7,4},{8,11},{9,10},{10,... | collective-permute-start | bytes 104456 | tf_op jit(solution)/shard_map/ppermute | solution.py:576
  33.9 5.7 %collective-permute-start.14 = (bf16[8,2176]{1,0:T(8,128)(2,1)S(1)}, bf16[8,2176]{1,0:T(8,128)(2,1)S(1)}, u32[]{:S(2)}, u32[]{:S(2)}) collective-permute-start(bf16[8,2176]{1,0:T(8,128)(2,1)S(1)} %get-tuple-element.84.refs_0_), channel_id=1, source_target_pairs={{0,2},{1,3},{2,0},{3,1},{4,6},{5,7},{6,4},{7,5},{8,10},{9,11},{10,... | collective-permute-start | bytes 104456 | tf_op jit(solution)/shard_map/ppermute | solution.py:576
  33.9 5.7 %collective-permute-start.13 = (bf16[8,2176]{1,0:T(8,128)(2,1)S(1)}, bf16[8,2176]{1,0:T(8,128)(2,1)S(1)}, u32[]{:S(2)}, u32[]{:S(2)}) collective-permute-start(bf16[8,2176]{1,0:T(8,128)(2,1)S(1)} %get-tuple-element.84.refs_0_), channel_id=1, source_target_pairs={{0,1},{1,0},{2,3},{3,2},{4,5},{5,4},{6,7},{7,6},{8,9},{9,8},{10,11... | collective-permute-start | bytes 104456 | tf_op jit(solution)/shard_map/ppermute | solution.py:576
  39.6 4.4 %collective-permute-start.16 = (bf16[96,2048]{1,0:T(8,128)(2,1)S(1)}, bf16[96,2048]{1,0:T(8,128)(2,1)S(1)}, u32[]{:S(2)}, u32[]{:S(2)}) collective-permute-start(bf16[96,2048]{1,0:T(8,128)(2,1)S(1)} %early_half.1), channel_id=1, source_target_pairs={{0,4},{4,0},{8,12},{12,8},{16,20},{20,16},{24,28},{28,24},{1,5},{5... | collective-permute-start | bytes 1179656 | tf_op jit(solution)/shard_map/ppermute | solution.py:576
  39.7 7.3 %collective-permute-start.20 = (bf16[32,2048]{1,0:T(8,128)(2,1)S(1)}, bf16[32,2048]{1,0:T(8,128)(2,1)S(1)}, u32[]{:S(2)}, u32[]{:S(2)}) collective-permute-start(bf16[32,2048]{1,0:T(8,128)(2,1)S(1)} %get-tuple-element.86.refs_6_.refs_0_.rows_ref), channel_id=1, source_target_pairs={{0,24},{4,28},{8,16},{12,20},{16,8},{20,12},{24,0},{28,4},{1,25},{... | collective-permute-start | bytes 393224 | tf_op jit(solution)/shard_map/ppermute | solution.py:576
  41.6 7.8 %collective-permute-start.19 = (bf16[32,2048]{1,0:T(8,128)(2,1)S(1)}, bf16[32,2048]{1,0:T(8,128)(2,1)S(1)}, u32[]{:S(2)}, u32[]{:S(2)}) collective-permute-start(bf16[32,2048]{1,0:T(8,128)(2,1)S(1)} %get-tuple-element.86.refs_6_.refs_0_.rows_ref), channel_id=1, source_target_pairs={{0,16},{4,20},{8,24},{12,28},{16,0},{20,4},{24,8},{28,12},{1,17},{... | collective-permute-start | bytes 393224 | tf_op jit(solution)/shard_map/ppermute | solution.py:576
  42.7 6.7 %collective-permute-start.18 = (bf16[32,2048]{1,0:T(8,128)(2,1)S(1)}, bf16[32,2048]{1,0:T(8,128)(2,1)S(1)}, u32[]{:S(2)}, u32[]{:S(2)}) collective-permute-start(bf16[32,2048]{1,0:T(8,128)(2,1)S(1)} %get-tuple-element.86.refs_6_.refs_0_.rows_ref), channel_id=1, source_target_pairs={{0,8},{4,12},{8,0},{12,4},{16,24},{20,28},{24,16},{28,20},{1,9},{5... | collective-permute-start | bytes 393224 | tf_op jit(solution)/shard_map/ppermute | solution.py:576
  43.9 6.0 %collective-permute-start.17 = (bf16[32,2048]{1,0:T(8,128)(2,1)S(1)}, bf16[32,2048]{1,0:T(8,128)(2,1)S(1)}, u32[]{:S(2)}, u32[]{:S(2)}) collective-permute-start(bf16[32,2048]{1,0:T(8,128)(2,1)S(1)} %get-tuple-element.86.refs_6_.refs_0_.rows_ref), channel_id=1, source_target_pairs={{0,4},{4,0},{8,12},{12,8},{16,20},{20,16},{24,28},{28,24},{1,5},{5... | collective-permute-start | bytes 393224 | tf_op jit(solution)/shard_map/ppermute | solution.py:576
  56.3 5.0 %collective-permute-start.24 = (bf16[24,2048]{1,0:T(8,128)(2,1)S(1)}, bf16[24,2048]{1,0:T(8,128)(2,1)S(1)}, u32[]{:S(2)}, u32[]{:S(2)}) collective-permute-start(bf16[24,2048]{1,0:T(8,128)(2,1)S(1)} %get-tuple-element.91), channel_id=1, source_target_pairs={{0,8},{4,12},{8,0},{12,4},{16,24},{20,28},{24,16},{28,20},{1,9},{5... | collective-permute-start | bytes 294920 | tf_op jit(solution)/shard_map/ppermute | solution.py:576
  57.7 6.9 %collective-permute-start.25 = (bf16[24,2048]{1,0:T(8,128)(2,1)S(1)}, bf16[24,2048]{1,0:T(8,128)(2,1)S(1)}, u32[]{:S(2)}, u32[]{:S(2)}) collective-permute-start(bf16[24,2048]{1,0:T(8,128)(2,1)S(1)} %get-tuple-element.92), channel_id=1, source_target_pairs={{0,16},{4,20},{8,24},{12,28},{16,0},{20,4},{24,8},{28,12},{1,17},{... | collective-permute-start | bytes 294920 | tf_op jit(solution)/shard_map/ppermute | solution.py:576
  58.5 6.0 %collective-permute-start.26 = (bf16[24,2048]{1,0:T(8,128)(2,1)S(1)}, bf16[24,2048]{1,0:T(8,128)(2,1)S(1)}, u32[]{:S(2)}, u32[]{:S(2)}) collective-permute-start(bf16[24,2048]{1,0:T(8,128)(2,1)S(1)} %get-tuple-element.93), channel_id=1, source_target_pairs={{0,24},{4,28},{8,16},{12,20},{16,8},{20,12},{24,0},{28,4},{1,25},{... | collective-permute-start | bytes 294920 | tf_op jit(solution)/shard_map/ppermute | solution.py:576
  64.7 11.7 %collective-permute-start.32 = (bf16[40,2048]{1,0:T(8,128)(2,1)S(1)}, bf16[40,2048]{1,0:T(8,128)(2,1)S(1)}, u32[]{:S(2)}, u32[]{:S(2)}) collective-permute-start(bf16[40,2048]{1,0:T(8,128)(2,1)S(1)} %get-tuple-element.105), channel_id=1, source_target_pairs={{0,8},{4,12},{8,0},{12,4},{16,24},{20,28},{24,16},{28,20},{1,9},{5... | collective-permute-start | bytes 491528 | tf_op jit(solution)/shard_map/ppermute | solution.py:576
  65.4 11.0 %collective-permute-start.33 = (bf16[40,2048]{1,0:T(8,128)(2,1)S(1)}, bf16[40,2048]{1,0:T(8,128)(2,1)S(1)}, u32[]{:S(2)}, u32[]{:S(2)}) collective-permute-start(bf16[40,2048]{1,0:T(8,128)(2,1)S(1)} %get-tuple-element.106), channel_id=1, source_target_pairs={{0,16},{4,20},{8,24},{12,28},{16,0},{20,4},{24,8},{28,12},{1,17},{... | collective-permute-start | bytes 491528 | tf_op jit(solution)/shard_map/ppermute | solution.py:576
  66.7 9.7 %collective-permute-start.34 = (bf16[40,2048]{1,0:T(8,128)(2,1)S(1)}, bf16[40,2048]{1,0:T(8,128)(2,1)S(1)}, u32[]{:S(2)}, u32[]{:S(2)}) collective-permute-start(bf16[40,2048]{1,0:T(8,128)(2,1)S(1)} %get-tuple-element.107), channel_id=1, source_target_pairs={{0,24},{4,28},{8,16},{12,20},{16,8},{20,12},{24,0},{28,4},{1,25},{... | collective-permute-start | bytes 491528 | tf_op jit(solution)/shard_map/ppermute | solution.py:576
  68.7 6.4 %collective-permute-start.30 = (bf16[32,2048]{1,0:T(8,128)(2,1)S(1)}, bf16[32,2048]{1,0:T(8,128)(2,1)S(1)}, u32[]{:S(2)}, u32[]{:S(2)}) collective-permute-start(bf16[32,2048]{1,0:T(8,128)(2,1)S(1)} %get-tuple-element.104), channel_id=1, source_target_pairs={{0,1},{1,0},{2,3},{3,2},{4,5},{5,4},{6,7},{7,6},{8,9},{9,8},{10,11... | collective-permute-start | bytes 393224 | tf_op jit(solution)/shard_map/ppermute | solution.py:576
  70.7 13.2 %collective-permute-start.29 = (bf16[32,2048]{1,0:T(8,128)(2,1)S(1)}, bf16[32,2048]{1,0:T(8,128)(2,1)S(1)}, u32[]{:S(2)}, u32[]{:S(2)}) collective-permute-start(bf16[32,2048]{1,0:T(8,128)(2,1)S(1)} %get-tuple-element.102), channel_id=1, source_target_pairs={{0,1},{1,0},{2,3},{3,2},{4,5},{5,4},{6,7},{7,6},{8,9},{9,8},{10,11... | collective-permute-start | bytes 393224 | tf_op jit(solution)/shard_map/ppermute | solution.py:576
  75.2 8.8 %collective-permute-start.31 = (bf16[32,2048]{1,0:T(8,128)(2,1)S(1)}, bf16[32,2048]{1,0:T(8,128)(2,1)S(1)}, u32[]{:S(2)}, u32[]{:S(2)}) collective-permute-start(bf16[32,2048]{1,0:T(8,128)(2,1)S(1)} %add_high.1.own_ref), channel_id=1, source_target_pairs={{0,2},{1,3},{2,0},{3,1},{4,6},{5,7},{6,4},{7,5},{8,10},{9,11},{10,... | collective-permute-start | bytes 393224 | tf_op jit(solution)/shard_map/ppermute | solution.py:576
  76.5 5.3 %collective-permute-start.35 = (bf16[16,2048]{1,0:T(8,128)(2,1)S(1)}, bf16[16,2048]{1,0:T(8,128)(2,1)S(1)}, u32[]{:S(2)}, u32[]{:S(2)}) collective-permute-start(bf16[16,2048]{1,0:T(8,128)(2,1)S(1)} %get-tuple-element.109), channel_id=1, source_target_pairs={{0,1},{1,0},{2,3},{3,2},{4,5},{5,4},{6,7},{7,6},{8,9},{9,8},{10,11... | collective-permute-start | bytes 196616 | tf_op jit(solution)/shard_map/ppermute | solution.py:576
  81.8 9.3 %collective-permute-start.36 = (bf16[24,2048]{1,0:T(8,128)(2,1)S(1)}, bf16[24,2048]{1,0:T(8,128)(2,1)S(1)}, u32[]{:S(2)}, u32[]{:S(2)}) collective-permute-start(bf16[24,2048]{1,0:T(8,128)(2,1)S(1)} %grad_join.1.joined_ref), channel_id=1, source_target_pairs={{0,2},{1,3},{2,0},{3,1},{4,6},{5,7},{6,4},{7,5},{8,10},{9,11},{10,... | collective-permute-start | bytes 294920 | tf_op jit(solution)/shard_map/ppermute | solution.py:576
  83.9 11.8 %collective-permute-start.38 = (bf16[32,2048]{1,0:T(8,128)(2,1)S(1)}, bf16[32,2048]{1,0:T(8,128)(2,1)S(1)}, u32[]{:S(2)}, u32[]{:S(2)}) collective-permute-start(bf16[32,2048]{1,0:T(8,128)(2,1)S(1)} %add_low.1.own_ref), channel_id=1, source_target_pairs={{0,2},{1,3},{2,0},{3,1},{4,6},{5,7},{6,4},{7,5},{8,10},{9,11},{10,... | collective-permute-start | bytes 393224 | tf_op jit(solution)/shard_map/ppermute | solution.py:576
  91.9 7.4 %collective-permute-start.37 = (bf16[32,2048]{1,0:T(8,128)(2,1)S(1)}, bf16[32,2048]{1,0:T(8,128)(2,1)S(1)}, u32[]{:S(2)}, u32[]{:S(2)}) collective-permute-start(bf16[32,2048]{1,0:T(8,128)(2,1)S(1)} %finish.2.refs_0_), channel_id=1, source_target_pairs={{0,1},{1,0},{2,3},{3,2},{4,5},{5,4},{6,7},{7,6},{8,9},{9,8},{10,11... | collective-permute-start | bytes 393224 | tf_op jit(solution)/shard_map/ppermute | solution.py:576
  96.2 5.0 %collective-permute-start.40 = (bf16[32,2048]{1,0:T(8,128)(2,1)S(1)}, bf16[32,2048]{1,0:T(8,128)(2,1)S(1)}, u32[]{:S(2)}, u32[]{:S(2)}) collective-permute-start(bf16[32,2048]{1,0:T(8,128)(2,1)S(1)} %finish.3.refs_2_), channel_id=1, source_target_pairs={{0,1},{1,0},{2,3},{3,2},{4,5},{5,4},{6,7},{7,6},{8,9},{9,8},{10,11... | collective-permute-start | bytes 393224 | tf_op jit(solution)/shard_map/ppermute | solution.py:576
  (28 other events, 290.6 us)

commit v6 on v5

--- a/solution.py
+++ b/solution.py
@@ -775,7 +775,7 @@
     )
 
     laid = {}
-    for turn, value, other, gate in zip((0, step), sums, others, ([other], vision_grads[1:])):
+    for turn, value, other, gate in zip((0, step), sums, others, ([], vision_grads[1:])):
         laid[turn] = run(
             functools.partial(finish_kernel, blocks=blocks, turn=turn), shape((part, width)),
             placed, text, value, other, *vision, *gate,

time: 102 us -> 102 us (level)
  no operation moved by 1% of the time
where the time goes in v6:
time: 102 us
  starting transfers between devices  39.8 us (39%)
  waiting for transfers between devices  37.7 us (37%)
  Pallas kernels  19.2 us (19%)
  local copies, waits for them, and re-layouts  4.22 us (4%)
  between operations  1.03 us (1%)
    ppermute x41, starting transfers between devices, swap(): return lax.ppermute(value, axis, [(i, i ^ step) for i in range(count)])  39.8 us
    ppermute x41, waiting for transfers between devices, swap(): return lax.ppermute(value, axis, [(i, i ^ step) for i in range(count)])  37.7 us
    pallas_call x24, Pallas kernels, run(): pl.pallas_call(kernel, out_shape=outs, in_specs=specs, out_specs=jax.tree...  19.2 us
    unnamed x38, local copies, waits for them, and re-layouts  4.22 us
  transfers between devices with their start and end apart: 41, of which 21 were waited for; matrix products, arithmetic and copies ran while one was open for 0% of the time, Pallas kernels for 11%

profile of v6, /device:TPU:0, one launch (start us, length us, event | category | flops | bytes accessed | tf_op | source)
XLA Modules:
  0.0 102.0 jit_solution(14666667818049652060)
XLA Ops:
  0.7 1.8 %pack.1 = bf16[592,128]{1,0:T(8,128)(2,1)} custom-call(bf16[288,128]{1,0:T(8,128)(2,1)} %bitcast.11, bf16[288,128]{1,0:T(8,128)(2,1)} %bitcast.13, s32[1,32]{1,0:T(1,128)} %bitcast.22, s32[1,32]{1,0:T(1,128)} %bitcast.24, s32[8,128]{1,0:T(8,128)} %bitcast.18), custom_call_target="tpu_custom_call" | custom-call | bytes 3000000 | tf_op jit(solution)/shard_map/pack/pallas_call | solution.py:530
  2.6 4.0 %collective-permute-start.3 = (bf16[592,128]{1,0:T(8,128)(2,1)}, bf16[592,128]{1,0:T(8,128)(2,1)S(1)}, u32[]{:S(2)}, u32[]{:S(2)}) collective-permute-start(bf16[592,128]{1,0:T(8,128)(2,1)} %pack.1), channel_id=1, source_target_pairs={{0,24},{4,28},{8,16},{12,20},{16,8},{20,12},{24,0},{28,4},{1,25},{... | collective-permute-start | bytes 454664 | tf_op jit(solution)/shard_map/ppermute | solution.py:576
  12.6 1.4 %collective-permute-done.2.refs_1_ = bf16[592,128]{1,0:T(8,128)(2,1)S(1)} collective-permute-done((bf16[592,128]{1,0:T(8,128)(2,1)}, bf16[592,128]{1,0:T(8,128)(2,1)S(1)}, u32[]{:S(2)}, u32[]{:S(2)}) %collective-permute-start.2) | collective-permute-done | bytes 151584 | tf_op jit(solution)/shard_map/ppermute | solution.py:576
  14.2 1.5 %collective-permute-start.7 = (bf16[48,2048]{1,0:T(8,128)(2,1)S(1)}, bf16[48,2048]{1,0:T(8,128)(2,1)S(1)}, u32[]{:S(2)}, u32[]{:S(2)}) collective-permute-start(bf16[48,2048]{1,0:T(8,128)(2,1)S(1)} %get-tuple-element.72), channel_id=1, source_target_pairs={{0,8},{4,12},{8,0},{12,4},{16,24},{20,28},{24,16},{28,20},{1,9},{5... | collective-permute-start | bytes 589832 | tf_op jit(solution)/shard_map/ppermute | solution.py:576
  19.4 2.6 %attend.1 = (bf16[32,1152]{1,0:T(8,128)(2,1)S(1)}, bf16[128,128]{1,0:T(8,128)(2,1)S(1)}, bf16[48,1152]{1,0:T(8,128)(2,1)S(1)}, f32[32,128]{1,0:T(8,128)S(1)}) custom-call(bf16[4,72,128]{2,1,0:T(8,128)(2,1)S(1)} %copy-done.12, f32[4,288]{1,0:T(4,128)S(1)} %copy-done.15, bf16[288,128]{1,0:T(8,128)(2,1)S(1)} %bitcast.12, bf16[288,128]{1,0:T(8,128)(2,1)S(1)} %bitcast.14, ...), custom_call_target="tpu_custom_call" | custom-call | bytes 9000000 | tf_op jit(solution)/shard_map/attend/pallas_call | solution.py:530
  23.0 1.6 %collective-permute-start.10 = (bf16[8,2432]{1,0:T(8,128)(2,1)S(1)}, bf16[8,2432]{1,0:T(8,128)(2,1)S(1)}, u32[]{:S(2)}, u32[]{:S(2)}) collective-permute-start(bf16[8,2432]{1,0:T(8,128)(2,1)S(1)} %get-tuple-element.77), channel_id=1, source_target_pairs={{0,1},{1,0},{2,3},{3,2},{4,5},{5,4},{6,7},{7,6},{8,9},{9,8},{10,11... | collective-permute-start | bytes 116744 | tf_op jit(solution)/shard_map/ppermute | solution.py:576
  24.6 2.6 %collective-permute-start.11 = (bf16[8,2432]{1,0:T(8,128)(2,1)S(1)}, bf16[8,2432]{1,0:T(8,128)(2,1)S(1)}, u32[]{:S(2)}, u32[]{:S(2)}) collective-permute-start(bf16[8,2432]{1,0:T(8,128)(2,1)S(1)} %get-tuple-element.78), channel_id=1, source_target_pairs={{0,2},{1,3},{2,0},{3,1},{4,6},{5,7},{6,4},{7,5},{8,10},{9,11},{10,... | collective-permute-start | bytes 116744 | tf_op jit(solution)/shard_map/ppermute | solution.py:576
  27.4 2.8 %collective-permute-done.11.refs_4_.refs_2_ = bf16[8,2432]{1,0:T(8,128)(2,1)S(1)} collective-permute-done((bf16[8,2432]{1,0:T(8,128)(2,1)S(1)}, bf16[8,2432]{1,0:T(8,128)(2,1)S(1)}, u32[]{:S(2)}, u32[]{:S(2)}) %collective-permute-start.11) | collective-permute-done | bytes 38944 | tf_op jit(solution)/shard_map/ppermute | solution.py:576
  30.2 2.8 %collective-permute-done.12.refs_5_.refs_3_ = bf16[8,2432]{1,0:T(8,128)(2,1)S(1)} collective-permute-done((bf16[8,2432]{1,0:T(8,128)(2,1)S(1)}, bf16[8,2432]{1,0:T(8,128)(2,1)S(1)}, u32[]{:S(2)}, u32[]{:S(2)}) %collective-permute-start.12) | collective-permute-done | bytes 38944 | tf_op jit(solution)/shard_map/ppermute | solution.py:576
  33.9 3.7 %collective-permute-start.13 = (bf16[8,2176]{1,0:T(8,128)(2,1)S(1)}, bf16[8,2176]{1,0:T(8,128)(2,1)S(1)}, u32[]{:S(2)}, u32[]{:S(2)}) collective-permute-start(bf16[8,2176]{1,0:T(8,128)(2,1)S(1)} %get-tuple-element.84.refs_0_), channel_id=1, source_target_pairs={{0,1},{1,0},{2,3},{3,2},{4,5},{5,4},{6,7},{7,6},{8,9},{9,8},{10,11... | collective-permute-start | bytes 104456 | tf_op jit(solution)/shard_map/ppermute | solution.py:576
  37.6 1.4 %collective-permute-done.15.refs_6_.refs_3_ = bf16[8,2176]{1,0:T(8,128)(2,1)S(1)} collective-permute-done((bf16[8,2176]{1,0:T(8,128)(2,1)S(1)}, bf16[8,2176]{1,0:T(8,128)(2,1)S(1)}, u32[]{:S(2)}, u32[]{:S(2)}) %collective-permute-start.15) | collective-permute-done | bytes 34848 | tf_op jit(solution)/shard_map/ppermute | solution.py:576
  39.7 1.9 %collective-permute-start.20 = (bf16[32,2048]{1,0:T(8,128)(2,1)S(1)}, bf16[32,2048]{1,0:T(8,128)(2,1)S(1)}, u32[]{:S(2)}, u32[]{:S(2)}) collective-permute-start(bf16[32,2048]{1,0:T(8,128)(2,1)S(1)} %get-tuple-element.86.refs_6_.refs_0_.rows_ref), channel_id=1, source_target_pairs={{0,24},{4,28},{8,16},{12,20},{16,8},{20,12},{24,0},{28,4},{1,25},{... | collective-permute-start | bytes 393224 | tf_op jit(solution)/shard_map/ppermute | solution.py:576
  44.0 1.3 %early.1 = (bf16[96,2048]{1,0:T(8,128)(2,1)S(1)}, f32[96,768]{1,0:T(8,128)S(1)}) custom-call(bf16[1,768,2048]{2,1,0:T(8,128)(2,1)S(1)} %copy-done.3, bf16[48,2048]{1,0:T(8,128)(2,1)S(1)} %get-tuple-element.71.refs_0_, bf16[48,2048]{1,0:T(8,128)(2,1)S(1)} %get-tuple-element.80._.refs_1_, bf16[48,2048]{1,0:T(8,128)(2,1)S(1)} %get-tuple-element.81.refs_2_, ...), custom_call_target="tpu_custom_call" | custom-call | bytes 9000000 | tf_op jit(solution)/shard_map/early/pallas_call | solution.py:530
  45.3 1.7 %collective-permute-done.20.refs_2_ = bf16[32,2048]{1,0:T(8,128)(2,1)S(1)} collective-permute-done((bf16[32,2048]{1,0:T(8,128)(2,1)S(1)}, bf16[32,2048]{1,0:T(8,128)(2,1)S(1)}, u32[]{:S(2)}, u32[]{:S(2)}) %collective-permute-start.20) | collective-permute-done | bytes 131104 | tf_op jit(solution)/shard_map/ppermute | solution.py:576
  47.0 2.4 %collective-permute-done.19.refs_1_ = bf16[32,2048]{1,0:T(8,128)(2,1)S(1)} collective-permute-done((bf16[32,2048]{1,0:T(8,128)(2,1)S(1)}, bf16[32,2048]{1,0:T(8,128)(2,1)S(1)}, u32[]{:S(2)}, u32[]{:S(2)}) %collective-permute-start.19) | collective-permute-done | bytes 131104 | tf_op jit(solution)/shard_map/ppermute | solution.py:576
  51.3 3.2 %forward.1 = (f32[96,768]{1,0:T(8,128)S(1)}, f32[96,768]{1,0:T(8,128)S(1)}, bf16[24,2048]{1,0:T(8,128)(2,1)S(1)}, bf16[24,2048]{1,0:T(8,128)(2,1)S(1)}, bf16[24,...) custom-call(bf16[96,256]{1,0:T(8,128)(2,1)S(1)} %get-tuple-element.70.refs_4_.refs_0_.slots_ref, ...), custom_call_target="tpu_custom_call" | custom-call | bytes 12000000 | tf_op jit(solution)/shard_map/forward/pallas_call | solution.py:530
  54.5 1.5 %backward.1 = (bf16[160,2048]{1,0:T(8,128)(2,1)S(1)}, bf16[160,2048]{1,0:T(8,128)(2,1)S(1)}) custom-call(bf16[96,256]{1,0:T(8,128)(2,1)S(1)} %get-tuple-element.70.refs_4_.refs_0_.slots_ref, f32[96,768]{1,0:T(8,128)S(1)} %get-tuple-element.94.grad_ref, f32[96,768]{1,0:T(8,128)S(1)} %get-tuple-element.95.gate_in, f32[96,768]{1,0:T(8,128)S(1)} %get-tuple-element.96.up_in, ...), custom_call_target="tpu_custom_call" | custom-call | bytes 12000000 | tf_op jit(solution)/shard_map/backward/pallas_call | solution.py:530
  56.3 1.4 %collective-permute-start.24 = (bf16[24,2048]{1,0:T(8,128)(2,1)S(1)}, bf16[24,2048]{1,0:T(8,128)(2,1)S(1)}, u32[]{:S(2)}, u32[]{:S(2)}) collective-permute-start(bf16[24,2048]{1,0:T(8,128)(2,1)S(1)} %get-tuple-element.91), channel_id=1, source_target_pairs={{0,8},{4,12},{8,0},{12,4},{16,24},{20,28},{24,16},{28,20},{1,9},{5... | collective-permute-start | bytes 294920 | tf_op jit(solution)/shard_map/ppermute | solution.py:576
  59.9 1.4 %collective-permute-done.24.refs_1_ = bf16[24,2048]{1,0:T(8,128)(2,1)S(1)} collective-permute-done((bf16[24,2048]{1,0:T(8,128)(2,1)S(1)}, bf16[24,2048]{1,0:T(8,128)(2,1)S(1)}, u32[]{:S(2)}, u32[]{:S(2)}) %collective-permute-start.24) | collective-permute-done | bytes 98336 | tf_op jit(solution)/shard_map/ppermute | solution.py:576
  61.3 3.2 %collective-permute-done.25.refs_2_ = bf16[24,2048]{1,0:T(8,128)(2,1)S(1)} collective-permute-done((bf16[24,2048]{1,0:T(8,128)(2,1)S(1)}, bf16[24,2048]{1,0:T(8,128)(2,1)S(1)}, u32[]{:S(2)}, u32[]{:S(2)}) %collective-permute-start.25) | collective-permute-done | bytes 98336 | tf_op jit(solution)/shard_map/ppermute | solution.py:576
  65.4 1.4 %collective-permute-start.35 = (bf16[40,2048]{1,0:T(8,128)(2,1)S(1)}, bf16[40,2048]{1,0:T(8,128)(2,1)S(1)}, u32[]{:S(2)}, u32[]{:S(2)}) collective-permute-start(bf16[40,2048]{1,0:T(8,128)(2,1)S(1)} %get-tuple-element.106), channel_id=1, source_target_pairs={{0,16},{4,20},{8,24},{12,28},{16,0},{20,4},{24,8},{28,12},{1,17},{... | collective-permute-start | bytes 491528 | tf_op jit(solution)/shard_map/ppermute | solution.py:576
  66.8 1.4 %collective-permute-start.36 = (bf16[40,2048]{1,0:T(8,128)(2,1)S(1)}, bf16[40,2048]{1,0:T(8,128)(2,1)S(1)}, u32[]{:S(2)}, u32[]{:S(2)}) collective-permute-start(bf16[40,2048]{1,0:T(8,128)(2,1)S(1)} %get-tuple-element.107), channel_id=1, source_target_pairs={{0,24},{4,28},{8,16},{12,20},{16,8},{20,12},{24,0},{28,4},{1,25},{... | collective-permute-start | bytes 491528 | tf_op jit(solution)/shard_map/ppermute | solution.py:576
  68.7 2.1 %collective-permute-start.30 = (bf16[32,2048]{1,0:T(8,128)(2,1)S(1)}, bf16[32,2048]{1,0:T(8,128)(2,1)S(1)}, u32[]{:S(2)}, u32[]{:S(2)}) collective-permute-start(bf16[32,2048]{1,0:T(8,128)(2,1)S(1)} %get-tuple-element.104), channel_id=1, source_target_pairs={{0,1},{1,0},{2,3},{3,2},{4,5},{5,4},{6,7},{7,6},{8,9},{9,8},{10,11... | collective-permute-start | bytes 393224 | tf_op jit(solution)/shard_map/ppermute | solution.py:576
  70.8 4.3 %collective-permute-done.30.arrived_ref.refs_4_ = bf16[32,2048]{1,0:T(8,128)(2,1)S(1)} collective-permute-done((bf16[32,2048]{1,0:T(8,128)(2,1)S(1)}, bf16[32,2048]{1,0:T(8,128)(2,1)S(1)}, u32[]{:S(2)}, u32[]{:S(2)}) %collective-permute-start.30) | collective-permute-done | bytes 131104 | tf_op jit(solution)/shard_map/ppermute | solution.py:576
  76.5 1.8 %collective-permute-start.37 = (bf16[16,2048]{1,0:T(8,128)(2,1)S(1)}, bf16[16,2048]{1,0:T(8,128)(2,1)S(1)}, u32[]{:S(2)}, u32[]{:S(2)}) collective-permute-start(bf16[16,2048]{1,0:T(8,128)(2,1)S(1)} %get-tuple-element.109), channel_id=1, source_target_pairs={{0,1},{1,0},{2,3},{3,2},{4,5},{5,4},{6,7},{7,6},{8,9},{9,8},{10,11... | collective-permute-start | bytes 196616 | tf_op jit(solution)/shard_map/ppermute | solution.py:576
  78.3 3.5 %collective-permute-done.37.arrived_ref = bf16[16,2048]{1,0:T(8,128)(2,1)S(1)} collective-permute-done((bf16[16,2048]{1,0:T(8,128)(2,1)S(1)}, bf16[16,2048]{1,0:T(8,128)(2,1)S(1)}, u32[]{:S(2)}, u32[]{:S(2)}) %collective-permute-start.37) | collective-permute-done | bytes 65568 | tf_op jit(solution)/shard_map/ppermute | solution.py:576
  81.8 2.1 %collective-permute-start.38 = (bf16[24,2048]{1,0:T(8,128)(2,1)S(1)}, bf16[24,2048]{1,0:T(8,128)(2,1)S(1)}, u32[]{:S(2)}, u32[]{:S(2)}) collective-permute-start(bf16[24,2048]{1,0:T(8,128)(2,1)S(1)} %grad_join.1.joined_ref), channel_id=1, source_target_pairs={{0,2},{1,3},{2,0},{3,1},{4,6},{5,7},{6,4},{7,5},{8,10},{9,11},{10,... | collective-permute-start | bytes 294920 | tf_op jit(solution)/shard_map/ppermute | solution.py:576
  84.9 6.1 %collective-permute-done.38.other_ref = bf16[24,2048]{1,0:T(8,128)(2,1)S(1)} collective-permute-done((bf16[24,2048]{1,0:T(8,128)(2,1)S(1)}, bf16[24,2048]{1,0:T(8,128)(2,1)S(1)}, u32[]{:S(2)}, u32[]{:S(2)}) %collective-permute-start.38) | collective-permute-done | bytes 98336 | tf_op jit(solution)/shard_map/ppermute | solution.py:576
  91.8 2.1 %collective-permute-start.32 = (bf16[32,2048]{1,0:T(8,128)(2,1)S(1)}, bf16[32,2048]{1,0:T(8,128)(2,1)S(1)}, u32[]{:S(2)}, u32[]{:S(2)}) collective-permute-start(bf16[32,2048]{1,0:T(8,128)(2,1)S(1)} %finish.2.refs_0_), channel_id=1, source_target_pairs={{0,1},{1,0},{2,3},{3,2},{4,5},{5,4},{6,7},{7,6},{8,9},{9,8},{10,11... | collective-permute-start | bytes 393224 | tf_op jit(solution)/shard_map/ppermute | solution.py:576
  93.9 1.8 %collective-permute-done.39.refs_8_.refs_5_ = bf16[16,2176]{1,0:T(8,128)(2,1)S(1)} collective-permute-done((bf16[16,2176]{1,0:T(8,128)(2,1)S(1)}, bf16[16,2176]{1,0:T(8,128)(2,1)S(1)}, u32[]{:S(2)}, u32[]{:S(2)}) %collective-permute-start.39) | collective-permute-done | bytes 69664 | tf_op jit(solution)/shard_map/ppermute | solution.py:576
  96.5 3.0 %merge_grad.1 = f32[288,128]{1,0:T(8,128)} custom-call(f32[4,288]{1,0:T(4,128)S(1)} %copy-done.15, bf16[32,1152]{1,0:T(8,128)(2,1)S(1)} %get-tuple-element.112.refs_1_, bf16[32,128]{1,0:T(8,128)(2,1)S(1)} %get-tuple-element.113.refs_2_, bf16[1152,2048]{1,0:T(8,128)(2,1)S(1)} %bitcast.10, bf16[16,2176]{1,0:T(8,128)(2,1)S(1)} %norm_grad.1.refs_4_, ...), custom_call_target="tpu_custom_call" | custom-call | bytes 12000000 | tf_op jit(solution)/shard_map/merge_grad/pallas_call | solution.py:530
  99.5 1.7 %collective-permute-done.40.refs_3_ = bf16[32,2048]{1,0:T(8,128)(2,1)S(1)} collective-permute-done((bf16[32,2048]{1,0:T(8,128)(2,1)S(1)}, bf16[32,2048]{1,0:T(8,128)(2,1)S(1)}, u32[]{:S(2)}, u32[]{:S(2)}) %collective-permute-start.40) | collective-permute-done | bytes 131104 | tf_op jit(solution)/shard_map/ppermute | solution.py:576
  (116 shorter events, 25.7 us)
Async XLA Ops:
  2.6 10.0 %collective-permute-start.3 = (bf16[592,128]{1,0:T(8,128)(2,1)}, bf16[592,128]{1,0:T(8,128)(2,1)S(1)}, u32[]{:S(2)}, u32[]{:S(2)}) collective-permute-start(bf16[592,128]{1,0:T(8,128)(2,1)} %pack.1), channel_id=1, source_target_pairs={{0,24},{4,28},{8,16},{12,20},{16,8},{20,12},{24,0},{28,4},{1,25},{... | collective-permute-start | bytes 454664 | tf_op jit(solution)/shard_map/ppermute | solution.py:576
  6.5 7.4 %collective-permute-start.2 = (bf16[592,128]{1,0:T(8,128)(2,1)}, bf16[592,128]{1,0:T(8,128)(2,1)S(1)}, u32[]{:S(2)}, u32[]{:S(2)}) collective-permute-start(bf16[592,128]{1,0:T(8,128)(2,1)} %pack.1), channel_id=1, source_target_pairs={{0,16},{4,20},{8,24},{12,28},{16,0},{20,4},{24,8},{28,12},{1,17},{... | collective-permute-start | bytes 454664 | tf_op jit(solution)/shard_map/ppermute | solution.py:576
  7.0 7.2 %collective-permute-start.1 = (bf16[592,128]{1,0:T(8,128)(2,1)}, bf16[592,128]{1,0:T(8,128)(2,1)S(1)}, u32[]{:S(2)}, u32[]{:S(2)}) collective-permute-start(bf16[592,128]{1,0:T(8,128)(2,1)} %pack.1), channel_id=1, source_target_pairs={{0,8},{4,12},{8,0},{12,4},{16,24},{20,28},{24,16},{28,20},{1,9},{5... | collective-permute-start | bytes 454664 | tf_op jit(solution)/shard_map/ppermute | solution.py:576
  7.2 10.5 %collective-permute-start = (bf16[592,128]{1,0:T(8,128)(2,1)}, bf16[592,128]{1,0:T(8,128)(2,1)S(1)}, u32[]{:S(2)}, u32[]{:S(2)}) collective-permute-start(bf16[592,128]{1,0:T(8,128)(2,1)} %pack.1), channel_id=1, source_target_pairs={{0,4},{4,0},{8,12},{12,8},{16,20},{20,16},{24,28},{28,24},{1,5},{5... | collective-permute-start | bytes 454664 | tf_op jit(solution)/shard_map/ppermute | solution.py:576
  14.2 7.8 %collective-permute-start.7 = (bf16[48,2048]{1,0:T(8,128)(2,1)S(1)}, bf16[48,2048]{1,0:T(8,128)(2,1)S(1)}, u32[]{:S(2)}, u32[]{:S(2)}) collective-permute-start(bf16[48,2048]{1,0:T(8,128)(2,1)S(1)} %get-tuple-element.72), channel_id=1, source_target_pairs={{0,8},{4,12},{8,0},{12,4},{16,24},{20,28},{24,16},{28,20},{1,9},{5... | collective-permute-start | bytes 589832 | tf_op jit(solution)/shard_map/ppermute | solution.py:576
  15.7 11.7 %collective-permute-start.8 = (bf16[48,2048]{1,0:T(8,128)(2,1)S(1)}, bf16[48,2048]{1,0:T(8,128)(2,1)S(1)}, u32[]{:S(2)}, u32[]{:S(2)}) collective-permute-start(bf16[48,2048]{1,0:T(8,128)(2,1)S(1)} %get-tuple-element.73), channel_id=1, source_target_pairs={{0,16},{4,20},{8,24},{12,28},{16,0},{20,4},{24,8},{28,12},{1,17},{... | collective-permute-start | bytes 589832 | tf_op jit(solution)/shard_map/ppermute | solution.py:576
  16.6 10.9 %collective-permute-start.9 = (bf16[48,2048]{1,0:T(8,128)(2,1)S(1)}, bf16[48,2048]{1,0:T(8,128)(2,1)S(1)}, u32[]{:S(2)}, u32[]{:S(2)}) collective-permute-start(bf16[48,2048]{1,0:T(8,128)(2,1)S(1)} %get-tuple-element.74), channel_id=1, source_target_pairs={{0,24},{4,28},{8,16},{12,20},{16,8},{20,12},{24,0},{28,4},{1,25},{... | collective-permute-start | bytes 589832 | tf_op jit(solution)/shard_map/ppermute | solution.py:576
  23.0 4.5 %collective-permute-start.10 = (bf16[8,2432]{1,0:T(8,128)(2,1)S(1)}, bf16[8,2432]{1,0:T(8,128)(2,1)S(1)}, u32[]{:S(2)}, u32[]{:S(2)}) collective-permute-start(bf16[8,2432]{1,0:T(8,128)(2,1)S(1)} %get-tuple-element.77), channel_id=1, source_target_pairs={{0,1},{1,0},{2,3},{3,2},{4,5},{5,4},{6,7},{7,6},{8,9},{9,8},{10,11... | collective-permute-start | bytes 116744 | tf_op jit(solution)/shard_map/ppermute | solution.py:576
  24.6 5.6 %collective-permute-start.11 = (bf16[8,2432]{1,0:T(8,128)(2,1)S(1)}, bf16[8,2432]{1,0:T(8,128)(2,1)S(1)}, u32[]{:S(2)}, u32[]{:S(2)}) collective-permute-start(bf16[8,2432]{1,0:T(8,128)(2,1)S(1)} %get-tuple-element.78), channel_id=1, source_target_pairs={{0,2},{1,3},{2,0},{3,1},{4,6},{5,7},{6,4},{7,5},{8,10},{9,11},{10,... | collective-permute-start | bytes 116744 | tf_op jit(solution)/shard_map/ppermute | solution.py:576
  27.2 5.8 %collective-permute-start.12 = (bf16[8,2432]{1,0:T(8,128)(2,1)S(1)}, bf16[8,2432]{1,0:T(8,128)(2,1)S(1)}, u32[]{:S(2)}, u32[]{:S(2)}) collective-permute-start(bf16[8,2432]{1,0:T(8,128)(2,1)S(1)} %get-tuple-element.79), channel_id=1, source_target_pairs={{0,3},{1,2},{2,1},{3,0},{4,7},{5,6},{6,5},{7,4},{8,11},{9,10},{10,... | collective-permute-start | bytes 116744 | tf_op jit(solution)/shard_map/ppermute | solution.py:576
  33.1 5.9 %collective-permute-start.15 = (bf16[8,2176]{1,0:T(8,128)(2,1)S(1)}, bf16[8,2176]{1,0:T(8,128)(2,1)S(1)}, u32[]{:S(2)}, u32[]{:S(2)}) collective-permute-start(bf16[8,2176]{1,0:T(8,128)(2,1)S(1)} %get-tuple-element.84.refs_0_), channel_id=1, source_target_pairs={{0,3},{1,2},{2,1},{3,0},{4,7},{5,6},{6,5},{7,4},{8,11},{9,10},{10,... | collective-permute-start | bytes 104456 | tf_op jit(solution)/shard_map/ppermute | solution.py:576
  33.9 5.7 %collective-permute-start.14 = (bf16[8,2176]{1,0:T(8,128)(2,1)S(1)}, bf16[8,2176]{1,0:T(8,128)(2,1)S(1)}, u32[]{:S(2)}, u32[]{:S(2)}) collective-permute-start(bf16[8,2176]{1,0:T(8,128)(2,1)S(1)} %get-tuple-element.84.refs_0_), channel_id=1, source_target_pairs={{0,2},{1,3},{2,0},{3,1},{4,6},{5,7},{6,4},{7,5},{8,10},{9,11},{10,... | collective-permute-start | bytes 104456 | tf_op jit(solution)/shard_map/ppermute | solution.py:576
  33.9 5.7 %collective-permute-start.13 = (bf16[8,2176]{1,0:T(8,128)(2,1)S(1)}, bf16[8,2176]{1,0:T(8,128)(2,1)S(1)}, u32[]{:S(2)}, u32[]{:S(2)}) collective-permute-start(bf16[8,2176]{1,0:T(8,128)(2,1)S(1)} %get-tuple-element.84.refs_0_), channel_id=1, source_target_pairs={{0,1},{1,0},{2,3},{3,2},{4,5},{5,4},{6,7},{7,6},{8,9},{9,8},{10,11... | collective-permute-start | bytes 104456 | tf_op jit(solution)/shard_map/ppermute | solution.py:576
  39.6 4.4 %collective-permute-start.16 = (bf16[96,2048]{1,0:T(8,128)(2,1)S(1)}, bf16[96,2048]{1,0:T(8,128)(2,1)S(1)}, u32[]{:S(2)}, u32[]{:S(2)}) collective-permute-start(bf16[96,2048]{1,0:T(8,128)(2,1)S(1)} %early_half.1), channel_id=1, source_target_pairs={{0,4},{4,0},{8,12},{12,8},{16,20},{20,16},{24,28},{28,24},{1,5},{5... | collective-permute-start | bytes 1179656 | tf_op jit(solution)/shard_map/ppermute | solution.py:576
  39.7 7.3 %collective-permute-start.20 = (bf16[32,2048]{1,0:T(8,128)(2,1)S(1)}, bf16[32,2048]{1,0:T(8,128)(2,1)S(1)}, u32[]{:S(2)}, u32[]{:S(2)}) collective-permute-start(bf16[32,2048]{1,0:T(8,128)(2,1)S(1)} %get-tuple-element.86.refs_6_.refs_0_.rows_ref), channel_id=1, source_target_pairs={{0,24},{4,28},{8,16},{12,20},{16,8},{20,12},{24,0},{28,4},{1,25},{... | collective-permute-start | bytes 393224 | tf_op jit(solution)/shard_map/ppermute | solution.py:576
  41.6 7.8 %collective-permute-start.19 = (bf16[32,2048]{1,0:T(8,128)(2,1)S(1)}, bf16[32,2048]{1,0:T(8,128)(2,1)S(1)}, u32[]{:S(2)}, u32[]{:S(2)}) collective-permute-start(bf16[32,2048]{1,0:T(8,128)(2,1)S(1)} %get-tuple-element.86.refs_6_.refs_0_.rows_ref), channel_id=1, source_target_pairs={{0,16},{4,20},{8,24},{12,28},{16,0},{20,4},{24,8},{28,12},{1,17},{... | collective-permute-start | bytes 393224 | tf_op jit(solution)/shard_map/ppermute | solution.py:576
  42.7 6.7 %collective-permute-start.18 = (bf16[32,2048]{1,0:T(8,128)(2,1)S(1)}, bf16[32,2048]{1,0:T(8,128)(2,1)S(1)}, u32[]{:S(2)}, u32[]{:S(2)}) collective-permute-start(bf16[32,2048]{1,0:T(8,128)(2,1)S(1)} %get-tuple-element.86.refs_6_.refs_0_.rows_ref), channel_id=1, source_target_pairs={{0,8},{4,12},{8,0},{12,4},{16,24},{20,28},{24,16},{28,20},{1,9},{5... | collective-permute-start | bytes 393224 | tf_op jit(solution)/shard_map/ppermute | solution.py:576
  43.9 6.0 %collective-permute-start.17 = (bf16[32,2048]{1,0:T(8,128)(2,1)S(1)}, bf16[32,2048]{1,0:T(8,128)(2,1)S(1)}, u32[]{:S(2)}, u32[]{:S(2)}) collective-permute-start(bf16[32,2048]{1,0:T(8,128)(2,1)S(1)} %get-tuple-element.86.refs_6_.refs_0_.rows_ref), channel_id=1, source_target_pairs={{0,4},{4,0},{8,12},{12,8},{16,20},{20,16},{24,28},{28,24},{1,5},{5... | collective-permute-start | bytes 393224 | tf_op jit(solution)/shard_map/ppermute | solution.py:576
  56.3 5.0 %collective-permute-start.24 = (bf16[24,2048]{1,0:T(8,128)(2,1)S(1)}, bf16[24,2048]{1,0:T(8,128)(2,1)S(1)}, u32[]{:S(2)}, u32[]{:S(2)}) collective-permute-start(bf16[24,2048]{1,0:T(8,128)(2,1)S(1)} %get-tuple-element.91), channel_id=1, source_target_pairs={{0,8},{4,12},{8,0},{12,4},{16,24},{20,28},{24,16},{28,20},{1,9},{5... | collective-permute-start | bytes 294920 | tf_op jit(solution)/shard_map/ppermute | solution.py:576
  57.7 6.8 %collective-permute-start.25 = (bf16[24,2048]{1,0:T(8,128)(2,1)S(1)}, bf16[24,2048]{1,0:T(8,128)(2,1)S(1)}, u32[]{:S(2)}, u32[]{:S(2)}) collective-permute-start(bf16[24,2048]{1,0:T(8,128)(2,1)S(1)} %get-tuple-element.92), channel_id=1, source_target_pairs={{0,16},{4,20},{8,24},{12,28},{16,0},{20,4},{24,8},{28,12},{1,17},{... | collective-permute-start | bytes 294920 | tf_op jit(solution)/shard_map/ppermute | solution.py:576
  58.5 6.0 %collective-permute-start.26 = (bf16[24,2048]{1,0:T(8,128)(2,1)S(1)}, bf16[24,2048]{1,0:T(8,128)(2,1)S(1)}, u32[]{:S(2)}, u32[]{:S(2)}) collective-permute-start(bf16[24,2048]{1,0:T(8,128)(2,1)S(1)} %get-tuple-element.93), channel_id=1, source_target_pairs={{0,24},{4,28},{8,16},{12,20},{16,8},{20,12},{24,0},{28,4},{1,25},{... | collective-permute-start | bytes 294920 | tf_op jit(solution)/shard_map/ppermute | solution.py:576
  64.7 11.8 %collective-permute-start.34 = (bf16[40,2048]{1,0:T(8,128)(2,1)S(1)}, bf16[40,2048]{1,0:T(8,128)(2,1)S(1)}, u32[]{:S(2)}, u32[]{:S(2)}) collective-permute-start(bf16[40,2048]{1,0:T(8,128)(2,1)S(1)} %get-tuple-element.105), channel_id=1, source_target_pairs={{0,8},{4,12},{8,0},{12,4},{16,24},{20,28},{24,16},{28,20},{1,9},{5... | collective-permute-start | bytes 491528 | tf_op jit(solution)/shard_map/ppermute | solution.py:576
  65.4 11.0 %collective-permute-start.35 = (bf16[40,2048]{1,0:T(8,128)(2,1)S(1)}, bf16[40,2048]{1,0:T(8,128)(2,1)S(1)}, u32[]{:S(2)}, u32[]{:S(2)}) collective-permute-start(bf16[40,2048]{1,0:T(8,128)(2,1)S(1)} %get-tuple-element.106), channel_id=1, source_target_pairs={{0,16},{4,20},{8,24},{12,28},{16,0},{20,4},{24,8},{28,12},{1,17},{... | collective-permute-start | bytes 491528 | tf_op jit(solution)/shard_map/ppermute | solution.py:576
  66.8 9.7 %collective-permute-start.36 = (bf16[40,2048]{1,0:T(8,128)(2,1)S(1)}, bf16[40,2048]{1,0:T(8,128)(2,1)S(1)}, u32[]{:S(2)}, u32[]{:S(2)}) collective-permute-start(bf16[40,2048]{1,0:T(8,128)(2,1)S(1)} %get-tuple-element.107), channel_id=1, source_target_pairs={{0,24},{4,28},{8,16},{12,20},{16,8},{20,12},{24,0},{28,4},{1,25},{... | collective-permute-start | bytes 491528 | tf_op jit(solution)/shard_map/ppermute | solution.py:576
  68.7 6.4 %collective-permute-start.30 = (bf16[32,2048]{1,0:T(8,128)(2,1)S(1)}, bf16[32,2048]{1,0:T(8,128)(2,1)S(1)}, u32[]{:S(2)}, u32[]{:S(2)}) collective-permute-start(bf16[32,2048]{1,0:T(8,128)(2,1)S(1)} %get-tuple-element.104), channel_id=1, source_target_pairs={{0,1},{1,0},{2,3},{3,2},{4,5},{5,4},{6,7},{7,6},{8,9},{9,8},{10,11... | collective-permute-start | bytes 393224 | tf_op jit(solution)/shard_map/ppermute | solution.py:576
  70.7 13.2 %collective-permute-start.29 = (bf16[32,2048]{1,0:T(8,128)(2,1)S(1)}, bf16[32,2048]{1,0:T(8,128)(2,1)S(1)}, u32[]{:S(2)}, u32[]{:S(2)}) collective-permute-start(bf16[32,2048]{1,0:T(8,128)(2,1)S(1)} %get-tuple-element.102), channel_id=1, source_target_pairs={{0,1},{1,0},{2,3},{3,2},{4,5},{5,4},{6,7},{7,6},{8,9},{9,8},{10,11... | collective-permute-start | bytes 393224 | tf_op jit(solution)/shard_map/ppermute | solution.py:576
  75.2 8.8 %collective-permute-start.31 = (bf16[32,2048]{1,0:T(8,128)(2,1)S(1)}, bf16[32,2048]{1,0:T(8,128)(2,1)S(1)}, u32[]{:S(2)}, u32[]{:S(2)}) collective-permute-start(bf16[32,2048]{1,0:T(8,128)(2,1)S(1)} %add_high.1.own_ref), channel_id=1, source_target_pairs={{0,2},{1,3},{2,0},{3,1},{4,6},{5,7},{6,4},{7,5},{8,10},{9,11},{10,... | collective-permute-start | bytes 393224 | tf_op jit(solution)/shard_map/ppermute | solution.py:576
  76.5 5.3 %collective-permute-start.37 = (bf16[16,2048]{1,0:T(8,128)(2,1)S(1)}, bf16[16,2048]{1,0:T(8,128)(2,1)S(1)}, u32[]{:S(2)}, u32[]{:S(2)}) collective-permute-start(bf16[16,2048]{1,0:T(8,128)(2,1)S(1)} %get-tuple-element.109), channel_id=1, source_target_pairs={{0,1},{1,0},{2,3},{3,2},{4,5},{5,4},{6,7},{7,6},{8,9},{9,8},{10,11... | collective-permute-start | bytes 196616 | tf_op jit(solution)/shard_map/ppermute | solution.py:576
  81.8 9.2 %collective-permute-start.38 = (bf16[24,2048]{1,0:T(8,128)(2,1)S(1)}, bf16[24,2048]{1,0:T(8,128)(2,1)S(1)}, u32[]{:S(2)}, u32[]{:S(2)}) collective-permute-start(bf16[24,2048]{1,0:T(8,128)(2,1)S(1)} %grad_join.1.joined_ref), channel_id=1, source_target_pairs={{0,2},{1,3},{2,0},{3,1},{4,6},{5,7},{6,4},{7,5},{8,10},{9,11},{10,... | collective-permute-start | bytes 294920 | tf_op jit(solution)/shard_map/ppermute | solution.py:576
  84.0 11.7 %collective-permute-start.33 = (bf16[32,2048]{1,0:T(8,128)(2,1)S(1)}, bf16[32,2048]{1,0:T(8,128)(2,1)S(1)}, u32[]{:S(2)}, u32[]{:S(2)}) collective-permute-start(bf16[32,2048]{1,0:T(8,128)(2,1)S(1)} %add_low.1.own_ref), channel_id=1, source_target_pairs={{0,2},{1,3},{2,0},{3,1},{4,6},{5,7},{6,4},{7,5},{8,10},{9,11},{10,... | collective-permute-start | bytes 393224 | tf_op jit(solution)/shard_map/ppermute | solution.py:576
  91.8 7.6 %collective-permute-start.32 = (bf16[32,2048]{1,0:T(8,128)(2,1)S(1)}, bf16[32,2048]{1,0:T(8,128)(2,1)S(1)}, u32[]{:S(2)}, u32[]{:S(2)}) collective-permute-start(bf16[32,2048]{1,0:T(8,128)(2,1)S(1)} %finish.2.refs_0_), channel_id=1, source_target_pairs={{0,1},{1,0},{2,3},{3,2},{4,5},{5,4},{6,7},{7,6},{8,9},{9,8},{10,11... | collective-permute-start | bytes 393224 | tf_op jit(solution)/shard_map/ppermute | solution.py:576
  96.2 5.0 %collective-permute-start.40 = (bf16[32,2048]{1,0:T(8,128)(2,1)S(1)}, bf16[32,2048]{1,0:T(8,128)(2,1)S(1)}, u32[]{:S(2)}, u32[]{:S(2)}) collective-permute-start(bf16[32,2048]{1,0:T(8,128)(2,1)S(1)} %finish.3.refs_2_), channel_id=1, source_target_pairs={{0,1},{1,0},{2,3},{3,2},{4,5},{5,4},{6,7},{7,6},{8,9},{9,8},{10,11... | collective-permute-start | bytes 393224 | tf_op jit(solution)/shard_map/ppermute | solution.py:576
  (28 other events, 290.5 us)
